TPU v7x, 32 devices: a whole 2x2x4 slice. The times are simulated.
32 devices in a mesh: groups: 16 (over z, y, x), mp: 2 (over core).
Axes of the slice: x: 2, y: 2, z: 4, core: 2. Of those that a mesh axis runs over, the one named last changes fastest.
Arguments:
- latents: float32 [1536, 256], P('groups', 'mp'), may hold values from -6 to 6
- tile_slot: int32 [1536], replicated, may hold values from 0 to 1535, as said below
- live: int32 [16], replicated, may hold values from 192 to 384, as said below
- partner: int32 [16], replicated, may hold values from 0 to 15, as said below
- text_states: bfloat16 [16, 2, 154, 2432], P('groups'), may hold values from -6 to 6
- modulation: float32 [16, 2, 5, 2432], P('groups'), may hold values from -3 to 3
- w_embed: bfloat16 [64, 2432], replicated, may hold values from -0.75 to 0.75
- w_qkv: bfloat16 [2432, 3, 1280], P(None, None, 'mp'), may hold values from -0.125 to 0.125
- w_text_kv: bfloat16 [2432, 2, 1280], P(None, None, 'mp'), may hold values from -0.125 to 0.125
- w_out: bfloat16 [1280, 2432], P('mp'), may hold values from -0.15625 to 0.15625
- w_final: bfloat16 [2432, 64], replicated, may hold values from -0.125 to 0.125
- norm_gains: float32 [3, 64], replicated, may hold values from 0.5 to 24
Outputs:
- new_latents: float32 [1536, 256], P('groups', 'mp')
Inputs may be any that keep to these rules, and one draw needn't show every extreme that they name: `tile_slot`: every slot appears once; the tiles of one group go to any one group at most 6 times, and exactly 6 times for some pairs of groups. `live`: two groups that share a request hold equal counts; some group is full in every draw. partner[g] is g or g with its lowest bit flipped, and partner[partner[g]] = g; some pair shares a request in every draw.
All inputs are finite; a program needn't handle non-finite values.
Results may differ from a plain program's by a relative error of at most 0.012.
The roundings to bfloat16 on the way count: a program that leaves them out, or rounds other values in their place, can miss the bound.
Values may be sent and summed in bfloat16 or wider, within the bound.
No kernel may reach another device: no remote copies, remote signals or barrier semaphores. Data moves between devices by JAX's collectives and lax.ppermute only.
A program may use at most 128 MiB of HBM per device.

v0:
```python
import jax
import jax.numpy as jnp
from jax import lax
from jax.sharding import PartitionSpec as P

HEAD = 64
CH = 64
TEXT = 154
ROWS = 384
TILE = 4


GUIDE = 3.5
STEP = -0.25
EPS = 1e-06


def partner_2(value, axis, apart):
    mask = 2**apart
    pairs = [(source, source ^ mask) for source in range(lax.axis_size(axis))]
    return lax.ppermute(value, axis, pairs)


def layer_norm(inputs):
    centre = jnp.mean(inputs, axis=-1, keepdims=True)
    centred = inputs - centre
    spread = jnp.mean(centred * centred, axis=-1, keepdims=True)
    return centred * lax.rsqrt(spread + EPS)


def head_norm(inputs, gains):
    square = jnp.mean(inputs * inputs, axis=-1, keepdims=True)
    return (inputs * lax.rsqrt(square + EPS) * gains).astype(jnp.bfloat16)


def exactly(left, right):
    return jnp.dot(left, right, precision=lax.Precision.HIGHEST)


def finish(residue, mixed, adaptive, w_final):
    state = residue + adaptive[:, 2, None, :] * mixed
    final = (layer_norm(state) * (1.0 + adaptive[:, 4, None, :]) + adaptive[:, 3, None, :]).astype(
        jnp.bfloat16
    )
    velocity = jnp.einsum("brd,dc->brc", final, w_final, preferred_element_type=jnp.float32)
    return velocity[1] + GUIDE * (velocity[0] - velocity[1])


def deal_tables(tile_slot, tile_count, groups_n, capacity, group_index):
    target = (tile_slot // tile_count).reshape(groups_n, tile_count)
    placed = (tile_slot % tile_count).reshape(groups_n, tile_count)
    tile_ids = jnp.arange(tile_count, dtype=jnp.int32)
    earlier = (target[:, :, None] == target[:, None, :]) & (
        tile_ids[None, None, :] < tile_ids[None, :, None]
    )
    order_rank = jnp.sum(earlier.astype(jnp.int32), axis=2)
    own_target = lax.dynamic_index_in_dim(target, group_index, 0, keepdims=False)
    own_rank = lax.dynamic_index_in_dim(order_rank, group_index, 0, keepdims=False)
    bucket_ids = jnp.arange(groups_n * capacity, dtype=jnp.int32)
    send_pos = own_target * capacity + own_rank
    sender = (bucket_ids[:, None] == send_pos[None, :]).astype(jnp.float32)
    levels = jnp.arange(capacity, dtype=jnp.int32)
    matched = (target[:, None, :] == group_index) & (
        order_rank[:, None, :] == levels[None, :, None]
    )
    position = jnp.sum(jnp.where(matched, placed[:, None, :], 0), axis=2).reshape(-1)
    present = jnp.any(matched, axis=2).reshape(-1)
    receiver = ((position[None, :] == tile_ids[:, None]) & present[None, :]).astype(jnp.float32)
    return (sender, receiver)


def shards(
    latents,
    tile_slot,
    live,
    partner,
    text_states,
    modulation,
    w_embed,
    w_qkv,
    w_text_kv,
    w_out,
    w_final,
    norm_gains,
):
    groups_n = lax.axis_size("groups")
    group_index = lax.axis_index("groups")
    member = lax.axis_index("mp")
    tile_count = ROWS // TILE
    capacity = max(2, (tile_count + groups_n - 1) // groups_n)
    narrow = latents.shape[1]
    sender, receiver = deal_tables(tile_slot, tile_count, groups_n, capacity, group_index)
    outbound = exactly(sender, latents).reshape(groups_n, capacity, narrow)
    inbound = (
        lax.all_to_all(
            outbound.astype(jnp.bfloat16), "groups", split_axis=0, concat_axis=0, tiled=True
        )
        .astype(outbound.dtype)
        .reshape(groups_n * capacity, narrow)
    )
    own_tiles = exactly(receiver, inbound)
    complete = lax.all_gather(own_tiles.astype(jnp.bfloat16), "mp", axis=1, tiled=True).astype(
        own_tiles.dtype
    )
    tokens = complete.reshape(ROWS, CH)
    hidden = jnp.dot(tokens.astype(jnp.bfloat16), w_embed, preferred_element_type=jnp.float32)
    adaptive = modulation[0]
    normed = (
        layer_norm(hidden)[None] * (1.0 + adaptive[:, 1, None, :]) + adaptive[:, 0, None, :]
    ).astype(jnp.bfloat16)
    projected = jnp.einsum("brd,dcn->brcn", normed, w_qkv, preferred_element_type=jnp.float32)
    local_width = projected.shape[-1]
    local_heads = local_width // HEAD
    projected = projected.reshape(2, ROWS, 3, local_heads, HEAD)
    query = head_norm(projected[:, :, 0], norm_gains[0])
    image_key = head_norm(projected[:, :, 1], norm_gains[1])
    image_value = projected[:, :, 2].astype(jnp.bfloat16)
    paired = jnp.stack([image_key, image_value], axis=2).reshape(2, ROWS, 2, local_width)
    mate_keys = partner_2(paired, "groups", 0).reshape(2, ROWS, 2, local_heads, HEAD)
    text_proj = jnp.einsum(
        "btd,dcn->btcn", text_states[0], w_text_kv, preferred_element_type=jnp.float32
    )
    text_proj = text_proj.reshape(2, TEXT, 2, local_heads, HEAD)
    text_key = head_norm(text_proj[:, :, 0], norm_gains[2])
    text_value = text_proj[:, :, 1].astype(jnp.bfloat16)
    mate = partner[group_index]
    joined = mate != group_index
    own_len = live[group_index]
    mate_len = jnp.where(joined, live[mate], 0)
    position = jnp.arange(ROWS, dtype=jnp.int32)
    all_keys = jnp.concatenate([text_key, image_key, mate_keys[:, :, 0]], axis=1)
    all_values = jnp.concatenate([text_value, image_value, mate_keys[:, :, 1]], axis=1)
    usable = jnp.concatenate([jnp.ones((TEXT,), bool), position < own_len, position < mate_len])

    def branch_attention(items):
        branch_query, branch_keys, branch_values = items
        scores = jnp.einsum(
            "qhe,khe->hqk", branch_query, branch_keys, preferred_element_type=jnp.float32
        ) * HEAD ** (-0.5)
        scores = jnp.where(usable[None, None, :], scores, -1e30)
        highest = jnp.max(scores, axis=-1, keepdims=True)
        raised = jnp.exp(scores - highest)
        summed = jnp.sum(raised, axis=-1, keepdims=True)
        weights = (raised / summed).astype(jnp.bfloat16)
        result_heads = jnp.einsum(
            "hqk,khe->qhe", weights, branch_values, preferred_element_type=jnp.float32
        )
        return result_heads.astype(jnp.bfloat16)

    attended = lax.map(branch_attention, (query, all_keys, all_values)).reshape(
        2, ROWS, local_width
    )
    partial_sum = jnp.einsum("brn,nd->brd", attended, w_out, preferred_element_type=jnp.float32)
    mixed = lax.psum(partial_sum.astype(jnp.bfloat16), "mp").astype(jnp.float32)
    guided = finish(hidden[None], mixed, adaptive, w_final)
    living = (position < own_len)[:, None]
    updated = tokens + STEP * jnp.where(living, guided, 0.0)
    new_tiles = updated.reshape(tile_count, TILE * CH)
    columns = lax.dynamic_slice_in_dim(new_tiles, member * narrow, narrow, 1)
    homeward = exactly(receiver.T, columns).reshape(groups_n, capacity, narrow)
    returned = (
        lax.all_to_all(
            homeward.astype(jnp.bfloat16), "groups", split_axis=0, concat_axis=0, tiled=True
        )
        .astype(homeward.dtype)
        .reshape(groups_n * capacity, narrow)
    )
    result = exactly(sender.T, returned)
    return result


def solution(mesh):
    placed = (
        P("groups", "mp"),
        P(),
        P(),
        P(),
        P("groups", None, None, None),
        P("groups", None, None, None),
        P(),
        P(None, None, "mp"),
        P(None, None, "mp"),
        P("mp", None),
        P(),
        P(),
    )
    return jax.shard_map(
        shards, mesh=mesh, in_specs=placed, out_specs=P("groups", "mp"), check_vma=False
    )
```

profile of v0, /device:TPU:0, one launch (start us, length us, event | category | flops | bytes accessed | tf_op | source)
XLA Modules:
  0.0 209.7 jit_solution(11390787566061059934)
XLA Ops:
  9.7 8.3 %all-to-all-start = ((bf16[16,6,128]{2,1,0:T(8,128)(2,1)}), bf16[16,6,128]{2,1,0:T(8,128)(2,1)S(1)}, u32[]{:S(2)}, u32[]{:S(2)}) async-start(bf16[16,6,128]{2,1,0:T(8,128)(2,1)} %convert_element_type.75), calls=%async_computation | async-start | bytes 65536 | tf_op jit(solution)/shard_map/all_to_all | solution.py:95
  21.2 16.8 %copy.31 = bf16[2432,2,640]{0,2,1:T(8,128)(2,1)} copy(bf16[2432,2,640]{2,1,0:T(2,128)(2,1)} %param.22) | data formatting | bytes 12451840 | tf_op args[8]
  38.2 2.0 all_gather.3
  43.6 10.6 %fusion.45 = f32[2,384,3,640]{1,3,2,0:T(8,128)S(1)} fusion(bf16[2432,3,640]{2,0,1:T(8,128)(2,1)} %param.21, f32[2,2432]{1,0:T(2,128)S(1)} %get-tuple-element.63, f32[2,2432]{1,0:T(2,128)S(1)} %copy-done.10, f32[384,2432]{1,0:T(8,128)S(1)} %subtract_multiply_fusion), kind=kOutput, calls=%fused_computation.29 | convolution fusion | flops 7177863168 | bytes 19011584 | tf_op jit(solution)/shard_map/brd,dcn->brcn/dot_general | solution.py:111
  58.4 1.9 collective-permute-start
  60.3 5.1 %fusion.60 = f32[2,154,2,10,64]{1,4,3,2,0:T(8,128)} fusion(bf16[2,10,64,2432,1]{3,2,1,0,4:T(8,128)(2,1)S(1)} %bitcast.146, bf16[2,154,2432,1,1]{2,0,1,4,3:T(2,128)(2,1)S(1)} %bitcast.151), kind=kOutput, calls=%fused_computation.60 | convolution fusion | flops 1917583360 | bytes 9300992 | tf_op jit(solution)/shard_map/btd,dcn->btcn/dot_general | solution.py:120
  73.5 1.7 multiply_convert_fusion.2
  75.2 1.7 fusion.109
  76.9 3.8 %fusion.59 = (bf16[2,384,10,64]{1,3,2,0:T(8,128)(2,1)S(1)}, bf16[2,384,10,64]{1,3,2,0:T(8,128)(2,1)}) fusion(f32[2,384,3,10,64]{1,4,3,2,0:T(8,128)} %bitcast.143, f32[64]{0:T(128)S(1)} %get-tuple-element.68, f32[2,384,10]{1,2,0:T(8,128)S(1)} %get-tuple-element.75, f32[64]{0:T(128)S(1)} %get-tuple-element.69, f32[2,384,10]{1,2,0:T(8,128)S(1)} %get-tuple-element.74), kind=kLoop, calls=%fused_computation.56 | loop fusion | flops 2949120 | bytes 5960192 | tf_op jit(solution)/shard_map/convert_element_type | solution.py:33
  80.6 23.1 %collective-permute-done = bf16[2,384,2,640]{1,3,0,2:T(8,128)(2,1)} collective-permute-done((bf16[2,384,2,640]{1,3,0,2:T(8,128)(2,1)}, bf16[2,384,2,640]{1,3,0,2:T(8,128)(2,1)}, u32[]{:S(2)}, u32[]{:S(2)}) %collective-permute-start) | collective-permute-done | bytes 1966112 | tf_op jit(solution)/shard_map/ppermute | solution.py:21
  103.7 1.7 slice_bitcast_fusion.3
  105.5 2.8 %pad_maximum_fusion.1 = bf16[2,922,10,64]{1,3,2,0:T(8,128)(2,1)} fusion(bf16[2,384,10,64]{1,3,2,0:T(8,128)(2,1)S(1)} %get-tuple-element.56, bf16[2,384,10,64]{1,3,2,0:T(8,128)(2,1)S(1)} %get-tuple-element.54, bf16[2,154,10,64]{1,3,2,0:T(8,128)(2,1)S(1)} %multiply_convert_fusion.2), kind=kLoop, calls=%fused_computation.47 | loop fusion | flops 7080960 | bytes 4720640 | tf_op jit(solution)/shard_map/concatenate | solution.py:131
  108.3 2.8 %pad_maximum_fusion = bf16[2,922,10,64]{1,3,2,0:T(8,128)(2,1)} fusion(bf16[2,384,10,64]{1,3,2,0:T(8,128)(2,1)S(1)} %get-tuple-element.57, bf16[2,384,10,64]{1,3,2,0:T(8,128)(2,1)S(1)} %fusion.109, bf16[2,154,10,64]{1,3,2,0:T(8,128)(2,1)S(1)} %fusion.62), kind=kLoop, calls=%fused_computation.46 | loop fusion | flops 7080960 | bytes 4720640 | tf_op jit(solution)/shard_map/concatenate | solution.py:132
  111.1 34.0 %while.10 = (s32[]{:T(128)}, bf16[2,384,10,64]{1,3,2,0:T(8,128)(2,1)}, bf16[2,922,10,64]{1,3,2,0:T(8,128)(2,1)}, pred[922]{0:T(1024)(128)(4,1)S(1)}, bf16[2,384,...) while((s32[]{:T(128)}, bf16[2,384,10,64]{1,3,2,0:T(8,128)(2,1)}, ...), condition=%wide.region_11.12_spmd, body=%wide.region_8.11_spmd.sunk | while | flops 927852416 | bytes 32054248 | solution.py:150
  111.1 9.4 %fusion.125 = (f32[10,384]{1,0:T(8,128)S(1)}, f32[10,384,922]{1,2,0:T(8,128)}) fusion(pred[922]{0:T(1024)(128)(4,1)S(1)} %get-tuple-element.136, bf16[2,922,10,64]{1,3,2,0:T(8,128)(2,1)} %get-tuple-element.138, s32[]{:T(128)} %get-tuple-element.126, bf16[2,384,10,64]{1,3,2,0:T(8,128)(2,1)} %get-tuple-element.137), kind=kOutput, calls=%fused_computation.137.clone.1 | convolution fusion | flops 467344288 | bytes 15981466 | tf_op jit(solution)/shard_map/while/body/eval_jaxpr/sub | solution.py:142
  120.5 7.6 %fusion.126 = bf16[2,384,10,64]{1,3,2,0:T(8,128)(2,1)} fusion(bf16[2,384,10,64]{1,3,2,0:T(8,128)(2,1)} %get-tuple-element.127, s32[]{:T(128)} %get-tuple-element.126, f32[10,384,922]{1,2,0:T(8,128)} %get-tuple-element.117, f32[10,384]{1,0:T(8,128)S(1)} %get-tuple-element.118, bf16[2,922,10,64]{1,3,2,0:T(8,128)(2,1)} %get-tuple-element.135), kind=kOutput, calls=%fused_computation.17.clone.1 | convolution fusion | flops 460508160 | bytes 16072704 | tf_op jit(solution)/shard_map/while/body/eval_jaxpr/hqk,khe->qhe/dot_general | solution.py:145
  128.0 9.4 %fusion.125 = (f32[10,384]{1,0:T(8,128)S(1)}, f32[10,384,922]{1,2,0:T(8,128)}) fusion(pred[922]{0:T(1024)(128)(4,1)S(1)} %get-tuple-element.136, bf16[2,922,10,64]{1,3,2,0:T(8,128)(2,1)} %get-tuple-element.138, s32[]{:T(128)} %get-tuple-element.126, bf16[2,384,10,64]{1,3,2,0:T(8,128)(2,1)} %get-tuple-element.137), kind=kOutput, calls=%fused_computation.137.clone.1 | convolution fusion | flops 467344288 | bytes 15981466 | tf_op jit(solution)/shard_map/while/body/eval_jaxpr/sub | solution.py:142
  137.4 7.6 %fusion.126 = bf16[2,384,10,64]{1,3,2,0:T(8,128)(2,1)} fusion(bf16[2,384,10,64]{1,3,2,0:T(8,128)(2,1)} %get-tuple-element.127, s32[]{:T(128)} %get-tuple-element.126, f32[10,384,922]{1,2,0:T(8,128)} %get-tuple-element.117, f32[10,384]{1,0:T(8,128)S(1)} %get-tuple-element.118, bf16[2,922,10,64]{1,3,2,0:T(8,128)(2,1)} %get-tuple-element.135), kind=kOutput, calls=%fused_computation.17.clone.1 | convolution fusion | flops 460508160 | bytes 16072704 | tf_op jit(solution)/shard_map/while/body/eval_jaxpr/hqk,khe->qhe/dot_general | solution.py:145
  145.1 6.0 %convolution_convert_fusion = bf16[2,384,2432]{2,1,0:T(8,128)(2,1)} fusion(bf16[2,384,640]{1,2,0:T(8,128)(2,1)} %bitcast.152, bf16[640,2432]{1,0:T(8,128)(2,1)S(1)} %copy-done), kind=kOutput, calls=%fused_computation.37 | convolution fusion | flops 2392621056 | bytes 7831552 | tf_op jit(solution)/shard_map/brn,nd->brd/dot_general | solution.py:153
  152.5 24.2 %all-reduce.2.cloned.1.call-done = bf16[2,384,2432]{2,1,0:T(8,128)(2,1)} async-done(((bf16[2,384,2432]{2,1,0:T(8,128)(2,1)}), bf16[2,384,2432]{2,1,0:T(8,128)(2,1)}) %all-reduce.2.cloned.1.call-update) | async-done | bytes 3735568 | tf_op jit(solution)/shard_map/psum | solution.py:154
  176.7 4.4 %fusion.48 = f32[2,384]{1,0:T(2,128)S(1)} fusion(bf16[2,384,2432]{2,1,0:T(8,128)(2,1)} %all-reduce.2.cloned.1.call-done, f32[2,2432]{1,0:T(2,128)S(1)} %copy-done.7, f32[384,2432]{1,0:T(8,128)} %copy-done.1), kind=kLoop, calls=%fused_computation.35 | loop fusion | flops 7470336 | bytes 7493632 | tf_op jit(solution)/shard_map/reduce_sum | solution.py:25
  182.1 1.6 multiply_reduce_fusion
  183.7 2.2 %fusion.54 = f32[2,384,64]{1,2,0:T(8,128)S(1)} fusion(bf16[2,384,2432]{2,1,0:T(8,128)(2,1)S(1)} %copy-done.4, f32[2,2432]{1,0:T(2,128)S(1)} %copy-done.8, f32[2,2432]{1,0:T(2,128)S(1)} %copy-done.9, f32[2,384]{1,0:T(2,128)S(1)} %add_rsqrt_fusion.3, f32[2,384]{1,0:T(2,128)S(1)} %broadcast_multiply_fusion, f32[2,2432]{1,0:T(2,128)S(1)} %copy-done.7, ...), kind=kOutput, calls=%fused_computation.43 | convolution fusion | flops 254017536 | bytes 8043520 | tf_op jit(solution)/shard_map/brd,dc->brc/dot_general | solution.py:45
  187.4 14.0 %all_to_all.10 = bf16[16,6,128]{2,1,0:T(8,128)(2,1)S(1)} all-to-all(bf16[16,6,128]{2,1,0:T(8,128)(2,1)S(1)} %convert_element_type.91), channel_id=1, replica_groups=mesh['groups'=16,'mp'=2] {'groups'}, dimensions={0} | all-to-all | bytes 49152 | tf_op jit(solution)/shard_map/all_to_all | solution.py:162
  (98 shorter events, 24.0 us)
Async XLA Ops:
  6.5 138.5 %copy-start = (bf16[640,2432]{1,0:T(8,128)(2,1)S(1)}, bf16[640,2432]{1,0:T(8,128)(2,1)}, u32[]{:S(2)}) copy-start(bf16[640,2432]{1,0:T(8,128)(2,1)} %param.23) | copy-start | bytes 9338884
  8.1 1.6 copy-start.13
  9.7 28.3 %all-to-all-start = ((bf16[16,6,128]{2,1,0:T(8,128)(2,1)}), bf16[16,6,128]{2,1,0:T(8,128)(2,1)S(1)}, u32[]{:S(2)}, u32[]{:S(2)}) async-start(bf16[16,6,128]{2,1,0:T(8,128)(2,1)} %convert_element_type.75), calls=%async_computation | async-start | bytes 65536 | tf_op jit(solution)/shard_map/all_to_all | solution.py:95
  18.0 158.6 %all-reduce.2.cloned.1.call-start = ((), (), s32[]{:S(2)}) async-start(), calls=%async_computation.2 | async-start | bytes 7471104 | tf_op jit(solution)/shard_map/psum | solution.py:154
  20.9 17.1 %copy-start.11 = (s32[96]{0:T(128)}, s32[96]{0:T(128)S(1)}, u32[]{:S(2)}) copy-start(s32[96]{0:T(128)S(1)} %eq.81) | copy-start | bytes 1156
  21.1 16.9 %copy-start.12 = (pred[96]{0:T(512)(128)(4,1)}, pred[96]{0:T(512)(128)(4,1)S(1)}, u32[]{:S(2)}) copy-start(pred[96]{0:T(512)(128)(4,1)S(1)} %and.42) | copy-start | bytes 292
  21.2 19.9 %copy-start.5 = (bf16[64,2432]{1,0:T(8,128)(2,1)S(1)}, bf16[64,2432]{1,0:T(8,128)(2,1)}, u32[]{:S(2)}) copy-start(bf16[64,2432]{1,0:T(8,128)(2,1)} %param.20) | copy-start | bytes 933892
  41.8 1.8 copy-start.1
  42.3 1.3 copy-start.10
  43.6 16.7 %slice-start = ((s8[6225920]{0:T(1024)(128)(4,1)}), s8[4194304]{0:T(1024)(128)(4,1)S(1)}, s32[]{:S(2)}) async-start(s8[6225920]{0:T(1024)(128)(4,1)} %bitcast.144), calls=%async_computation.3 | async-start | bytes 8388608
  43.6 16.7 %slice-start.1 = ((s8[6225920]{0:T(1024)(128)(4,1)}), s8[2031616]{0:T(1024)(128)(4,1)S(1)}, s32[]{:S(2)}) async-start(s8[6225920]{0:T(1024)(128)(4,1)} %bitcast.144), calls=%async_computation.4 | async-start | bytes 4063232
  54.2 2.6 %copy-start.3 = (f32[2,384,3,640]{1,3,2,0:T(8,128)}, f32[2,384,3,640]{1,3,2,0:T(8,128)S(1)}, u32[]{:S(2)}) copy-start(f32[2,384,3,640]{1,3,2,0:T(8,128)S(1)} %fusion.45) | copy-start | bytes 17694724
  54.9 5.4 %copy-start.15 = (bf16[1,2,154,2432]{3,1,2,0:T(2,128)(2,1)S(1)}, bf16[1,2,154,2432]{3,1,2,0:T(2,128)(2,1)}, u32[]{:S(2)}) copy-start(bf16[1,2,154,2432]{3,1,2,0:T(2,128)(2,1)} %param.18) | copy-start | bytes 4494340
  58.4 45.4 %collective-permute-start = (bf16[2,384,2,640]{1,3,0,2:T(8,128)(2,1)}, bf16[2,384,2,640]{1,3,0,2:T(8,128)(2,1)}, u32[]{:S(2)}, u32[]{:S(2)}) collective-permute-start(bf16[2,384,2,640]{1,3,0,2:T(8,128)(2,1)} %pad_maximum_fusion.2), channel_id=1, source_target_pairs={{0,2},{2,0},{4,6},{6,4},{8,10},{10,8},{12,14},{14,12},{16,18},{18,... | collective-permute-start | bytes 5898248 | tf_op jit(solution)/shard_map/ppermute | solution.py:21
  60.3 5.1 %copy-start.17 = (s32[16]{0:T(128)S(1)}, s32[16]{0:T(128)}, u32[]{:S(2)}) copy-start(s32[16]{0:T(128)} %param.17) | copy-start | bytes 196
  60.3 8.3 %copy-start.14 = (s32[16]{0:T(128)S(1)}, s32[16]{0:T(128)}, u32[]{:S(2)}) copy-start(s32[16]{0:T(128)} %param.16) | copy-start | bytes 196
  151.0 25.6 %copy-start.7 = (f32[2,2432]{1,0:T(2,128)S(1)}, f32[2,2432]{1,0:T(2,128)}, u32[]{:S(2)}) copy-start(f32[2,2432]{1,0:T(2,128)} %get-tuple-element.60) | copy-start | bytes 58372
  176.7 4.4 %copy-start.2 = (f32[384,2432]{1,0:T(8,128)S(1)}, f32[384,2432]{1,0:T(8,128)}, u32[]{:S(2)}) copy-start(f32[384,2432]{1,0:T(8,128)} %copy-done.1) | copy-start | bytes 11206660
  176.7 5.4 %copy-start.4 = (bf16[2,384,2432]{2,1,0:T(8,128)(2,1)S(1)}, bf16[2,384,2432]{2,1,0:T(8,128)(2,1)}, u32[]{:S(2)}) copy-start(bf16[2,384,2432]{2,1,0:T(8,128)(2,1)} %all-reduce.2.cloned.1.call-done) | copy-start | bytes 11206660
  182.0 1.6 copy-start.8
  182.1 1.6 copy-start.9
  182.1 1.6 copy-start.16
  183.7 2.7 %copy-start.6 = (bf16[96,256]{1,0:T(8,128)(2,1)S(1)}, bf16[96,256]{1,0:T(8,128)(2,1)}, u32[]{:S(2)}) copy-start(bf16[96,256]{1,0:T(8,128)(2,1)} %all_gather.3) | copy-start | bytes 147460
Sparse Core Ops, SparseCore 0:
  151.2 25.4 all-reduce.1
where the time goes:
time: 211 us; the launch traced here: 210 us
  matrix products  62 us (29%)
  waiting for transfers between devices  47.3 us (22%)
  local copies, waits for them, and re-layouts  30.4 us (14%)
  other arithmetic  26.7 us (13%)
  between operations  17.1 us (8%)
  blocking collectives  16 us (8%)
  starting transfers between devices  10.3 us (5%)
    psum x1, waiting for transfers between devices, shards(): mixed = lax.psum(partial_sum.astype(jnp.bfloat16), 'mp').astype(jnp.float32)  24.2 us
    ppermute x1, waiting for transfers between devices, partner_2(): return lax.ppermute(value, axis, pairs)  23.1 us
    unnamed x42, local copies, waits for them, and re-layouts  20.8 us
    sub x2, matrix products, branch_attention(): raised = jnp.exp(scores - highest)  18.8 us
    dot_general x2, matrix products, branch_attention(): jnp.einsum('hqk,khe->qhe', weights, branch_values, preferred_element_type...  15.2 us
    all_to_all x1, blocking collectives, shards(): lax.all_to_all(homeward.astype(jnp.bfloat16), 'groups', split_axis=0, con...  14 us
    dot_general x1, matrix products, shards(): jnp.einsum('brd,dcn->brcn', normed, w_qkv, preferred_element_type=jnp.flo...  10.6 us
    all_to_all x1, starting transfers between devices, shards(): lax.all_to_all(outbound.astype(jnp.bfloat16), 'groups', split_axis=0, con...  8.31 us
  transfers between devices with their start and end apart: 3, of which 2 were waited for; matrix products, arithmetic and copies ran while one was open for 18% of the time, Pallas kernels for 0%

commit v1 on v0

v1 whole, which is shorter than its diff:
```python
import functools

import jax
import jax.numpy as jnp
from jax import lax
from jax.experimental import pallas as pl
from jax.experimental.pallas import tpu as pltpu
from jax.sharding import PartitionSpec as P

HEAD = 64
CH = 64
TILE = 4
LANES = 128
PACK = 16

GUIDE = 3.5
STEP = -0.25
EPS = 1e-06
LOG2E = 1.4426950408889634
DEAD = -1e30

F32 = jnp.float32
BF16 = jnp.bfloat16
VMEM_LIMIT = 56 * 2**20


def round_up(value, step):
    return (value + step - 1) // step * step


def mm(left, right):
    return jnp.dot(left, right, preferred_element_type=F32)


def mm_nt(left, right):
    return lax.dot_general(left, right, (((1,), (1,)), ((), ())), preferred_element_type=F32)


def iota(shape, dim):
    return lax.broadcasted_iota(jnp.int32, shape, dim)


def two_terms(value):
    high = value.astype(BF16)
    return high, (value - high.astype(F32)).astype(BF16)


def one_hot(mask):
    return jnp.where(mask, 1.0, 0.0).astype(BF16)


def spec(space=pltpu.VMEM):
    return pl.BlockSpec(memory_space=space)


def params(**more):
    return pltpu.CompilerParams(vmem_limit_bytes=VMEM_LIMIT, **more)


def own_bucket(slots, tiles):
    target = slots // tiles
    row = target.astype(F32)
    diagonal = iota((tiles, tiles), 0) == iota((tiles, tiles), 1)
    column = jnp.sum(jnp.where(diagonal, row, 0.0), axis=1, keepdims=True)
    earlier = (column == row) & (iota((tiles, tiles), 0) < iota((tiles, tiles), 1))
    rank = jnp.sum(jnp.where(earlier, 1.0, 0.0), axis=0, keepdims=True).astype(jnp.int32)
    return target, rank


def send_kernel(capacity, block, where_ref, slots_ref, latents_ref, out_ref):
    tiles = latents_ref.shape[0]
    groups_n = out_ref.shape[0]
    target, rank = own_bucket(slots_ref[pl.ds(where_ref[0], 1), :], tiles)
    rows = groups_n * block
    bucket = iota((rows, tiles), 0)
    first = target * block + rank
    second = (target ^ 1) * block + capacity + rank
    sender = one_hot((bucket == first) | (bucket == second))
    sent = mm(sender, latents_ref[...].astype(BF16)).astype(BF16).reshape(groups_n, block, -1)
    out_ref[:, 0] = sent
    out_ref[:, 1] = sent


def tables(slots, group, tiles, capacity, block, offset):
    groups_n = slots.shape[0]
    target = slots // tiles
    placed = slots - target * tiles
    mine = target == group
    before = one_hot(iota((tiles, tiles), 0) < iota((tiles, tiles), 1))
    rank = mm(one_hot(mine), before)
    rank = jnp.where(mine, rank, float(capacity))
    columns = groups_n * block
    spread = one_hot(iota((groups_n, columns), 1) // block == iota((groups_n, columns), 0))
    turn = (((0,), (0,)), ((), ()))
    rank_of = lax.dot_general(rank.astype(BF16), spread, turn, preferred_element_type=F32)
    place_of = lax.dot_general(placed.astype(F32).astype(BF16), spread, turn, preferred_element_type=F32)
    level = (iota((tiles, columns), 1) % block - offset).astype(F32)
    hit = (rank_of == level) & (level >= 0.0) & (level < capacity)
    place = jnp.sum(jnp.where(hit, place_of + 1.0, 0.0), axis=0, keepdims=True) - 1.0
    return one_hot(iota((tiles, columns), 0).astype(F32) == place)


def fold_kernel(
    capacity,
    block,
    back,
    where_ref,
    slots_ref,
    embed_ref,
    own_mod_ref,
    mate_mod_ref,
    w_ref,
    own_out,
    mate_out,
    own_bias,
    mate_bias,
    gram_out,
    place_out,
    home_out,
    left,
):
    step = pl.program_id(0)
    depth = embed_ref.shape[1]
    own_rows = 4 * CH

    @pl.when(step == 0)
    def _():
        embed = embed_ref[...].astype(F32)
        centred = embed - jnp.mean(embed, axis=1, keepdims=True)
        for side, mod_ref in ((0, own_mod_ref), (1, mate_mod_ref)):
            base = side * (own_rows + 2 * PACK)
            for branch in range(2):
                scaled = centred * (1.0 + mod_ref[1, branch : branch + 1, :])
                high, low = two_terms(scaled)
                left[pl.ds(base + branch * 2 * CH, CH), :] = high
                left[pl.ds(base + branch * 2 * CH + CH, CH), :] = low
            high, low = two_terms(mod_ref[0])
            shifts = jnp.concatenate([high.astype(F32), low.astype(F32)], axis=0)
            shifts = jnp.concatenate([shifts, jnp.zeros((2 * PACK - 4, depth), F32)], axis=0)
            left[pl.ds(base + own_rows, 2 * PACK), :] = shifts.astype(BF16)
        high, low = two_terms(centred)
        parts = mm_nt(high, high) + (mm_nt(high, low) + mm_nt(low, high))
        parts = parts * (1.0 / depth)
        top, rest = two_terms(parts)
        bottom = (parts - top.astype(F32) - rest.astype(F32)).astype(BF16)
        gram_out[0:CH, :] = top
        gram_out[CH : 2 * CH, :] = rest
        gram_out[2 * CH : 3 * CH, :] = bottom
        gram_out[3 * CH : 4 * CH, :] = jnp.zeros((CH, CH), BF16)
        tiles = slots_ref.shape[1]
        slots = slots_ref[...]
        group = where_ref[0]
        place_out[0:tiles, :] = tables(slots, group, tiles, capacity, block, 0)
        place_out[tiles : 2 * tiles, :] = tables(slots, group ^ 1, tiles, capacity, block, capacity)
        home_out[...] = tables(slots, group, tiles, capacity, back, 0)

    def keep(product, out_ref, bias_ref):
        for branch in range(2):
            base = branch * 2 * CH
            value = product[base : base + CH] + product[base + CH : base + 2 * CH]
            high, low = two_terms(value)
            out_ref[branch, 0:CH, :] = high
            out_ref[branch, CH : 2 * CH, :] = low
        bias = product[own_rows : own_rows + 2] + product[own_rows + 2 : own_rows + 4]
        bias_ref[0:2, :] = bias

    half = own_rows + 2 * PACK

    @pl.when(step == 0)
    def _():
        keep(mm(left[0:half, :], w_ref[0]), own_out, own_bias)

    @pl.when(step > 0)
    def _():
        product = mm(left[...], w_ref[0])
        keep(product[0:half], own_out, own_bias)
        keep(product[half:], mate_out, mate_bias)


def attend_kernel(
    where_ref,
    live_ref,
    partner_ref,
    arrived_ref,
    place_ref,
    gram_ref,
    own_ref,
    mate_ref,
    own_bias_ref,
    mate_bias_ref,
    text_ref,
    gains_ref,
    keep_ref,
    send_ref,
    tokens_ref,
    proj,
    mate_proj,
    keys_bf,
    values_bf,
):
    group, member = where_ref[0], where_ref[1]
    groups_n, _, block, narrow = arrived_ref.shape
    tiles = place_ref.shape[0] // 2
    rows = tiles * TILE
    half_rows = rows // 2
    width = keep_ref.shape[2]
    text = text_ref.shape[2]
    keys_n = keys_bf.shape[0]
    mate = partner_ref[group]
    own_len = live_ref[group]
    mate_len = jnp.where(mate != group, live_ref[mate], 0)

    own_parts, mate_parts = [], []
    for turn in range(2):
        source = member ^ turn
        block_rows = arrived_ref[:, pl.ds(source, 1)].reshape(groups_n * block, narrow)
        found = mm(place_ref[...], block_rows)
        for parts, base in ((own_parts, 0), (mate_parts, tiles)):
            pair = found[base : base + tiles]
            parts.append(jnp.concatenate([pair[:, :CH], pair[:, :CH]], axis=1))
            parts.append(jnp.concatenate([pair[:, CH:], pair[:, CH:]], axis=1))
    own_tokens = jnp.concatenate(own_parts, axis=0)
    mate_tokens = jnp.concatenate(mate_parts, axis=0)
    tokens_ref[...] = own_tokens[:half_rows].astype(BF16)

    def spread_of(tokens):
        narrow_tokens = tokens.astype(BF16)
        image = mm(narrow_tokens, gram_ref[0 : 2 * CH]) + mm(narrow_tokens, gram_ref[2 * CH :])
        variance = jnp.sum(image * tokens[:, :CH], axis=1, keepdims=True)
        return lax.rsqrt(jnp.maximum(variance, 0.0) + EPS)

    own_scale = spread_of(own_tokens)
    mate_scale = spread_of(mate_tokens)
    own_narrow = own_tokens.astype(BF16)
    mate_narrow = mate_tokens.astype(BF16)

    row = iota((rows, 1), 0)
    turn_of = row // half_rows
    inside = row - turn_of * half_rows
    second = inside // tiles
    slot = (inside - second * tiles) * TILE + 2 * (turn_of ^ member) + second
    own_dead = jnp.where(slot < own_len, 0.0, DEAD)
    mate_dead = jnp.where(slot < mate_len, 0.0, DEAD)
    rest = keys_n - 2 * rows
    text_dead = jnp.where(iota((rest, 1), 0) < text, 0.0, DEAD)
    dead = jnp.concatenate([own_dead, mate_dead, text_dead], axis=0)

    lane = iota((1, LANES), 1)
    even = lane < HEAD
    averaging = jnp.where(
        iota((LANES, LANES), 0) // HEAD == iota((LANES, LANES), 1) // HEAD, 1.0 / HEAD, 0.0
    ).astype(BF16)

    def head_norm(value, gains):
        square = mm((value * value).astype(BF16), averaging)
        return value * (lax.rsqrt(square + EPS) * gains)

    values_bf[2 * rows :, :] = jnp.zeros((rest, LANES), BF16)

    for branch in range(2):
        proj[...] = (
            mm(own_narrow, own_ref[branch]) * own_scale + own_bias_ref[branch : branch + 1, :]
        )
        mate_proj[...] = (
            mm(mate_narrow, mate_ref[branch]) * mate_scale + mate_bias_ref[branch : branch + 1, :]
        )
        for pair in range(width // LANES):
            at = pair * LANES
            query = head_norm(proj[:, at : at + LANES], gains_ref[0:1, :] * (LOG2E * HEAD**-0.5))
            keys = jnp.concatenate(
                [
                    head_norm(proj[:, width + at : width + at + LANES], gains_ref[1:2, :]),
                    head_norm(mate_proj[:, at : at + LANES], gains_ref[1:2, :]),
                    head_norm(text_ref[branch, 0, :, at : at + LANES], gains_ref[2:3, :]),
                    jnp.zeros((rest - text, LANES), F32),
                ],
                axis=0,
            )
            values_bf[0:rows, :] = proj[:, 2 * width + at : 2 * width + at + LANES].astype(BF16)
            values_bf[rows : 2 * rows, :] = mate_proj[:, width + at : width + at + LANES].astype(BF16)
            values_bf[2 * rows : 2 * rows + text, :] = text_ref[branch, 1, :, at : at + LANES].astype(BF16)
            values = values_bf[...]
            outs = []
            for side in range(2):
                inside_head = even if side == 0 else jnp.logical_not(even)
                marker = lane == (HEAD if side == 0 else 0)
                one_query = jnp.where(inside_head, query, jnp.where(marker, 1.0, 0.0)).astype(BF16)
                one_keys = jnp.where(inside_head, keys, jnp.where(marker, dead, 0.0)).astype(BF16)
                one_values = jnp.where(inside_head, values, jnp.ones_like(values))
                scores = mm_nt(one_query, one_keys)
                highest = jnp.max(scores, axis=1, keepdims=True)
                weights = jnp.exp2(scores - highest).astype(BF16)
                outs.append(mm(weights, one_values))
            total = jnp.where(even, outs[1], outs[0])
            total = jnp.concatenate([total[:, HEAD:], total[:, :HEAD]], axis=1)
            merged = (jnp.where(even, outs[0], outs[1]) / total).astype(BF16)
            keep_ref[branch, :, at : at + LANES] = merged[:half_rows]
            send_ref[branch, :, at : at + LANES] = merged[half_rows:]


def finish_kernel(
    back,
    where_ref,
    live_ref,
    kept_ref,
    came_ref,
    w_own_ref,
    w_came_ref,
    tokens_ref,
    embed_ref,
    mod_ref,
    w_final_ref,
    home_ref,
    out_ref,
):
    group, member = where_ref[0], where_ref[1]
    half_rows = tokens_ref.shape[0]
    tiles = home_ref.shape[0]
    hidden = mm(tokens_ref[:, :CH], embed_ref[...])
    velocities = []
    for branch in range(2):
        mixed = mm(kept_ref[branch], w_own_ref[...]).astype(BF16).astype(F32) + mm(
            came_ref[branch], w_came_ref[...]
        ).astype(BF16).astype(F32)
        state = hidden + mod_ref[2, branch : branch + 1, :] * mixed
        centred = state - jnp.mean(state, axis=1, keepdims=True)
        spread = jnp.mean(centred * centred, axis=1, keepdims=True)
        normed = centred * lax.rsqrt(spread + EPS)
        final = normed * (1.0 + mod_ref[4, branch : branch + 1, :]) + mod_ref[3, branch : branch + 1, :]
        velocities.append(mm_nt(final.astype(BF16), w_final_ref[...]))
    guided = velocities[1] + GUIDE * (velocities[0] - velocities[1])
    row = iota((half_rows, 1), 0)
    second = row // tiles
    slot = (row - second * tiles) * TILE + 2 * member + second
    guided = jnp.where(slot < live_ref[group], guided, 0.0)
    columns = jnp.concatenate([guided[:tiles], guided[tiles:]], axis=1).astype(BF16)
    out_ref[...] = lax.dot_general(
        home_ref[...], columns, (((0,), (0,)), ((), ())), preferred_element_type=F32
    ).astype(BF16)


def update_kernel(back, where_ref, slots_ref, latents_ref, returned_ref, out_ref):
    tiles = latents_ref.shape[0]
    target, rank = own_bucket(slots_ref[pl.ds(where_ref[0], 1), :], tiles)
    sender = one_hot(iota((returned_ref.shape[0], tiles), 0) == target * back + rank)
    guided = lax.dot_general(
        sender, returned_ref[...], (((0,), (0,)), ((), ())), preferred_element_type=F32
    )
    out_ref[...] = latents_ref[...] + STEP * guided


def shards(
    latents,
    tile_slot,
    live,
    partner,
    text_states,
    modulation,
    w_embed,
    w_qkv,
    w_text_kv,
    w_out,
    w_final,
    norm_gains,
):
    groups_n = lax.axis_size("groups")
    group = lax.axis_index("groups").astype(jnp.int32)
    member = lax.axis_index("mp").astype(jnp.int32)
    tiles, narrow = latents.shape
    rows = tiles * TILE
    depth = w_embed.shape[1]
    width = w_out.shape[0]
    text = text_states.shape[2]
    capacity = max(2, (tiles + groups_n - 1) // groups_n)
    block = round_up(2 * capacity, PACK)
    back = round_up(capacity, PACK)
    where = jnp.stack([group, member])
    slots = tile_slot.reshape(groups_n, tiles)
    both = ("groups", "mp")

    outbound = pl.pallas_call(
        functools.partial(send_kernel, capacity, block),
        out_shape=jax.ShapeDtypeStruct((groups_n, 2, block, narrow), BF16),
        in_specs=[spec(pltpu.SMEM), spec(), spec()],
        out_specs=spec(),
        compiler_params=params(),
    )(where, slots, latents)
    arrived = lax.all_to_all(
        outbound.reshape(groups_n * 2, block, narrow), both, split_axis=0, concat_axis=0, tiled=True
    ).reshape(groups_n, 2, block, narrow)

    adaptive = jnp.swapaxes(modulation[0], 0, 1)
    pairs = [(source, source ^ 1) for source in range(groups_n)]
    mate_mod = lax.ppermute(adaptive[:2], "groups", pairs)
    came_w_out = lax.ppermute(w_out, "mp", [(0, 1), (1, 0)])

    text_proj = jnp.einsum(
        "btd,dcn->bctn", text_states[0], w_text_kv, preferred_element_type=F32
    )

    left_rows = 2 * (4 * CH + 2 * PACK)
    constant2 = lambda i: (0, 0)
    constant3 = lambda i: (0, 0, 0)
    later = lambda i: jnp.maximum(i - 1, 0)
    own_fold, mate_fold, own_bias, mate_bias, gram, place, home = pl.pallas_call(
        functools.partial(fold_kernel, capacity, block, back),
        grid=(3,),
        out_shape=[
            jax.ShapeDtypeStruct((2, 2 * CH, 3 * width), BF16),
            jax.ShapeDtypeStruct((2, 2 * CH, 2 * width), BF16),
            jax.ShapeDtypeStruct((8, 3 * width), F32),
            jax.ShapeDtypeStruct((8, 2 * width), F32),
            jax.ShapeDtypeStruct((4 * CH, CH), BF16),
            jax.ShapeDtypeStruct((2 * tiles, groups_n * block), BF16),
            jax.ShapeDtypeStruct((tiles, groups_n * back), BF16),
        ],
        in_specs=[
            spec(pltpu.SMEM),
            pl.BlockSpec((groups_n, tiles), constant2),
            pl.BlockSpec((CH, depth), constant2),
            pl.BlockSpec((5, 2, depth), constant3),
            pl.BlockSpec((2, 2, depth), constant3),
            pl.BlockSpec((1, depth, width), lambda i: (i, 0, 0)),
        ],
        out_specs=[
            pl.BlockSpec((2, 2 * CH, width), lambda i: (0, 0, i)),
            pl.BlockSpec((2, 2 * CH, width), lambda i: (0, 0, later(i))),
            pl.BlockSpec((8, width), lambda i: (0, i)),
            pl.BlockSpec((8, width), lambda i: (0, later(i))),
            pl.BlockSpec((4 * CH, CH), constant2),
            pl.BlockSpec((2 * tiles, groups_n * block), constant2),
            pl.BlockSpec((tiles, groups_n * back), constant2),
        ],
        scratch_shapes=[pltpu.VMEM((left_rows, depth), BF16)],
        compiler_params=params(),
        cost_estimate=pl.CostEstimate(
            flops=2 * left_rows * depth * 3 * width, bytes_accessed=2 * depth * 3 * width, transcendentals=0
        ),
    )(where, slots, w_embed, adaptive, mate_mod, jnp.swapaxes(w_qkv, 0, 1))

    gains = jnp.concatenate([norm_gains, norm_gains], axis=1)
    keys_n = round_up(2 * rows + text, LANES)
    half = jax.ShapeDtypeStruct((2, rows // 2, width), BF16)
    kept, sent, tokens = pl.pallas_call(
        attend_kernel,
        out_shape=[half, half, jax.ShapeDtypeStruct((rows // 2, 2 * CH), BF16)],
        in_specs=[spec(pltpu.SMEM)] * 3 + [spec()] * 9,
        out_specs=[spec()] * 3,
        scratch_shapes=[
            pltpu.VMEM((rows, 3 * width), F32),
            pltpu.VMEM((rows, 2 * width), F32),
            pltpu.VMEM((keys_n, LANES), BF16),
            pltpu.VMEM((keys_n, LANES), BF16),
        ],
        compiler_params=params(),
    )(
        where,
        live,
        partner,
        arrived,
        place,
        gram,
        own_fold,
        mate_fold,
        own_bias,
        mate_bias,
        text_proj,
        gains,
    )
    came = lax.ppermute(sent, "mp", [(0, 1), (1, 0)])

    homeward = pl.pallas_call(
        functools.partial(finish_kernel, back),
        out_shape=jax.ShapeDtypeStruct((groups_n * back, narrow), BF16),
        in_specs=[spec(pltpu.SMEM)] * 2 + [spec()] * 9,
        out_specs=spec(),
        compiler_params=params(),
    )(where, live, kept, came, w_out, came_w_out, tokens, w_embed, adaptive, w_final.T, home)
    returned = lax.all_to_all(
        homeward.reshape(groups_n, back, narrow), "groups", split_axis=0, concat_axis=0, tiled=True
    ).reshape(groups_n * back, narrow)
    return pl.pallas_call(
        functools.partial(update_kernel, back),
        out_shape=jax.ShapeDtypeStruct((tiles, narrow), F32),
        in_specs=[spec(pltpu.SMEM)] + [spec()] * 3,
        out_specs=spec(),
        compiler_params=params(),
    )(where, slots, latents, returned)


def solution(mesh):
    placed = (
        P("groups", "mp"),
        P(),
        P(),
        P(),
        P("groups", None, None, None),
        P("groups", None, None, None),
        P(),
        P(None, None, "mp"),
        P(None, None, "mp"),
        P("mp", None),
        P(),
        P(),
    )
    return jax.shard_map(
        shards, mesh=mesh, in_specs=placed, out_specs=P("groups", "mp"), check_vma=False
    )
```

time: 211 us -> 77.7 us (0.37)
  matrix products: 62 us -> 6.25 us
  waiting for transfers between devices: 47.3 us -> 1.84 us
  Pallas kernels: 0 us -> 40.9 us
  local copies, waits for them, and re-layouts: 30.4 us -> 4.17 us
  other arithmetic: 26.7 us -> 1.3 us
  between operations: 17.1 us -> 0.06 us
    pallas_call x0 -> x5, Pallas kernels: none -> 40.9 us  [the longest x1 17.5 us: shards(): pl.pallas_call(attend_kernel, out_shape=[half, half, jax.ShapeDtypeStruct...]
    dot_general x11 -> x1, matrix products: 43.2 us -> 6.25 us  [shards(): jnp.einsum('btd,dcn->bctn', text_states[0], w_text_kv, preferred_element_...]
    psum x1 -> x0, waiting for transfers between devices: 24.2 us -> none  [shards(): mixed = lax.psum(partial_sum.astype(jnp.bfloat16), 'mp').astype(jnp.float32)]
    ppermute x1 -> x3, waiting for transfers between devices: 23.1 us -> 1.84 us  [the longest x1 1.83 us: shards(): came = lax.ppermute(sent, 'mp', [(0, 1), (1, 0)])]
    sub x2 -> x0, matrix products: 18.8 us -> none  [branch_attention(): raised = jnp.exp(scores - highest)]
    unnamed x42 -> x10, local copies, waits for them, and re-layouts: 20.8 us -> 2.03 us
    reduce_sum x7 -> x0, other arithmetic: 9.21 us -> none  [the longest x1 4.38 us: layer_norm(): centre = jnp.mean(inputs, axis=-1, keepdims=True)]
    convert_element_type x3 -> x0, other arithmetic: 5.93 us -> none  [head_norm(): return (inputs * lax.rsqrt(square + EPS) * gains).astype(jnp.bfloat16)]
  transfers between devices with their start and end apart: 3 -> 4, of which waited for: 2 -> 1; matrix products, arithmetic and copies ran while one was open for 18% -> 13% of each run, Pallas kernels for 0% -> 38%
where the time goes in v1:
time: 77.7 us; the launch traced here: 77.3 us
  Pallas kernels  40.9 us (53%)
  blocking collectives  14.5 us (19%)
  starting transfers between devices  8.25 us (11%)
  matrix products  6.25 us (8%)
  local copies, waits for them, and re-layouts  4.17 us (5%)
  waiting for transfers between devices  1.84 us (2%)
  other arithmetic  1.3 us (2%)
    pallas_call x1, Pallas kernels, shards(): pl.pallas_call(attend_kernel, out_shape=[half, half, jax.ShapeDtypeStruct...  17.5 us
    all_to_all x1, blocking collectives, shards(): lax.all_to_all(homeward.reshape(groups_n, back, narrow), 'groups', split_...  14.5 us
    pallas_call x1, Pallas kernels, shards(): pl.pallas_call(functools.partial(fold_kernel, capacity, block, back), gri...  10.4 us
    pallas_call x1, Pallas kernels, shards(): pl.pallas_call(functools.partial(finish_kernel, back), out_shape=jax.Shap...  9.54 us
    dot_general x1, matrix products, shards(): jnp.einsum('btd,dcn->bctn', text_states[0], w_text_kv, preferred_element_...  6.25 us
    all_to_all x1, starting transfers between devices, shards(): lax.all_to_all(outbound.reshape(groups_n * 2, block, narrow), both, split...  4.92 us
    ppermute x1, starting transfers between devices, shards(): mate_mod = lax.ppermute(adaptive[:2], 'groups', pairs)  2.63 us
    unnamed x10, local copies, waits for them, and re-layouts  2.03 us
  transfers between devices with their start and end apart: 4, of which 1 were waited for; matrix products, arithmetic and copies ran while one was open for 13% of the time, Pallas kernels for 38%

profile of v1, /device:TPU:0, one launch (start us, length us, event | category | flops | bytes accessed | tf_op | source)
XLA Modules:
  0.0 77.3 jit_solution(3170886892594009457)
XLA Ops:
  0.0 0.0 copy-start
  0.0 0.5 collective-permute-start.2
  0.5 0.8 %slice.4 = f32[2,2,2432]{2,1,0:T(2,128)S(1)} slice(f32[5,2,2432]{2,1,0:T(2,128)} %bitcast.27), slice={[0:2], [0:2], [0:2432]} | slice | bytes 77824 | tf_op jit(solution)/shard_map/slice | solution.py:394
  1.2 2.6 %collective-permute-start = (f32[2,2,2432]{2,1,0:T(2,128)S(1)}, f32[2,2,2432]{2,1,0:T(2,128)S(1)}, u32[]{:S(2)}, u32[]{:S(2)}) collective-permute-start(f32[2,2,2432]{2,1,0:T(2,128)S(1)} %slice.4), channel_id=1, source_target_pairs={{0,2},{2,0},{4,6},{6,4},{8,10},{10,8},{12,14},{14,12},{16,18},{18,... | collective-permute-start | bytes 116744 | tf_op jit(solution)/shard_map/ppermute | solution.py:394
  3.9 1.4 %reshape.15.slots_ref = s32[16,96]{1,0:T(8,128)} reshape(s32[1536]{0:T(1024)} %param.13) | data formatting | bytes 12288 | tf_op jit(solution)/shard_map/reshape | solution.py:378
  5.2 0.6 pad_add_fusion.where_ref
  5.9 1.7 %shard_map.118 = bf16[16,2,16,128]{3,2,1,0:T(8,128)(2,1)} custom-call(s32[2]{0:T(128)} %pad_add_fusion.where_ref, s32[16,96]{1,0:T(8,128)} %reshape.15.slots_ref, f32[96,128]{1,0:T(8,128)} %latents_ref.3), custom_call_target="tpu_custom_call" | custom-call | tf_op jit(solution)/shard_map/pallas_call | solution.py:381
  7.6 4.9 %all-to-all-start = ((bf16[32,16,128]{2,1,0:T(8,128)(2,1)}), bf16[32,16,128]{2,1,0:T(8,128)(2,1)S(1)}, u32[]{:S(2)}, u32[]{:S(2)}) async-start(bf16[32,16,128]{2,1,0:T(8,128)(2,1)} %bitcast.23), calls=%async_computation | async-start | bytes 262144 | tf_op jit(solution)/shard_map/all_to_all | solution.py:388
  12.6 0.0 copy-start.3
  12.6 6.2 %fusion.4.text_ref = f32[2,2,154,640]{3,2,1,0:T(8,128)} fusion(bf16[2,154,2432,1]{2,0,1,3:T(2,128)(2,1)S(1)} %bitcast.21, bf16[2432,2,640]{2,1,0:T(2,128)(2,1)} %param.20), kind=kOutput, calls=%fused_computation.4 | convolution fusion | flops 1917583360 | bytes 9300992 | tf_op jit(solution)/shard_map/btd,dcn->bctn/dot_general | solution.py:397
  18.8 0.7 pad_maximum_fusion.gains_ref
  19.5 0.0 collective-permute-done.mate_mod_ref
  19.5 0.6 copy-done.4
  20.1 10.4 %shard_map.119 = (bf16[2,128,1920]{2,1,0:T(8,128)(2,1)}, bf16[2,128,1280]{2,1,0:T(8,128)(2,1)}, f32[8,1920]{1,0:T(8,128)}, f32[8,1280]{1,0:T(8,128)}, bf16[256,6...) custom-call(s32[2]{0:T(128)} %pad_add_fusion.where_ref, s32[16,96]{1,0:T(8,128)} %reshape.15.slots_ref, ...), custom_call_target="tpu_custom_call" | custom-call | flops 5379194880 | bytes 9338880 | tf_op jit(solution)/shard_map/pallas_call | solution.py:405
  30.5 0.0 all-to-all-done
  30.5 0.6 copy-done.1
  31.1 17.5 %shard_map.120 = (bf16[2,192,640]{2,1,0:T(8,128)(2,1)}, bf16[2,192,640]{2,1,0:T(8,128)(2,1)}, bf16[192,128]{1,0:T(8,128)(2,1)}) custom-call(s32[2]{0:T(128)} %pad_add_fusion.where_ref, s32[16]{0:T(128)} %live_ref.3, s32[16]{0:T(128)} %partner_ref.1, bf16[16,2,16,128]{3,2,1,0:T(8,128)(2,1)} %bitcast.22, bf16[192,256]{1,0:T(8,128)(2,1)} %get-tuple-element.15.place_ref, ...), custom_call_target="tpu_custom_call" | custom-call | tf_op jit(solution)/shard_map/pallas_call | solution.py:444
  48.6 0.2 collective-permute-start.1
  48.8 1.8 %collective-permute-done.1.came_ref = bf16[2,192,640]{2,1,0:T(8,128)(2,1)S(1)} collective-permute-done((bf16[2,192,640]{2,1,0:T(8,128)(2,1)}, bf16[2,192,640]{2,1,0:T(8,128)(2,1)S(1)}, u32[]{:S(2)}, u32[]{:S(2)}) %collective-permute-start.1) | collective-permute-done | bytes 491552 | tf_op jit(solution)/shard_map/ppermute | solution.py:470
  50.7 0.0 collective-permute-done.2.w_came_ref
  50.7 0.8 copy-done.2
  51.5 9.5 %shard_map.121 = bf16[256,128]{1,0:T(8,128)(2,1)} custom-call(s32[2]{0:T(128)} %pad_add_fusion.where_ref, s32[16]{0:T(128)} %live_ref.3, bf16[2,192,640]{2,1,0:T(8,128)(2,1)} %get-tuple-element.21.kept_ref, bf16[2,192,640]{2,1,0:T(8,128)(2,1)} %copy-done.2, bf16[640,2432]{1,0:T(8,128)(2,1)} %w_own_ref.1, ...), custom_call_target="tpu_custom_call" | custom-call | tf_op jit(solution)/shard_map/pallas_call | solution.py:472
  61.0 14.5 %all_to_all.10 = bf16[16,16,128]{2,1,0:T(8,128)(2,1)} all-to-all(bf16[16,16,128]{2,1,0:T(8,128)(2,1)} %bitcast.25), channel_id=1, replica_groups=mesh['groups'=16,'mp'=2] {'groups'}, dimensions={0} | all-to-all | bytes 131072 | tf_op jit(solution)/shard_map/all_to_all | solution.py:479
  75.5 1.8 %shard_map.122 = f32[96,128]{1,0:T(8,128)} custom-call(s32[2]{0:T(128)} %pad_add_fusion.where_ref, s32[16,96]{1,0:T(8,128)} %reshape.15.slots_ref, f32[96,128]{1,0:T(8,128)} %latents_ref.3, bf16[256,128]{1,0:T(8,128)(2,1)} %bitcast.26), custom_call_target="tpu_custom_call" | custom-call | tf_op jit(solution)/shard_map/pallas_call | solution.py:482
  (5 shorter events, 0.0 us)
Async XLA Ops:
  0.0 12.5 %copy-start = (bf16[1,2,154,2432]{3,1,2,0:T(2,128)(2,1)S(1)}, bf16[1,2,154,2432]{3,1,2,0:T(2,128)(2,1)}, u32[]{:S(2)}) copy-start(bf16[1,2,154,2432]{3,1,2,0:T(2,128)(2,1)} %param.16) | copy-start | bytes 4494340
  0.0 50.7 %collective-permute-start.2 = (bf16[640,2432]{1,0:T(8,128)(2,1)}, bf16[640,2432]{1,0:T(8,128)(2,1)}, u32[]{:S(2)}, u32[]{:S(2)}) collective-permute-start(bf16[640,2432]{1,0:T(8,128)(2,1)} %w_own_ref.1), channel_id=1, source_target_pairs={{0,1},{1,0},{2,3},{3,2},{4,5},{5,4},{6,7},{7,6},{8,9},{9,8},{10,11... | collective-permute-start | bytes 9338888 | tf_op jit(solution)/shard_map/ppermute | solution.py:395
  1.2 18.2 %collective-permute-start = (f32[2,2,2432]{2,1,0:T(2,128)S(1)}, f32[2,2,2432]{2,1,0:T(2,128)S(1)}, u32[]{:S(2)}, u32[]{:S(2)}) collective-permute-start(f32[2,2,2432]{2,1,0:T(2,128)S(1)} %slice.4), channel_id=1, source_target_pairs={{0,2},{2,0},{4,6},{6,4},{8,10},{10,8},{12,14},{14,12},{16,18},{18,... | collective-permute-start | bytes 116744 | tf_op jit(solution)/shard_map/ppermute | solution.py:394
  7.6 22.9 %all-to-all-start = ((bf16[32,16,128]{2,1,0:T(8,128)(2,1)}), bf16[32,16,128]{2,1,0:T(8,128)(2,1)S(1)}, u32[]{:S(2)}, u32[]{:S(2)}) async-start(bf16[32,16,128]{2,1,0:T(8,128)(2,1)} %bitcast.23), calls=%async_computation | async-start | bytes 262144 | tf_op jit(solution)/shard_map/all_to_all | solution.py:388
  12.6 6.3 %copy-start.3 = (f32[3,64]{1,0:T(4,128)S(1)}, f32[3,64]{1,0:T(4,128)}, u32[]{:S(2)}) copy-start(f32[3,64]{1,0:T(4,128)} %param.23) | copy-start | bytes 2308
  19.5 0.6 copy-start.4
  30.5 0.7 copy-start.1
  48.6 2.1 %collective-permute-start.1 = (bf16[2,192,640]{2,1,0:T(8,128)(2,1)}, bf16[2,192,640]{2,1,0:T(8,128)(2,1)S(1)}, u32[]{:S(2)}, u32[]{:S(2)}) collective-permute-start(bf16[2,192,640]{2,1,0:T(8,128)(2,1)} %get-tuple-element.22), channel_id=1, source_target_pairs={{0,1},{1,0},{2,3},{3,2},{4,5},{5,4},{6,7},{7,6},{8,9},{9,8},{10,11... | collective-permute-start | bytes 1474568 | tf_op jit(solution)/shard_map/ppermute | solution.py:470
  50.7 0.8 %copy-start.2 = (bf16[2,192,640]{2,1,0:T(8,128)(2,1)}, bf16[2,192,640]{2,1,0:T(8,128)(2,1)S(1)}, u32[]{:S(2)}) copy-start(bf16[2,192,640]{2,1,0:T(8,128)(2,1)S(1)} %collective-permute-done.1.came_ref) | copy-start | bytes 1474564

commit v2 on v1

v2 whole, which is shorter than its diff:
```python
import functools
import math

import jax
import jax.numpy as jnp
from jax import lax
from jax.experimental import pallas as pl
from jax.experimental.pallas import tpu as pltpu
from jax.sharding import PartitionSpec as P

HEAD = 64
CH = 64
TILE = 4
LANES = 128
PACK = 16

GUIDE = 3.5
STEP = -0.25
EPS = 1e-06
LOG2E = 1.4426950408889634
DEAD = -1e30
SEND_MIB, PREPARE_MIB, ATTEND_MIB, FINISH_MIB = 16, 56, 40, 24

F32 = jnp.float32
BF16 = jnp.bfloat16
MIB = 2**20


def round_up(value, step):
    return (value + step - 1) // step * step


def spans(total, step):
    return [(start, min(start + step, total)) for start in range(0, total, step)]


def mm(left, right):
    return jnp.dot(left, right, preferred_element_type=F32)


def mm_nt(left, right):
    return lax.dot_general(left, right, (((1,), (1,)), ((), ())), preferred_element_type=F32)


def mm_tn(left, right):
    return lax.dot_general(left, right, (((0,), (0,)), ((), ())), preferred_element_type=F32)


def iota(shape, dim):
    return lax.broadcasted_iota(jnp.int32, shape, dim)


def two_terms(value):
    high = value.astype(BF16)
    return high, (value - high.astype(F32)).astype(BF16)


def one_hot(mask):
    return jnp.where(mask, 1.0, 0.0).astype(BF16)


def spec(space=pltpu.VMEM):
    return pl.BlockSpec(memory_space=space)


def grant(mib):
    return pltpu.CompilerParams(vmem_limit_bytes=mib * MIB)


def position():
    return lax.axis_index("groups").astype(jnp.int32), lax.axis_index("mp").astype(jnp.int32)


def head_norm(value, gains):
    wide = value.shape[1]
    same = iota((wide, wide), 0) // HEAD == iota((wide, wide), 1) // HEAD
    averaging = jnp.where(same, 1.0 / HEAD, 0.0).astype(BF16)
    square = mm((value * value).astype(BF16), averaging)
    return value * (lax.rsqrt(square + EPS) * gains)


def lanes_of(gains, wide):
    return jnp.concatenate([gains] * (wide // HEAD), axis=1)


def column_of(gains_ref, index):
    row = jnp.broadcast_to(gains_ref[index : index + 1, :], (LANES, HEAD))
    return row.T[:, 0:1]


def head_norm_down(value, gains):
    parts = []
    for at in range(0, value.shape[0], HEAD):
        head = value[at : at + HEAD]
        square = jnp.sum(head * head, axis=0, keepdims=True) * (1.0 / HEAD)
        parts.append(head * lax.rsqrt(square + EPS) * gains)
    return jnp.concatenate(parts, axis=0)


def own_bucket(slots_ref, group, tiles):
    first = group * tiles
    row = first // LANES
    after = jnp.minimum(row + 1, slots_ref.shape[0] - 1)
    window = jnp.concatenate([slots_ref[pl.ds(row, 1), :], slots_ref[pl.ds(after, 1), :]], axis=1)
    turn = 2 * LANES - (first - row * LANES)
    slots = pltpu.roll(window, turn, 1)[:, :tiles]
    target = slots // tiles
    across = target.astype(F32)
    diagonal = iota((tiles, tiles), 0) == iota((tiles, tiles), 1)
    down = jnp.sum(jnp.where(diagonal, across, 0.0), axis=1, keepdims=True)
    earlier = (down == across) & (iota((tiles, tiles), 0) < iota((tiles, tiles), 1))
    rank = jnp.sum(jnp.where(earlier, 1.0, 0.0), axis=0, keepdims=True).astype(jnp.int32)
    return target, rank


def send_kernel(capacity, block, slots_ref, latents_ref, out_ref):
    tiles = latents_ref.shape[0]
    groups_n = out_ref.shape[0]
    group, _ = position()
    target, rank = own_bucket(slots_ref, group, tiles)
    rows = groups_n * block
    bucket = iota((rows, tiles), 0)
    first = target * block + rank
    second = (target ^ 1) * block + capacity + rank
    sender = one_hot((bucket == first) | (bucket == second))
    sent = mm(sender, latents_ref[...].astype(BF16)).astype(BF16).reshape(groups_n, block, -1)
    out_ref[:, 0] = sent
    out_ref[:, 1] = sent


def slots_by_group(slots_ref, tiles):
    per = LANES // math.gcd(tiles, LANES)
    rows_per = per * tiles // LANES
    repeats = slots_ref.shape[0] // rows_per
    wide = jnp.concatenate(
        [slots_ref[pl.ds(row, repeats, stride=rows_per), :] for row in range(rows_per)], axis=1
    )
    parts = [wide[:, turn * tiles : (turn + 1) * tiles] for turn in range(per)]
    return jnp.concatenate(parts, axis=0), lambda row: per * (row % repeats) + row // repeats


def tables(slots, group_of, group, capacity, block, offset):
    groups_n, tiles = slots.shape
    target = slots // tiles
    placed = slots - target * tiles
    mine = target == group
    before = one_hot(iota((tiles, tiles), 0) < iota((tiles, tiles), 1))
    rank = jnp.where(mine, mm(one_hot(mine), before), float(capacity))
    columns = groups_n * block
    spread = one_hot(iota((groups_n, columns), 1) // block == group_of(iota((groups_n, columns), 0)))
    rank_of = mm_tn(rank.astype(BF16), spread)
    place_of = mm_tn(placed.astype(F32).astype(BF16), spread)
    level = (iota((tiles, columns), 1) % block - offset).astype(F32)
    hit = (rank_of == level) & (level >= 0.0) & (level < capacity)
    place = jnp.sum(jnp.where(hit, place_of + 1.0, 0.0), axis=0, keepdims=True) - 1.0
    return one_hot(iota((tiles, columns), 0).astype(F32) == place)


def prepare_kernel(
    capacity,
    block,
    back,
    step,
    slots_ref,
    embed_ref,
    own_mod_ref,
    mate_mod_ref,
    gains_ref,
    states_hbm,
    w_text_hbm,
    w_qkv_hbm,
    gram_out,
    place_out,
    home_out,
    folds_out,
    turned_out,
    text_keys_out,
    text_values_out,
    states,
    w_text,
    w_qkv,
    flat,
    mingled,
    wide,
    split,
    sums,
    left,
    sems,
):
    depth = embed_ref.shape[1]
    width = w_qkv.shape[2]
    text = states.shape[0]
    tiles = home_out.shape[0]
    group, _ = position()
    own_rows = 2 * CH
    half = own_rows + PACK
    chunks = spans(depth, step)
    lane_tiles = width // LANES

    def fetch(source, target, index):
        copy = pltpu.make_async_copy(source, target, sems.at[index])
        copy.start()
        return copy

    states_copy = fetch(states_hbm, states, 0)
    text_copies = [
        fetch(w_text_hbm.at[pl.ds(low, high - low)], w_text.at[pl.ds(low, high - low)], 1 + turn)
        for turn, (low, high) in enumerate(chunks)
    ]
    qkv_copies = [
        fetch(w_qkv_hbm.at[part], w_qkv.at[part], 1 + len(chunks) + part) for part in range(3)
    ]

    embed = embed_ref[...].astype(F32)
    centred = embed - jnp.mean(embed, axis=1, keepdims=True)
    for side, mod_ref in ((0, own_mod_ref), (1, mate_mod_ref)):
        base = side * half
        for branch in range(2):
            scaled = centred * (1.0 + mod_ref[1, branch : branch + 1, :])
            left[pl.ds(base + branch * CH, CH), :] = scaled.astype(BF16)
        high, low = two_terms(mod_ref[0])
        shifts = jnp.concatenate([high.astype(F32), low.astype(F32)], axis=0)
        shifts = jnp.concatenate([shifts, jnp.zeros((PACK - 4, depth), F32)], axis=0)
        left[pl.ds(base + own_rows, PACK), :] = shifts.astype(BF16)
    high, low = two_terms(centred)
    parts = (mm_nt(high, high) + (mm_nt(high, low) + mm_nt(low, high))) * (1.0 / depth)
    top, rest = two_terms(parts)
    bottom = (parts - top.astype(F32) - rest.astype(F32)).astype(BF16)
    gram_out[0:CH, :] = top
    gram_out[CH : 2 * CH, :] = rest
    gram_out[2 * CH : 3 * CH, :] = bottom
    gram_out[3 * CH : 4 * CH, :] = jnp.zeros((CH, CH), BF16)
    slots, group_of = slots_by_group(slots_ref, tiles)
    place_out[0:tiles, :] = tables(slots, group_of, group, capacity, block, 0)
    place_out[tiles : 2 * tiles, :] = tables(slots, group_of, group ^ 1, capacity, block, capacity)
    home_out[...] = tables(slots, group_of, group, capacity, back, 0)

    states_copy.wait()
    flat[...] = states[...].reshape(2 * text, depth)
    for turn, (low, high) in enumerate(chunks):
        text_copies[turn].wait()
        count = high - low
        mingled[0 : 2 * count, :] = w_text[low:high].reshape(2 * count, width)
        for index in range(lane_tiles):
            lanes = slice(index * LANES, (index + 1) * LANES)
            wide[index, 0 : 2 * count, :] = mingled[0 : 2 * count, lanes].astype(F32)
        for part in range(2):
            for index in range(lane_tiles):
                lanes = slice(part * width + index * LANES, part * width + (index + 1) * LANES)
                split[low:high, lanes] = wide[index, pl.ds(part, count, stride=2), :].astype(BF16)
    product = mm(flat[...], split[...])
    for index in range(2 * lane_tiles):
        sums[index] = product[:, index * LANES : (index + 1) * LANES]
    rest_rows = text_values_out.shape[1] - text
    padding = jnp.zeros((rest_rows, LANES), F32)
    gains = column_of(gains_ref, 2)
    for branch in range(2):
        for index in range(lane_tiles):
            lanes = slice(index * LANES, (index + 1) * LANES)
            rows = pl.ds(branch, text, stride=2)
            keys = jnp.concatenate([sums[index, rows, :], padding], axis=0).T
            text_keys_out[branch, lanes, :] = head_norm_down(keys, gains).astype(BF16)
            values = jnp.concatenate([sums[lane_tiles + index, rows, :], padding], axis=0)
            text_values_out[branch, :, lanes] = values.astype(BF16)

    def pieces(product, base, branch):
        bias = (
            product[base + own_rows + branch : base + own_rows + branch + 1]
            + product[base + own_rows + 2 + branch : base + own_rows + 3 + branch]
        )
        fold = product[base + branch * CH : base + (branch + 1) * CH]
        high, low = two_terms(fold)
        bias_high, bias_low = two_terms(bias)
        shift = [bias_high.astype(F32), bias_low.astype(F32)]
        return high.astype(F32), low.astype(F32), shift

    def keep(product, base, kind, lanes):
        for branch in range(2):
            high, low, shift = pieces(product, base, branch)
            zeros = jnp.zeros((PACK - 2, high.shape[1]), F32)
            stacked = jnp.concatenate([high, low] + shift + [zeros], axis=0)
            folds_out[branch, kind, :, lanes] = stacked.astype(BF16)

    def keep_turned(product, base, side, lanes):
        for branch in range(2):
            high, low, shift = pieces(product, base, branch)
            zeros = jnp.zeros((CH - 2, high.shape[1]), F32)
            stacked = jnp.concatenate([high, low, high] + shift + [zeros], axis=0)
            turned_out[branch, side, lanes, :] = stacked.T.astype(BF16)

    shared = width // (2 * LANES) * (2 * LANES)
    main, edge = slice(0, shared), slice(shared, width)
    qkv_copies[0].wait()
    keep(mm(left[0:half, :], w_qkv[0]), 0, 0, slice(0, width))
    qkv_copies[1].wait()
    product = mm(left[...], w_qkv[1, :, main])
    keep_turned(product, 0, 0, main)
    keep_turned(product, half, 1, main)
    qkv_copies[2].wait()
    product = mm(left[...], w_qkv[2, :, main])
    keep(product, 0, 1, main)
    keep(product, half, 2, main)
    if shared < width:
        edges = jnp.concatenate([w_qkv[1, :, edge], w_qkv[2, :, edge]], axis=1)
        product = mm(left[...], edges)
        keys, values = product[:, : width - shared], product[:, width - shared :]
        keep_turned(keys, 0, 0, edge)
        keep_turned(keys, half, 1, edge)
        keep(values, 0, 1, edge)
        keep(values, half, 2, edge)


def attend_kernel(
    live_ref,
    partner_ref,
    arrived_ref,
    place_ref,
    gram_ref,
    gains_ref,
    folds_ref,
    turned_ref,
    text_keys_ref,
    text_values_ref,
    keep_ref,
    send_ref,
    tokens_ref,
    queries,
    keys,
    values,
    *,
    text,
):
    group, member = position()
    groups_n, _, block, narrow = arrived_ref.shape
    tiles = place_ref.shape[0] // 2
    rows = tiles * TILE
    half_rows = rows // 2
    width = keep_ref.shape[2]
    rest = text_values_ref.shape[1]
    mate = partner_ref[group]
    own_len = live_ref[group]
    mate_len = jnp.where(mate != group, live_ref[mate], 0)

    own_parts, mate_parts = [], []
    for turn in range(2):
        source = member ^ turn
        block_rows = arrived_ref[:, pl.ds(source, 1)].reshape(groups_n * block, narrow)
        found = mm(place_ref[...], block_rows)
        for parts, base in ((own_parts, 0), (mate_parts, tiles)):
            pair = found[base : base + tiles]
            parts.append(jnp.concatenate([pair[:, :CH], pair[:, :CH]], axis=1))
            parts.append(jnp.concatenate([pair[:, CH:], pair[:, CH:]], axis=1))
    own_tokens = jnp.concatenate(own_parts, axis=0)
    mate_tokens = jnp.concatenate(mate_parts, axis=0)
    tokens_ref[...] = own_tokens[:half_rows].astype(BF16)
    lane = iota((1, LANES), 1)

    def normed(tokens):
        narrow_tokens = tokens.astype(BF16)
        image = mm(narrow_tokens, gram_ref[0 : 2 * CH]) + mm(narrow_tokens, gram_ref[2 * CH :])
        variance = jnp.sum(image * tokens[:, :CH], axis=1, keepdims=True)
        scaled = tokens * lax.rsqrt(jnp.maximum(variance, 0.0) + EPS)
        high = scaled.astype(BF16).astype(F32)
        ones = jnp.where(lane < CH + 2, 1.0, 0.0)
        return jnp.concatenate([high, jnp.where(lane < CH, scaled - high, ones)], axis=1)

    own_normed = normed(own_tokens)
    mate_normed = normed(mate_tokens)
    own_turned = own_normed.T.astype(BF16)
    mate_turned = mate_normed.T.astype(BF16)
    own_normed = own_normed.astype(BF16)
    mate_normed = mate_normed.astype(BF16)

    row = iota((1, rows), 1)
    turn_of = row // half_rows
    inside = row - turn_of * half_rows
    second = inside // tiles
    slot = (inside - second * tiles) * TILE + 2 * (turn_of ^ member) + second
    own_dead = jnp.where(slot < own_len, 0.0, DEAD)
    mate_dead = jnp.where(slot < mate_len, 0.0, DEAD)
    text_dead = jnp.where(iota((1, rest), 1) < text, 0.0, DEAD)
    dead = jnp.concatenate([own_dead, mate_dead, text_dead], axis=1)
    dead = jnp.where(iota((PACK, 1), 0) == 0, dead, 0.0).astype(BF16)
    dead = jnp.concatenate([dead, jnp.zeros((HEAD - PACK, dead.shape[1]), BF16)], axis=0)

    even = lane < HEAD
    query_gains = gains_ref[0:1, :] * (LOG2E * HEAD**-0.5)
    key_gains = column_of(gains_ref, 1)
    filling = jnp.zeros((CH - PACK, width), BF16)

    def fold_of(branch, kind):
        fold = folds_ref[branch, kind]
        return jnp.concatenate([fold[: 2 * CH], fold[:CH], fold[2 * CH :], filling], axis=0)

    def project(branch):
        queries[branch] = mm(own_normed, fold_of(branch, 0))
        values[branch, 0:rows, :] = mm(own_normed, fold_of(branch, 1)).astype(BF16)
        values[branch, rows : 2 * rows, :] = mm(mate_normed, fold_of(branch, 2)).astype(BF16)
        values[branch, 2 * rows :, :] = text_values_ref[branch]
        for side, turned in ((0, own_turned), (1, mate_turned)):
            found = mm(turned_ref[branch, side], turned)
            keys[branch, :, side * rows : (side + 1) * rows] = head_norm_down(found, key_gains).astype(BF16)
        keys[branch, :, 2 * rows :] = text_keys_ref[branch]

    outs = []

    def settle(branch, at, side, one_values, scores):
        highest = jnp.max(scores, axis=1, keepdims=True)
        outs.append(mm(jnp.exp2(scores - highest).astype(BF16), one_values))
        if side == 1:
            first, second = outs
            outs.clear()
            total = jnp.where(even, second, first)
            total = jnp.concatenate([total[:, HEAD:], total[:, :HEAD]], axis=1)
            merged = (jnp.where(even, first, second) / total).astype(BF16)
            keep_ref[branch, :, at : at + LANES] = merged[:half_rows]
            send_ref[branch, :, at : at + LANES] = merged[half_rows:]

    waiting = None
    for branch in range(2):
        project(branch)
        for low, high in spans(width, 2 * LANES):
            normed_queries = head_norm(queries[branch, :, low:high], lanes_of(query_gains, high - low))
            for at in range(low, high, LANES):
                query = normed_queries[:, at - low : at - low + LANES]
                for side in range(2):
                    inside_head = even if side == 0 else jnp.logical_not(even)
                    marker = lane == (HEAD if side == 0 else 0)
                    one_query = jnp.where(inside_head, query, jnp.where(marker, 1.0, 0.0)).astype(BF16)
                    first = at + side * HEAD
                    one_keys = keys[branch, first : first + HEAD, :]
                    one_keys = jnp.concatenate([one_keys, dead] if side == 0 else [dead, one_keys], axis=0)
                    scores = mm(one_query, one_keys)
                    if waiting is not None:
                        settle(*waiting)
                    one_values = values[branch, :, at : at + LANES]
                    one_values = jnp.where(inside_head, one_values, jnp.ones_like(one_values))
                    waiting = (branch, at, side, one_values, scores)
    settle(*waiting)


def finish_kernel(
    step,
    live_ref,
    kept_ref,
    came_ref,
    w_own_ref,
    w_came_ref,
    tokens_ref,
    embed_ref,
    mod_ref,
    w_final_ref,
    home_ref,
    out_ref,
    state,
):
    group, member = position()
    half_rows = tokens_ref.shape[0]
    tiles = home_ref.shape[0]
    width, depth = w_own_ref.shape
    both = 2 * half_rows
    kept = kept_ref[...].reshape(both, width)
    came = came_ref[...].reshape(both, width)
    chunks = spans(depth, step)

    def rows_of(index, low, high):
        first = jnp.broadcast_to(mod_ref[index, 0:1, low:high], (half_rows, high - low))
        second = jnp.broadcast_to(mod_ref[index, 1:2, low:high], (half_rows, high - low))
        return jnp.concatenate([first, second], axis=0)

    def folded(value):
        return sum(value[:, at : at + LANES] for at in range(0, value.shape[1], LANES))

    pivot = None
    total = jnp.zeros((both, LANES), F32)
    squares = jnp.zeros((both, LANES), F32)
    for low, high in chunks:
        mixed = mm(kept, w_own_ref[:, low:high]).astype(BF16).astype(F32) + mm(
            came, w_came_ref[:, low:high]
        ).astype(BF16).astype(F32)
        hidden = mm(tokens_ref[:, :CH], embed_ref[:, low:high])
        hidden = jnp.concatenate([hidden, hidden], axis=0)
        value = hidden + rows_of(2, low, high) * mixed
        if pivot is None:
            pivot = jnp.sum(folded(value), axis=1, keepdims=True) * (1.0 / (high - low))
        value = value - pivot
        state[:, low:high] = value
        total += folded(value)
        squares += folded(value * value)
    mean = jnp.sum(total, axis=1, keepdims=True) * (1.0 / depth)
    spread = jnp.sum(squares, axis=1, keepdims=True) * (1.0 / depth) - mean * mean
    scale = lax.rsqrt(jnp.maximum(spread, 0.0) + EPS)
    offset = -mean * scale
    velocity = jnp.zeros((both, CH), F32)
    for low, high in chunks:
        normed = state[:, low:high] * scale + offset
        final = normed * (1.0 + rows_of(4, low, high)) + rows_of(3, low, high)
        velocity += mm_nt(final.astype(BF16), w_final_ref[:, low:high])
    guided = velocity[half_rows:] + GUIDE * (velocity[:half_rows] - velocity[half_rows:])
    row = iota((half_rows, 1), 0)
    second = row // tiles
    slot = (row - second * tiles) * TILE + 2 * member + second
    guided = jnp.where(slot < live_ref[group], guided, 0.0)
    columns = jnp.concatenate([guided[:tiles], guided[tiles:]], axis=1).astype(BF16)
    out_ref[...] = mm_tn(home_ref[...], columns).astype(BF16)


def update_kernel(back, slots_ref, latents_ref, returned_ref, out_ref):
    tiles = latents_ref.shape[0]
    group, _ = position()
    target, rank = own_bucket(slots_ref, group, tiles)
    sender = one_hot(iota((returned_ref.shape[0], tiles), 0) == target * back + rank)
    out_ref[...] = latents_ref[...] + STEP * mm_tn(sender, returned_ref[...])


def shards(
    latents,
    tile_slot,
    live,
    partner,
    text_states,
    modulation,
    w_embed,
    w_qkv,
    w_text_kv,
    w_out,
    w_final,
    norm_gains,
):
    groups_n = lax.axis_size("groups")
    tiles, narrow = latents.shape
    rows = tiles * TILE
    depth = w_embed.shape[1]
    width = w_out.shape[0]
    text = text_states.shape[2]
    capacity = max(2, (tiles + groups_n - 1) // groups_n)
    block = round_up(2 * capacity, PACK)
    back = round_up(capacity, PACK)
    slots = tile_slot.reshape(groups_n * tiles // LANES, LANES)
    both = ("groups", "mp")
    cores = [(0, 1), (1, 0)]

    adaptive = jnp.swapaxes(modulation[0], 0, 1)
    pairs = [(source, source ^ 1) for source in range(groups_n)]
    mate_mod = lax.ppermute(adaptive, "groups", pairs)

    outbound = pl.pallas_call(
        functools.partial(send_kernel, capacity, block),
        out_shape=jax.ShapeDtypeStruct((groups_n, 2, block, narrow), BF16),
        in_specs=[spec(), spec()],
        out_specs=spec(),
        compiler_params=grant(SEND_MIB),
    )(slots, latents)
    arrived = lax.all_to_all(
        outbound.reshape(groups_n * 2, block, narrow), both, split_axis=0, concat_axis=0, tiled=True
    ).reshape(groups_n, 2, block, narrow)

    step = 5 * LANES
    chunk_n = len(spans(depth, step))
    left_rows = 2 * (2 * CH + PACK)
    rest = round_up(2 * rows + text, 2 * LANES) - 2 * rows
    gram, place, home, folds, turned, text_keys, text_values = pl.pallas_call(
        functools.partial(prepare_kernel, capacity, block, back, step),
        out_shape=[
            jax.ShapeDtypeStruct((4 * CH, CH), BF16),
            jax.ShapeDtypeStruct((2 * tiles, groups_n * block), BF16),
            jax.ShapeDtypeStruct((tiles, groups_n * back), BF16),
            jax.ShapeDtypeStruct((2, 3, 2 * CH + PACK, width), BF16),
            jax.ShapeDtypeStruct((2, 2, width, 4 * CH), BF16),
            jax.ShapeDtypeStruct((2, width, rest), BF16),
            jax.ShapeDtypeStruct((2, rest, width), BF16),
        ],
        in_specs=[spec()] * 5 + [spec(pltpu.HBM)] * 3,
        out_specs=[spec()] * 7,
        scratch_shapes=[
            pltpu.VMEM((text, 2, depth), BF16),
            pltpu.VMEM((depth, 2, width), BF16),
            pltpu.VMEM((3, depth, width), BF16),
            pltpu.VMEM((2 * text, depth), BF16),
            pltpu.VMEM((2 * step, width), BF16),
            pltpu.VMEM((width // LANES, 2 * step, LANES), F32),
            pltpu.VMEM((depth, 2 * width), BF16),
            pltpu.VMEM((2 * width // LANES, 2 * text, LANES), F32),
            pltpu.VMEM((left_rows, depth), BF16),
            pltpu.SemaphoreType.DMA((1 + chunk_n + 3,)),
        ],
        compiler_params=grant(PREPARE_MIB),
        cost_estimate=pl.CostEstimate(
            flops=2 * (left_rows * 3 + 4 * text) * depth * width,
            bytes_accessed=2 * depth * 5 * width,
            transcendentals=0,
        ),
    )(
        slots,
        w_embed,
        adaptive,
        mate_mod,
        norm_gains,
        jnp.swapaxes(text_states[0], 0, 1),
        w_text_kv,
        jnp.swapaxes(w_qkv, 0, 1),
    )

    _, w_out_sent = lax.optimization_barrier((gram, w_out))
    came_w_out = lax.ppermute(w_out_sent, "mp", cores)
    half = jax.ShapeDtypeStruct((2, rows // 2, width), BF16)
    kept, sent, tokens = pl.pallas_call(
        functools.partial(attend_kernel, text=text),
        out_shape=[half, half, jax.ShapeDtypeStruct((rows // 2, 2 * CH), BF16)],
        in_specs=[spec(pltpu.SMEM)] * 2 + [spec()] * 8,
        out_specs=[spec()] * 3,
        scratch_shapes=[
            pltpu.VMEM((2, rows, width), F32),
            pltpu.VMEM((2, width, 2 * rows + rest), BF16),
            pltpu.VMEM((2, 2 * rows + rest, width), BF16),
        ],
        compiler_params=grant(ATTEND_MIB),
        cost_estimate=pl.CostEstimate(
            flops=2 * 2 * 2 * rows * (2 * rows + rest) * width * 4,
            bytes_accessed=8 * MIB,
            transcendentals=0,
        ),
    )(live, partner, arrived, place, gram, norm_gains, folds, turned, text_keys, text_values)
    came = lax.ppermute(sent, "mp", cores)

    homeward = pl.pallas_call(
        functools.partial(finish_kernel, 4 * LANES),
        out_shape=jax.ShapeDtypeStruct((groups_n * back, narrow), BF16),
        in_specs=[spec(pltpu.SMEM)] + [spec()] * 9,
        out_specs=spec(),
        scratch_shapes=[pltpu.VMEM((rows, depth), F32)],
        compiler_params=grant(FINISH_MIB),
    )(live, kept, came, w_out, came_w_out, tokens, w_embed, adaptive, w_final.T, home)
    returned = lax.all_to_all(
        homeward.reshape(groups_n, back, narrow), "groups", split_axis=0, concat_axis=0, tiled=True
    ).reshape(groups_n * back, narrow)
    return pl.pallas_call(
        functools.partial(update_kernel, back),
        out_shape=jax.ShapeDtypeStruct((tiles, narrow), F32),
        in_specs=[spec()] * 3,
        out_specs=spec(),
        compiler_params=grant(SEND_MIB),
    )(slots, latents, returned)


def solution(mesh):
    placed = (
        P("groups", "mp"),
        P(),
        P(),
        P(),
        P("groups", None, None, None),
        P("groups", None, None, None),
        P(),
        P(None, None, "mp"),
        P(None, None, "mp"),
        P("mp", None),
        P(),
        P(),
    )
    return jax.shard_map(
        shards, mesh=mesh, in_specs=placed, out_specs=P("groups", "mp"), check_vma=False
    )
```

time: 77.7 us -> 75.2 us (0.968)
  blocking collectives: 14.5 us -> 24.6 us
  matrix products: 6.25 us -> 0 us
  Pallas kernels: 40.9 us -> 35 us
  starting transfers between devices: 8.25 us -> 3.29 us
  local copies, waits for them, and re-layouts: 4.17 us -> 7.14 us
  waiting for transfers between devices: 1.84 us -> 4.63 us
  other arithmetic: 1.3 us -> 0 us
    all_to_all x0 -> x1, blocking collectives: none -> 14.3 us  [shards(): lax.all_to_all(outbound.reshape(groups_n * 2, block, narrow), both, split...]
    dot_general x1 -> x0, matrix products: 6.25 us -> none  [shards(): jnp.einsum('btd,dcn->bctn', text_states[0], w_text_kv, preferred_element_...]
    unnamed x10 -> x34, local copies, waits for them, and re-layouts: 2.03 us -> 7.14 us
    all_to_all x1 -> x0, starting transfers between devices: 4.92 us -> none  [shards(): lax.all_to_all(outbound.reshape(groups_n * 2, block, narrow), both, split...]
    all_to_all x1, blocking collectives: 14.5 us -> 10.3 us  [shards(): lax.all_to_all(homeward.reshape(groups_n, back, narrow), 'groups', split_...]
    pallas_call x3, Pallas kernels: 37.4 us -> 33.7 us  [the longest x1 14.5 us: shards(): pl.pallas_call(functools.partial(prepare_kernel, capacity, block, back, s...]
    ppermute x3, waiting for transfers between devices: 1.84 us -> 4.63 us  [the longest x1 2.98 us: shards(): mate_mod = lax.ppermute(adaptive, 'groups', pairs)]
    pallas_call x1, Pallas kernels: 1.74 us -> 0.35 us  [shards(): pl.pallas_call(functools.partial(send_kernel, capacity, block), out_shape...]
  transfers between devices with their start and end apart: 4 -> 3, of which waited for: 1 -> 2; matrix products, arithmetic and copies ran while one was open for 13% -> 0% of each run, Pallas kernels for 38% -> 18%
where the time goes in v2:
time: 75.2 us; the launch traced here: 74.8 us
  Pallas kernels  35 us (47%)
  blocking collectives  24.6 us (33%)
  local copies, waits for them, and re-layouts  7.14 us (9%)
  waiting for transfers between devices  4.63 us (6%)
  starting transfers between devices  3.29 us (4%)
    pallas_call x1, Pallas kernels, shards(): pl.pallas_call(functools.partial(prepare_kernel, capacity, block, back, s...  14.5 us
    all_to_all x1, blocking collectives, shards(): lax.all_to_all(outbound.reshape(groups_n * 2, block, narrow), both, split...  14.3 us
    pallas_call x1, Pallas kernels, shards(): pl.pallas_call(functools.partial(attend_kernel, text=text), out_shape=[ha...  13 us
    all_to_all x1, blocking collectives, shards(): lax.all_to_all(homeward.reshape(groups_n, back, narrow), 'groups', split_...  10.3 us
    unnamed x34, local copies, waits for them, and re-layouts  7.14 us
    pallas_call x1, Pallas kernels, shards(): pl.pallas_call(functools.partial(finish_kernel, 4 * LANES), out_shape=jax...  6.12 us
    ppermute x1, waiting for transfers between devices, shards(): mate_mod = lax.ppermute(adaptive, 'groups', pairs)  2.98 us
    ppermute x1, starting transfers between devices, shards(): mate_mod = lax.ppermute(adaptive, 'groups', pairs)  2.94 us
  transfers between devices with their start and end apart: 3, of which 2 were waited for; matrix products, arithmetic and copies ran while one was open for 0% of the time, Pallas kernels for 18%

profile of v2, /device:TPU:0, one launch (start us, length us, event | category | flops | bytes accessed | tf_op | source)
XLA Modules:
  0.0 74.8 jit_solution(4096101149287351855)
XLA Ops:
  0.0 2.9 %collective-permute-start = (f32[5,2,2432]{2,1,0:T(2,128)}, f32[5,2,2432]{2,1,0:T(2,128)S(1)}, u32[]{:S(2)}, u32[]{:S(2)}) collective-permute-start(f32[5,2,2432]{2,1,0:T(2,128)} %bitcast.14), channel_id=1, source_target_pairs={{0,2},{2,0},{4,6},{6,4},{8,10},{10,8},{12,14},{14,12},{16,18},{18,... | collective-permute-start | bytes 291848 | tf_op jit(solution)/shard_map/ppermute | solution.py:545
  2.9 3.0 %collective-permute-done.mate_mod_ref = f32[5,2,2432]{2,1,0:T(2,128)S(1)} collective-permute-done((f32[5,2,2432]{2,1,0:T(2,128)}, f32[5,2,2432]{2,1,0:T(2,128)S(1)}, u32[]{:S(2)}, u32[]{:S(2)}) %collective-permute-start) | collective-permute-done | bytes 97312 | tf_op jit(solution)/shard_map/ppermute | solution.py:545
  5.9 0.6 copy-done.16
  6.6 0.0 copy-start.8
  6.6 0.0 copy-start.15
  6.6 14.5 %shard_map.119 = (bf16[256,64]{1,0:T(8,128)(2,1)}, bf16[192,256]{1,0:T(8,128)(2,1)}, bf16[96,256]{1,0:T(8,128)(2,1)}, bf16[2,3,144,640]{3,2,1,0:T(8,128)(2,1)}, ...) custom-call(s32[12,128]{1,0:T(8,128)} %bitcast.21, ...), custom_call_target="tpu_custom_call" | custom-call | flops 4607180800 | bytes 15564800 | tf_op jit(solution)/shard_map/pallas_call | solution.py:562
  21.1 0.0 copy-done
  21.1 0.1 collective-permute-start.2
  21.2 0.4 shard_map.118
  21.6 14.3 %all_to_all.10 = bf16[32,16,128]{2,1,0:T(8,128)(2,1)S(1)} all-to-all(bf16[32,16,128]{2,1,0:T(8,128)(2,1)S(1)} %bitcast.13), channel_id=1, replica_groups=mesh['groups'=16,'mp'=2] {'groups','mp'}, dimensions={0} | all-to-all | bytes 262144 | tf_op jit(solution)/shard_map/all_to_all | solution.py:554
  35.9 0.0 copy-done.8
  35.9 1.3 %copy-done.9 = bf16[2,2,640,256]{3,2,1,0:T(8,128)(2,1)S(1)} copy-done((bf16[2,2,640,256]{3,2,1,0:T(8,128)(2,1)S(1)}, bf16[2,2,640,256]{3,2,1,0:T(8,128)(2,1)}, u32[]{:S(2)}) %copy-start.9) | copy-done | bytes 1310744
  37.2 1.2 %copy-done.10 = bf16[2,3,144,640]{3,2,1,0:T(8,128)(2,1)S(1)} copy-done((bf16[2,3,144,640]{3,2,1,0:T(8,128)(2,1)S(1)}, bf16[2,3,144,640]{3,2,1,0:T(8,128)(2,1)}, u32[]{:S(2)}) %copy-start.10) | copy-done | bytes 1105944
  38.5 1.1 %copy-done.11 = bf16[2,640,256]{2,1,0:T(8,128)(2,1)S(1)} copy-done((bf16[2,640,256]{2,1,0:T(8,128)(2,1)S(1)}, bf16[2,640,256]{2,1,0:T(8,128)(2,1)}, u32[]{:S(2)}) %copy-start.11) | copy-done | bytes 655384
  39.6 1.1 %copy-done.12 = bf16[2,256,640]{2,1,0:T(8,128)(2,1)S(1)} copy-done((bf16[2,256,640]{2,1,0:T(8,128)(2,1)S(1)}, bf16[2,256,640]{2,1,0:T(8,128)(2,1)}, u32[]{:S(2)}) %copy-start.12) | copy-done | bytes 655384
  40.6 0.9 %copy-done.13 = bf16[192,256]{1,0:T(8,128)(2,1)S(1)} copy-done((bf16[192,256]{1,0:T(8,128)(2,1)S(1)}, bf16[192,256]{1,0:T(8,128)(2,1)}, u32[]{:S(2)}) %copy-start.13) | copy-done | bytes 98328
  41.5 0.8 %copy-done.14 = bf16[256,64]{1,0:T(8,128)(2,1)S(1)} copy-done((bf16[256,64]{1,0:T(8,128)(2,1)S(1)}, bf16[256,64]{1,0:T(8,128)(2,1)}, u32[]{:S(2)}) %copy-start.14) | copy-done | bytes 32792
  42.4 13.0 %shard_map.120 = (bf16[2,192,640]{2,1,0:T(8,128)(2,1)S(1)}, bf16[2,192,640]{2,1,0:T(8,128)(2,1)S(1)}, bf16[192,128]{1,0:T(8,128)(2,1)S(1)}) custom-call(s32[16]{0:T(128)S(1)} %copy-done.8, s32[16]{0:T(128)S(1)} %copy-done.15, bf16[16,2,16,128]{3,2,1,0:T(8,128)(2,1)S(1)} %bitcast.20, bf16[192,256]{1,0:T(8,128)(2,1)S(1)} %copy-done.13, ...), custom_call_target="tpu_custom_call" | custom-call | flops 8053063680 | bytes 8388608 | tf_op jit(solution)/shard_map/pallas_call | solution.py:607
  55.4 0.3 collective-permute-start.1
  55.7 1.6 %collective-permute-done.1.came_ref = bf16[2,192,640]{2,1,0:T(8,128)(2,1)S(1)} collective-permute-done((bf16[2,192,640]{2,1,0:T(8,128)(2,1)S(1)}, bf16[2,192,640]{2,1,0:T(8,128)(2,1)S(1)}, u32[]{:S(2)}, u32[]{:S(2)}) %collective-permute-start.1) | collective-permute-done | bytes 491552 | tf_op jit(solution)/shard_map/ppermute | solution.py:624
  57.3 0.0 collective-permute-done.2.w_came_ref
  57.4 6.1 %shard_map.121 = bf16[256,128]{1,0:T(8,128)(2,1)S(1)} custom-call(s32[16]{0:T(128)S(1)} %copy-done.8, bf16[2,192,640]{2,1,0:T(8,128)(2,1)S(1)} %get-tuple-element.22.kept_ref, bf16[2,192,640]{2,1,0:T(8,128)(2,1)S(1)} %collective-permute-done.1.came_ref, bf16[640,2432]{1,0:T(8,128)(2,1)S(1)} %copy-done, ...), custom_call_target="tpu_custom_call" | custom-call | tf_op jit(solution)/shard_map/pallas_call | solution.py:626
  63.5 10.3 %all_to_all.11 = bf16[16,16,128]{2,1,0:T(8,128)(2,1)S(1)} all-to-all(bf16[16,16,128]{2,1,0:T(8,128)(2,1)S(1)} %bitcast.18), channel_id=1, replica_groups=mesh['groups'=16,'mp'=2] {'groups'}, dimensions={0} | all-to-all | bytes 131072 | tf_op jit(solution)/shard_map/all_to_all | solution.py:634
  73.8 1.0 %shard_map.122 = f32[96,128]{1,0:T(8,128)} custom-call(s32[12,128]{1,0:T(8,128)S(1)} %bitcast.23, f32[96,128]{1,0:T(8,128)S(1)} %copy-done.4, bf16[256,128]{1,0:T(8,128)(2,1)S(1)} %bitcast.19), custom_call_target="tpu_custom_call" | custom-call | tf_op jit(solution)/shard_map/pallas_call | solution.py:637
  (23 shorter events, 0.0 us)
Async XLA Ops:
  0.0 5.9 %collective-permute-start = (f32[5,2,2432]{2,1,0:T(2,128)}, f32[5,2,2432]{2,1,0:T(2,128)S(1)}, u32[]{:S(2)}, u32[]{:S(2)}) collective-permute-start(f32[5,2,2432]{2,1,0:T(2,128)} %bitcast.14), channel_id=1, source_target_pairs={{0,2},{2,0},{4,6},{6,4},{8,10},{10,8},{12,14},{14,12},{16,18},{18,... | collective-permute-start | bytes 291848 | tf_op jit(solution)/shard_map/ppermute | solution.py:545
  5.9 0.6 copy-start.16
  6.6 14.6 %copy-start = (bf16[640,2432]{1,0:T(8,128)(2,1)S(1)}, bf16[640,2432]{1,0:T(8,128)(2,1)}, u32[]{:S(2)}) copy-start(bf16[640,2432]{1,0:T(8,128)(2,1)} %w_own_ref.1) | copy-start | bytes 9338884
  6.6 14.6 %copy-start.4 = (f32[96,128]{1,0:T(8,128)S(1)}, f32[96,128]{1,0:T(8,128)}, u32[]{:S(2)}) copy-start(f32[96,128]{1,0:T(8,128)} %latents_ref.3) | copy-start | bytes 147460
  6.6 14.7 %copy-start.5 = (s32[1536]{0:T(1024)S(1)}, s32[1536]{0:T(1024)}, u32[]{:S(2)}) copy-start(s32[1536]{0:T(1024)} %param.13) | copy-start | bytes 18436
  6.6 29.3 %copy-start.7 = (f32[3,64]{1,0:T(4,128)S(1)}, f32[3,64]{1,0:T(4,128)}, u32[]{:S(2)}) copy-start(f32[3,64]{1,0:T(4,128)} %gains_ref.3) | copy-start | bytes 2308
  6.6 29.3 %copy-start.8 = (s32[16]{0:T(128)S(1)}, s32[16]{0:T(128)}, u32[]{:S(2)}) copy-start(s32[16]{0:T(128)} %live_ref.3) | copy-start | bytes 196
  6.6 29.3 %copy-start.15 = (s32[16]{0:T(128)S(1)}, s32[16]{0:T(128)}, u32[]{:S(2)}) copy-start(s32[16]{0:T(128)} %partner_ref.1) | copy-start | bytes 196
  21.1 36.2 %collective-permute-start.2 = (bf16[640,2432]{1,0:T(8,128)(2,1)S(1)}, bf16[640,2432]{1,0:T(8,128)(2,1)S(1)}, u32[]{:S(2)}, u32[]{:S(2)}) collective-permute-start(bf16[640,2432]{1,0:T(8,128)(2,1)S(1)} %copy-done), channel_id=1, source_target_pairs={{0,1},{1,0},{2,3},{3,2},{4,5},{5,4},{6,7},{7,6},{8,9},{9,8},{10,11... | collective-permute-start | bytes 9338888 | tf_op jit(solution)/shard_map/ppermute | solution.py:605
  35.9 1.3 %copy-start.9 = (bf16[2,2,640,256]{3,2,1,0:T(8,128)(2,1)S(1)}, bf16[2,2,640,256]{3,2,1,0:T(8,128)(2,1)}, u32[]{:S(2)}) copy-start(bf16[2,2,640,256]{3,2,1,0:T(8,128)(2,1)} %get-tuple-element.19.turned_ref) | copy-start | bytes 3932164
  37.2 1.2 %copy-start.10 = (bf16[2,3,144,640]{3,2,1,0:T(8,128)(2,1)S(1)}, bf16[2,3,144,640]{3,2,1,0:T(8,128)(2,1)}, u32[]{:S(2)}) copy-start(bf16[2,3,144,640]{3,2,1,0:T(8,128)(2,1)} %get-tuple-element.18.folds_ref) | copy-start | bytes 3317764
  38.5 1.1 %copy-start.11 = (bf16[2,640,256]{2,1,0:T(8,128)(2,1)S(1)}, bf16[2,640,256]{2,1,0:T(8,128)(2,1)}, u32[]{:S(2)}) copy-start(bf16[2,640,256]{2,1,0:T(8,128)(2,1)} %get-tuple-element.20.text_keys_ref) | copy-start | bytes 1966084
  39.6 1.1 %copy-start.12 = (bf16[2,256,640]{2,1,0:T(8,128)(2,1)S(1)}, bf16[2,256,640]{2,1,0:T(8,128)(2,1)}, u32[]{:S(2)}) copy-start(bf16[2,256,640]{2,1,0:T(8,128)(2,1)} %get-tuple-element.21.text_values_ref) | copy-start | bytes 1966084
  40.6 0.9 %copy-start.13 = (bf16[192,256]{1,0:T(8,128)(2,1)S(1)}, bf16[192,256]{1,0:T(8,128)(2,1)}, u32[]{:S(2)}) copy-start(bf16[192,256]{1,0:T(8,128)(2,1)} %get-tuple-element.16.place_ref) | copy-start | bytes 294916
  41.5 0.8 %copy-start.14 = (bf16[256,64]{1,0:T(8,128)(2,1)S(1)}, bf16[256,64]{1,0:T(8,128)(2,1)}, u32[]{:S(2)}) copy-start(bf16[256,64]{1,0:T(8,128)(2,1)} %get-tuple-element.17.gram_ref) | copy-start | bytes 98308
  42.4 15.0 %copy-start.1 = (bf16[64,2432]{1,0:T(8,128)(2,1)S(1)}, bf16[64,2432]{1,0:T(8,128)(2,1)}, u32[]{:S(2)}) copy-start(bf16[64,2432]{1,0:T(8,128)(2,1)} %embed_ref.3) | copy-start | bytes 933892
  42.4 15.0 %copy-start.2 = (f32[1,2,5,2432]{3,1,2,0:T(2,128)S(1)}, f32[1,2,5,2432]{3,1,2,0:T(2,128)}, u32[]{:S(2)}) copy-start(f32[1,2,5,2432]{3,1,2,0:T(2,128)} %param.17) | copy-start | bytes 291844
  42.4 15.0 %copy-start.3 = (bf16[2432,64]{0,1:T(8,128)(2,1)S(1)}, bf16[2432,64]{0,1:T(8,128)(2,1)}, u32[]{:S(2)}) copy-start(bf16[2432,64]{0,1:T(8,128)(2,1)} %param.22) | copy-start | bytes 933892
  42.4 15.0 %copy-start.6 = (bf16[96,256]{1,0:T(8,128)(2,1)S(1)}, bf16[96,256]{1,0:T(8,128)(2,1)}, u32[]{:S(2)}) copy-start(bf16[96,256]{1,0:T(8,128)(2,1)} %get-tuple-element.26.home_ref) | copy-start | bytes 147460
  55.4 1.9 %collective-permute-start.1 = (bf16[2,192,640]{2,1,0:T(8,128)(2,1)S(1)}, bf16[2,192,640]{2,1,0:T(8,128)(2,1)S(1)}, u32[]{:S(2)}, u32[]{:S(2)}) collective-permute-start(bf16[2,192,640]{2,1,0:T(8,128)(2,1)S(1)} %get-tuple-element.23), channel_id=1, source_target_pairs={{0,1},{1,0},{2,3},{3,2},{4,5},{5,4},{6,7},{7,6},{8,9},{9,8},{10,11... | collective-permute-start | bytes 1474568 | tf_op jit(solution)/shard_map/ppermute | solution.py:624

commit v3 on v2

--- a/solution.py
+++ b/solution.py
@@ -19,7 +19,8 @@
 EPS = 1e-06
 LOG2E = 1.4426950408889634
 DEAD = -1e30
-SEND_MIB, PREPARE_MIB, ATTEND_MIB, FINISH_MIB = 16, 56, 40, 24
+SEND_MIB, PREPARE_MIB, ATTEND_MIB, FINISH_MIB, UPDATE_MIB = 60, 56, 52, 24, 16
+AHEAD = 99
 
 F32 = jnp.float32
 BF16 = jnp.bfloat16
@@ -172,20 +173,23 @@
     gram_out,
     place_out,
     home_out,
+    folds_hbm,
+    turned_hbm,
+    text_keys_hbm,
+    text_values_hbm,
     folds_out,
     turned_out,
     text_keys_out,
     text_values_out,
     states,
-    w_text,
+    mingled,
     w_qkv,
-    flat,
-    mingled,
     wide,
     split,
     sums,
     left,
     sems,
+    out_sems,
 ):
     depth = embed_ref.shape[1]
     width = w_qkv.shape[2]
@@ -197,19 +201,34 @@
     chunks = spans(depth, step)
     lane_tiles = width // LANES
 
-    def fetch(source, target, index):
-        copy = pltpu.make_async_copy(source, target, sems.at[index])
-        copy.start()
-        return copy
-
-    states_copy = fetch(states_hbm, states, 0)
-    text_copies = [
-        fetch(w_text_hbm.at[pl.ds(low, high - low)], w_text.at[pl.ds(low, high - low)], 1 + turn)
-        for turn, (low, high) in enumerate(chunks)
+    sources = []
+    for part in range(3):
+        for low, high in spans(depth, 2 * step):
+            rows = pl.ds(low, high - low)
+            sources.append((w_qkv_hbm.at[part, rows], w_qkv.at[part, rows]))
+    qkv_n = len(sources) // 3
+    sources.append((states_hbm, states))
+    w_mingled = w_text_hbm.reshape(2 * depth, width)
+    for low, high in chunks:
+        rows = pl.ds(2 * low, 2 * (high - low))
+        sources.append((w_mingled.at[rows], mingled.at[rows]))
+    copies = [
+        pltpu.make_async_copy(source, target, sems.at[index])
+        for index, (source, target) in enumerate(sources)
     ]
-    qkv_copies = [
-        fetch(w_qkv_hbm.at[part], w_qkv.at[part], 1 + len(chunks) + part) for part in range(3)
-    ]
+    started = [0]
+
+    def start(count):
+        while started[0] < min(count, len(copies)):
+            copies[started[0]].start()
+            started[0] += 1
+
+    def wait(first, last):
+        for index in range(first, last):
+            start(index + AHEAD)
+            copies[index].wait()
+
+    start(AHEAD)
 
     embed = embed_ref[...].astype(F32)
     centred = embed - jnp.mean(embed, axis=1, keepdims=True)
@@ -222,38 +241,88 @@
         shifts = jnp.concatenate([high.astype(F32), low.astype(F32)], axis=0)
         shifts = jnp.concatenate([shifts, jnp.zeros((PACK - 4, depth), F32)], axis=0)
         left[pl.ds(base + own_rows, PACK), :] = shifts.astype(BF16)
-    high, low = two_terms(centred)
-    parts = (mm_nt(high, high) + (mm_nt(high, low) + mm_nt(low, high))) * (1.0 / depth)
-    top, rest = two_terms(parts)
-    bottom = (parts - top.astype(F32) - rest.astype(F32)).astype(BF16)
-    gram_out[0:CH, :] = top
-    gram_out[CH : 2 * CH, :] = rest
-    gram_out[2 * CH : 3 * CH, :] = bottom
-    gram_out[3 * CH : 4 * CH, :] = jnp.zeros((CH, CH), BF16)
-    slots, group_of = slots_by_group(slots_ref, tiles)
-    place_out[0:tiles, :] = tables(slots, group_of, group, capacity, block, 0)
-    place_out[tiles : 2 * tiles, :] = tables(slots, group_of, group ^ 1, capacity, block, capacity)
-    home_out[...] = tables(slots, group_of, group, capacity, back, 0)
-
-    states_copy.wait()
-    flat[...] = states[...].reshape(2 * text, depth)
-    for turn, (low, high) in enumerate(chunks):
-        text_copies[turn].wait()
-        count = high - low
-        mingled[0 : 2 * count, :] = w_text[low:high].reshape(2 * count, width)
-        for index in range(lane_tiles):
-            lanes = slice(index * LANES, (index + 1) * LANES)
-            wide[index, 0 : 2 * count, :] = mingled[0 : 2 * count, lanes].astype(F32)
-        for part in range(2):
+    def pieces(product, base, branch):
+        first = base + own_rows + branch
+        bias = two_terms(product[first : first + 1] + product[first + 2 : first + 3])
+        fold = two_terms(product[base + branch * CH : base + (branch + 1) * CH])
+        return [part.astype(F32) for part in fold + bias]
+
+    def keep(product, base, side, lanes):
+        for branch in range(2):
+            zeros = jnp.zeros((PACK - 2, product.shape[1]), F32)
+            stacked = jnp.concatenate(pieces(product, base, branch) + [zeros], axis=0)
+            folds_out[branch, side, :, lanes] = stacked.astype(BF16)
+
+    def keep_turned(product, base, kind, lanes):
+        for branch in range(2):
+            high, low, bias_high, bias_low = pieces(product, base, branch)
+            zeros = jnp.zeros((CH - 2, product.shape[1]), F32)
+            stacked = jnp.concatenate([high, low, high, bias_high, bias_low, zeros], axis=0)
+            turned_out[branch, kind, lanes, :] = stacked.T.astype(BF16)
+
+    shared = width // (2 * LANES) * (2 * LANES)
+    main, edge = slice(0, shared), slice(shared, width)
+    def gram_and_tables():
+        high, low = two_terms(centred)
+        parts = (mm_nt(high, high) + (mm_nt(high, low) + mm_nt(low, high))) * (1.0 / depth)
+        top, rest = two_terms(parts)
+        bottom = (parts - top.astype(F32) - rest.astype(F32)).astype(BF16)
+        gram_out[0:CH, :] = top
+        gram_out[CH : 2 * CH, :] = rest
+        gram_out[2 * CH : 3 * CH, :] = bottom
+        gram_out[3 * CH : 4 * CH, :] = jnp.zeros((CH, CH), BF16)
+        slots, group_of = slots_by_group(slots_ref, tiles)
+        place_out[0:tiles, :] = tables(slots, group_of, group, capacity, block, 0)
+        place_out[tiles : 2 * tiles, :] = tables(slots, group_of, group ^ 1, capacity, block, capacity)
+        home_out[...] = tables(slots, group_of, group, capacity, back, 0)
+
+    out_copies = []
+
+    def put(source, target):
+        out_copies.append(pltpu.make_async_copy(source, target, out_sems.at[len(out_copies)]))
+        out_copies[-1].start()
+
+    def divide(first, last):
+        for low, high in chunks[first:last]:
+            count = high - low
             for index in range(lane_tiles):
-                lanes = slice(part * width + index * LANES, part * width + (index + 1) * LANES)
-                split[low:high, lanes] = wide[index, pl.ds(part, count, stride=2), :].astype(BF16)
-    product = mm(flat[...], split[...])
+                lanes = slice(index * LANES, (index + 1) * LANES)
+                wide[index, 0 : 2 * count, :] = mingled[2 * low : 2 * high, lanes].astype(F32)
+            for part in range(2):
+                for index in range(lane_tiles):
+                    lanes = slice(part * width + index * LANES, part * width + (index + 1) * LANES)
+                    split[low:high, lanes] = wide[index, pl.ds(part, count, stride=2), :].astype(BF16)
+
+    wait(0, qkv_n)
+    query_product = mm(left[0:half, :], w_qkv[0])
+    gram_and_tables()
+    wait(qkv_n, 2 * qkv_n)
+    key_product = mm(left[...], w_qkv[1, :, main])
+    keep_turned(query_product, 0, 0, slice(0, width))
+    wait(2 * qkv_n, 3 * qkv_n)
+    value_product = mm(left[...], w_qkv[2, :, main])
+    if shared < width:
+        edge_product = mm(left[...], jnp.concatenate([w_qkv[1, :, edge], w_qkv[2, :, edge]], axis=1))
+    keep_turned(key_product, 0, 1, main)
+    keep_turned(key_product, half, 2, main)
+    wait(3 * qkv_n, len(copies))
+    if shared < width:
+        keys, values = edge_product[:, : width - shared], edge_product[:, width - shared :]
+        keep_turned(keys, 0, 1, edge)
+        keep_turned(keys, half, 2, edge)
+        keep(values, 0, 0, edge)
+        keep(values, half, 1, edge)
+    keep(value_product, 0, 0, main)
+    keep(value_product, half, 1, main)
+    divide(0, len(chunks))
+    put(folds_out, folds_hbm)
+    put(turned_out, turned_hbm)
+
+    product = mm(states[...].reshape(2 * text, depth), split[...])
     for index in range(2 * lane_tiles):
         sums[index] = product[:, index * LANES : (index + 1) * LANES]
-    rest_rows = text_values_out.shape[1] - text
-    padding = jnp.zeros((rest_rows, LANES), F32)
     gains = column_of(gains_ref, 2)
+    padding = jnp.zeros((text_values_out.shape[1] - text, LANES), F32)
     for branch in range(2):
         for index in range(lane_tiles):
             lanes = slice(index * LANES, (index + 1) * LANES)
@@ -262,52 +331,10 @@
             text_keys_out[branch, lanes, :] = head_norm_down(keys, gains).astype(BF16)
             values = jnp.concatenate([sums[lane_tiles + index, rows, :], padding], axis=0)
             text_values_out[branch, :, lanes] = values.astype(BF16)
-
-    def pieces(product, base, branch):
-        bias = (
-            product[base + own_rows + branch : base + own_rows + branch + 1]
-            + product[base + own_rows + 2 + branch : base + own_rows + 3 + branch]
-        )
-        fold = product[base + branch * CH : base + (branch + 1) * CH]
-        high, low = two_terms(fold)
-        bias_high, bias_low = two_terms(bias)
-        shift = [bias_high.astype(F32), bias_low.astype(F32)]
-        return high.astype(F32), low.astype(F32), shift
-
-    def keep(product, base, kind, lanes):
-        for branch in range(2):
-            high, low, shift = pieces(product, base, branch)
-            zeros = jnp.zeros((PACK - 2, high.shape[1]), F32)
-            stacked = jnp.concatenate([high, low] + shift + [zeros], axis=0)
-            folds_out[branch, kind, :, lanes] = stacked.astype(BF16)
-
-    def keep_turned(product, base, side, lanes):
-        for branch in range(2):
-            high, low, shift = pieces(product, base, branch)
-            zeros = jnp.zeros((CH - 2, high.shape[1]), F32)
-            stacked = jnp.concatenate([high, low, high] + shift + [zeros], axis=0)
-            turned_out[branch, side, lanes, :] = stacked.T.astype(BF16)
-
-    shared = width // (2 * LANES) * (2 * LANES)
-    main, edge = slice(0, shared), slice(shared, width)
-    qkv_copies[0].wait()
-    keep(mm(left[0:half, :], w_qkv[0]), 0, 0, slice(0, width))
-    qkv_copies[1].wait()
-    product = mm(left[...], w_qkv[1, :, main])
-    keep_turned(product, 0, 0, main)
-    keep_turned(product, half, 1, main)
-    qkv_copies[2].wait()
-    product = mm(left[...], w_qkv[2, :, main])
-    keep(product, 0, 1, main)
-    keep(product, half, 2, main)
-    if shared < width:
-        edges = jnp.concatenate([w_qkv[1, :, edge], w_qkv[2, :, edge]], axis=1)
-        product = mm(left[...], edges)
-        keys, values = product[:, : width - shared], product[:, width - shared :]
-        keep_turned(keys, 0, 0, edge)
-        keep_turned(keys, half, 1, edge)
-        keep(values, 0, 1, edge)
-        keep(values, half, 2, edge)
+        put(text_keys_out.at[branch], text_keys_hbm.at[branch])
+        put(text_values_out.at[branch], text_values_hbm.at[branch])
+    for copy in out_copies:
+        copy.wait()
 
 
 def attend_kernel(
@@ -317,19 +344,33 @@
     place_ref,
     gram_ref,
     gains_ref,
+    folds_hbm,
+    turned_hbm,
+    text_keys_hbm,
+    text_values_hbm,
+    keep_ref,
+    send_ref,
+    tokens_ref,
     folds_ref,
     turned_ref,
     text_keys_ref,
     text_values_ref,
-    keep_ref,
-    send_ref,
-    tokens_ref,
     queries,
     keys,
     values,
+    sems,
     *,
     text,
 ):
+    copies = []
+    for source, target in (
+        (turned_hbm, turned_ref),
+        (folds_hbm, folds_ref),
+        (text_keys_hbm, text_keys_ref),
+        (text_values_hbm, text_values_ref),
+    ):
+        copies.append(pltpu.make_async_copy(source, target, sems.at[len(copies)]))
+        copies[-1].start()
     group, member = position()
     groups_n, _, block, narrow = arrived_ref.shape
     tiles = place_ref.shape[0] // 2
@@ -384,27 +425,43 @@
     dead = jnp.concatenate([dead, jnp.zeros((HEAD - PACK, dead.shape[1]), BF16)], axis=0)
 
     even = lane < HEAD
-    query_gains = gains_ref[0:1, :] * (LOG2E * HEAD**-0.5)
+    query_gains = column_of(gains_ref, 0) * (LOG2E * HEAD**-0.5)
     key_gains = column_of(gains_ref, 1)
     filling = jnp.zeros((CH - PACK, width), BF16)
-
-    def fold_of(branch, kind):
-        fold = folds_ref[branch, kind]
+    lane_tiles = width // LANES
+    for copy in copies:
+        copy.wait()
+
+    def fold_of(branch, side):
+        fold = folds_ref[branch, side]
         return jnp.concatenate([fold[: 2 * CH], fold[:CH], fold[2 * CH :], filling], axis=0)
 
     def project(branch):
-        queries[branch] = mm(own_normed, fold_of(branch, 0))
-        values[branch, 0:rows, :] = mm(own_normed, fold_of(branch, 1)).astype(BF16)
-        values[branch, rows : 2 * rows, :] = mm(mate_normed, fold_of(branch, 2)).astype(BF16)
+        query = head_norm_down(mm(turned_ref[branch, 0], own_turned), query_gains)
+        queries[branch] = query.T
+        for side, turned in ((0, own_turned), (1, mate_turned)):
+            key = head_norm_down(mm(turned_ref[branch, 1 + side], turned), key_gains)
+            keys[branch, :, side * rows : (side + 1) * rows] = key.astype(BF16)
+        keys[branch, :, 2 * rows :] = text_keys_ref[branch]
+        values[branch, 0:rows, :] = mm(own_normed, fold_of(branch, 0)).astype(BF16)
+        values[branch, rows : 2 * rows, :] = mm(mate_normed, fold_of(branch, 1)).astype(BF16)
         values[branch, 2 * rows :, :] = text_values_ref[branch]
-        for side, turned in ((0, own_turned), (1, mate_turned)):
-            found = mm(turned_ref[branch, side], turned)
-            keys[branch, :, side * rows : (side + 1) * rows] = head_norm_down(found, key_gains).astype(BF16)
-        keys[branch, :, 2 * rows :] = text_keys_ref[branch]
+
+    def score(branch, at, side):
+        inside_head = even if side == 0 else jnp.logical_not(even)
+        marker = lane == (HEAD if side == 0 else 0)
+        query = queries[branch, :, at : at + LANES]
+        query = jnp.where(inside_head, query, jnp.where(marker, 1.0, 0.0)).astype(BF16)
+        first = at + side * HEAD
+        one_keys = keys[branch, first : first + HEAD, :]
+        return mm(query, jnp.concatenate([one_keys, dead] if side == 0 else [dead, one_keys], axis=0))
 
     outs = []
 
-    def settle(branch, at, side, one_values, scores):
+    def settle(branch, at, side, scores):
+        inside_head = even if side == 0 else jnp.logical_not(even)
+        one_values = values[branch, :, at : at + LANES]
+        one_values = jnp.where(inside_head, one_values, jnp.ones_like(one_values))
         highest = jnp.max(scores, axis=1, keepdims=True)
         outs.append(mm(jnp.exp2(scores - highest).astype(BF16), one_values))
         if side == 1:
@@ -417,25 +474,17 @@
             send_ref[branch, :, at : at + LANES] = merged[half_rows:]
 
     waiting = None
+    project(0)
     for branch in range(2):
-        project(branch)
-        for low, high in spans(width, 2 * LANES):
-            normed_queries = head_norm(queries[branch, :, low:high], lanes_of(query_gains, high - low))
-            for at in range(low, high, LANES):
-                query = normed_queries[:, at - low : at - low + LANES]
-                for side in range(2):
-                    inside_head = even if side == 0 else jnp.logical_not(even)
-                    marker = lane == (HEAD if side == 0 else 0)
-                    one_query = jnp.where(inside_head, query, jnp.where(marker, 1.0, 0.0)).astype(BF16)
-                    first = at + side * HEAD
-                    one_keys = keys[branch, first : first + HEAD, :]
-                    one_keys = jnp.concatenate([one_keys, dead] if side == 0 else [dead, one_keys], axis=0)
-                    scores = mm(one_query, one_keys)
-                    if waiting is not None:
-                        settle(*waiting)
-                    one_values = values[branch, :, at : at + LANES]
-                    one_values = jnp.where(inside_head, one_values, jnp.ones_like(one_values))
-                    waiting = (branch, at, side, one_values, scores)
+        for pair in range(lane_tiles):
+            for side in range(2):
+                at = pair * LANES
+                scores = score(branch, at, side)
+                if waiting is not None:
+                    settle(*waiting)
+                waiting = (branch, at, side, scores)
+            if branch == 0 and pair == lane_tiles // 2:
+                project(1)
     settle(*waiting)
 
 
@@ -459,9 +508,9 @@
     tiles = home_ref.shape[0]
     width, depth = w_own_ref.shape
     both = 2 * half_rows
+    chunks = spans(depth, step)
     kept = kept_ref[...].reshape(both, width)
     came = came_ref[...].reshape(both, width)
-    chunks = spans(depth, step)
 
     def rows_of(index, low, high):
         first = jnp.broadcast_to(mod_ref[index, 0:1, low:high], (half_rows, high - low))
@@ -474,7 +523,7 @@
     pivot = None
     total = jnp.zeros((both, LANES), F32)
     squares = jnp.zeros((both, LANES), F32)
-    for low, high in chunks:
+    for turn, (low, high) in enumerate(chunks):
         mixed = mm(kept, w_own_ref[:, low:high]).astype(BF16).astype(F32) + mm(
             came, w_came_ref[:, low:high]
         ).astype(BF16).astype(F32)
@@ -555,34 +604,38 @@
         outbound.reshape(groups_n * 2, block, narrow), both, split_axis=0, concat_axis=0, tiled=True
     ).reshape(groups_n, 2, block, narrow)
 
-    step = 5 * LANES
+    step = 4 * LANES
     chunk_n = len(spans(depth, step))
+    qkv_n = len(spans(depth, 2 * step))
     left_rows = 2 * (2 * CH + PACK)
     rest = round_up(2 * rows + text, 2 * LANES) - 2 * rows
+    kept_shapes = [
+        jax.ShapeDtypeStruct((2, 2, 2 * CH + PACK, width), BF16),
+        jax.ShapeDtypeStruct((2, 3, width, 4 * CH), BF16),
+        jax.ShapeDtypeStruct((2, width, rest), BF16),
+        jax.ShapeDtypeStruct((2, rest, width), BF16),
+    ]
     gram, place, home, folds, turned, text_keys, text_values = pl.pallas_call(
         functools.partial(prepare_kernel, capacity, block, back, step),
         out_shape=[
             jax.ShapeDtypeStruct((4 * CH, CH), BF16),
             jax.ShapeDtypeStruct((2 * tiles, groups_n * block), BF16),
             jax.ShapeDtypeStruct((tiles, groups_n * back), BF16),
-            jax.ShapeDtypeStruct((2, 3, 2 * CH + PACK, width), BF16),
-            jax.ShapeDtypeStruct((2, 2, width, 4 * CH), BF16),
-            jax.ShapeDtypeStruct((2, width, rest), BF16),
-            jax.ShapeDtypeStruct((2, rest, width), BF16),
+            *kept_shapes,
         ],
         in_specs=[spec()] * 5 + [spec(pltpu.HBM)] * 3,
-        out_specs=[spec()] * 7,
+        out_specs=[spec()] * 3 + [spec(pltpu.HBM)] * 4,
         scratch_shapes=[
+            *(pltpu.VMEM(kept.shape, BF16) for kept in kept_shapes),
             pltpu.VMEM((text, 2, depth), BF16),
-            pltpu.VMEM((depth, 2, width), BF16),
+            pltpu.VMEM((2 * depth, width), BF16),
             pltpu.VMEM((3, depth, width), BF16),
-            pltpu.VMEM((2 * text, depth), BF16),
-            pltpu.VMEM((2 * step, width), BF16),
             pltpu.VMEM((width // LANES, 2 * step, LANES), F32),
             pltpu.VMEM((depth, 2 * width), BF16),
             pltpu.VMEM((2 * width // LANES, 2 * text, LANES), F32),
             pltpu.VMEM((left_rows, depth), BF16),
-            pltpu.SemaphoreType.DMA((1 + chunk_n + 3,)),
+            pltpu.SemaphoreType.DMA((1 + chunk_n + 3 * qkv_n,)),
+            pltpu.SemaphoreType.DMA((6,)),
         ],
         compiler_params=grant(PREPARE_MIB),
         cost_estimate=pl.CostEstimate(
@@ -601,22 +654,27 @@
         jnp.swapaxes(w_qkv, 0, 1),
     )
 
-    _, w_out_sent = lax.optimization_barrier((gram, w_out))
+    arrived, gram, w_out_sent = lax.optimization_barrier((arrived, gram, w_out))
     came_w_out = lax.ppermute(w_out_sent, "mp", cores)
     half = jax.ShapeDtypeStruct((2, rows // 2, width), BF16)
     kept, sent, tokens = pl.pallas_call(
         functools.partial(attend_kernel, text=text),
         out_shape=[half, half, jax.ShapeDtypeStruct((rows // 2, 2 * CH), BF16)],
-        in_specs=[spec(pltpu.SMEM)] * 2 + [spec()] * 8,
+        in_specs=[spec(pltpu.SMEM)] * 2 + [spec()] * 4 + [spec(pltpu.HBM)] * 4,
         out_specs=[spec()] * 3,
         scratch_shapes=[
+            pltpu.VMEM(folds.shape, BF16),
+            pltpu.VMEM(turned.shape, BF16),
+            pltpu.VMEM(text_keys.shape, BF16),
+            pltpu.VMEM(text_values.shape, BF16),
             pltpu.VMEM((2, rows, width), F32),
             pltpu.VMEM((2, width, 2 * rows + rest), BF16),
             pltpu.VMEM((2, 2 * rows + rest, width), BF16),
+            pltpu.SemaphoreType.DMA((4,)),
         ],
         compiler_params=grant(ATTEND_MIB),
         cost_estimate=pl.CostEstimate(
-            flops=2 * 2 * 2 * rows * (2 * rows + rest) * width * 4,
+            flops=40 * 2 * 2 * rows * (2 * rows + rest) * width,
             bytes_accessed=8 * MIB,
             transcendentals=0,
         ),
@@ -624,11 +682,13 @@
     came = lax.ppermute(sent, "mp", cores)
 
     homeward = pl.pallas_call(
-        functools.partial(finish_kernel, 4 * LANES),
+        functools.partial(finish_kernel, step),
         out_shape=jax.ShapeDtypeStruct((groups_n * back, narrow), BF16),
         in_specs=[spec(pltpu.SMEM)] + [spec()] * 9,
         out_specs=spec(),
-        scratch_shapes=[pltpu.VMEM((rows, depth), F32)],
+        scratch_shapes=[
+            pltpu.VMEM((rows, depth), F32),
+        ],
         compiler_params=grant(FINISH_MIB),
     )(live, kept, came, w_out, came_w_out, tokens, w_embed, adaptive, w_final.T, home)
     returned = lax.all_to_all(
@@ -639,7 +699,7 @@
         out_shape=jax.ShapeDtypeStruct((tiles, narrow), F32),
         in_specs=[spec()] * 3,
         out_specs=spec(),
-        compiler_params=grant(SEND_MIB),
+        compiler_params=grant(UPDATE_MIB),
     )(slots, latents, returned)
 
 

time: 75.2 us -> 65 us (0.86)
  blocking collectives: 24.6 us -> 14.1 us
  starting transfers between devices: 3.29 us -> 8.5 us
  local copies, waits for them, and re-layouts: 7.14 us -> 3.49 us
  waiting for transfers between devices: 4.63 us -> 1.6 us
  Pallas kernels: 35 us -> 36.8 us
    all_to_all x1 -> x0, blocking collectives: 14.3 us -> none  [shards(): lax.all_to_all(outbound.reshape(groups_n * 2, block, narrow), both, split...]
    all_to_all x0 -> x1, starting transfers between devices: none -> 4.92 us  [shards(): lax.all_to_all(outbound.reshape(groups_n * 2, block, narrow), both, split...]
    all_to_all x1, blocking collectives: 10.3 us -> 14.1 us  [shards(): lax.all_to_all(homeward.reshape(groups_n, back, narrow), 'groups', split_...]
    unnamed x34 -> x28, local copies, waits for them, and re-layouts: 7.14 us -> 3.49 us
    ppermute x1, waiting for transfers between devices: 2.98 us -> 0.01 us  [shards(): mate_mod = lax.ppermute(adaptive, 'groups', pairs)]
    pallas_call x1, Pallas kernels: 0.35 us -> 1.81 us  [shards(): pl.pallas_call(functools.partial(send_kernel, capacity, block), out_shape...]
    pallas_call x1, Pallas kernels: 13 us -> 14.1 us  [shards(): pl.pallas_call(functools.partial(attend_kernel, text=text), out_shape=[ha...]
    pallas_call x1, Pallas kernels: 14.5 us -> 13.7 us  [shards(): pl.pallas_call(functools.partial(prepare_kernel, capacity, block, back, s...]
  transfers between devices with their start and end apart: 3 -> 4, of which waited for: 2 -> 1; matrix products, arithmetic and copies ran while one was open for 0% -> 0% of each run, Pallas kernels for 18% -> 46%
where the time goes in v3:
time: 65 us; the launch traced here: 64.6 us
  Pallas kernels  36.8 us (57%)
  blocking collectives  14.1 us (22%)
  starting transfers between devices  8.5 us (13%)
  local copies, waits for them, and re-layouts  3.49 us (5%)
  waiting for transfers between devices  1.6 us (2%)
    all_to_all x1, blocking collectives, shards(): lax.all_to_all(homeward.reshape(groups_n, back, narrow), 'groups', split_...  14.1 us
    pallas_call x1, Pallas kernels, shards(): pl.pallas_call(functools.partial(attend_kernel, text=text), out_shape=[ha...  14.1 us
    pallas_call x1, Pallas kernels, shards(): pl.pallas_call(functools.partial(prepare_kernel, capacity, block, back, s...  13.7 us
    pallas_call x1, Pallas kernels, shards(): pl.pallas_call(functools.partial(finish_kernel, step), out_shape=jax.Shap...  6.14 us
    all_to_all x1, starting transfers between devices, shards(): lax.all_to_all(outbound.reshape(groups_n * 2, block, narrow), both, split...  4.92 us
    unnamed x28, local copies, waits for them, and re-layouts  3.49 us
    ppermute x1, starting transfers between devices, shards(): mate_mod = lax.ppermute(adaptive, 'groups', pairs)  2.94 us
    pallas_call x1, Pallas kernels, shards(): pl.pallas_call(functools.partial(send_kernel, capacity, block), out_shape...  1.81 us
  transfers between devices with their start and end apart: 4, of which 1 were waited for; matrix products, arithmetic and copies ran while one was open for 0% of the time, Pallas kernels for 46%

profile of v3, /device:TPU:0, one launch (start us, length us, event | category | flops | bytes accessed | tf_op | source)
XLA Modules:
  0.0 64.6 jit_solution(7044705536322686603)
XLA Ops:
  0.0 2.9 %collective-permute-start = (f32[5,2,2432]{2,1,0:T(2,128)}, f32[5,2,2432]{2,1,0:T(2,128)S(1)}, u32[]{:S(2)}, u32[]{:S(2)}) collective-permute-start(f32[5,2,2432]{2,1,0:T(2,128)} %bitcast.13), channel_id=1, source_target_pairs={{0,2},{2,0},{4,6},{6,4},{8,10},{10,8},{12,14},{14,12},{16,18},{18,... | collective-permute-start | bytes 291848 | tf_op jit(solution)/shard_map/ppermute | solution.py:594
  2.9 1.8 %shard_map.118 = bf16[16,2,16,128]{3,2,1,0:T(8,128)(2,1)} custom-call(s32[12,128]{1,0:T(8,128)} %bitcast.20, f32[96,128]{1,0:T(8,128)} %latents_ref.3), custom_call_target="tpu_custom_call" | custom-call | tf_op jit(solution)/shard_map/pallas_call | solution.py:596
  4.7 4.9 %all-to-all-start = ((bf16[32,16,128]{2,1,0:T(8,128)(2,1)}), bf16[32,16,128]{2,1,0:T(8,128)(2,1)S(1)}, u32[]{:S(2)}, u32[]{:S(2)}) async-start(bf16[32,16,128]{2,1,0:T(8,128)(2,1)} %bitcast.25), calls=%async_computation | async-start | bytes 262144 | tf_op jit(solution)/shard_map/all_to_all | solution.py:603
  9.7 0.0 collective-permute-done.mate_mod_ref
  9.7 0.0 copy-start.13
  9.7 0.6 copy-done.13
  10.3 13.7 %shard_map.119 = (bf16[256,64]{1,0:T(8,128)(2,1)}, bf16[192,256]{1,0:T(8,128)(2,1)}, bf16[96,256]{1,0:T(8,128)(2,1)}, bf16[2,2,144,640]{3,2,1,0:T(8,128)(2,1)}, ...) custom-call(s32[12,128]{1,0:T(8,128)} %bitcast.21, ...), custom_call_target="tpu_custom_call" | custom-call | flops 4607180800 | bytes 15564800 | tf_op jit(solution)/shard_map/pallas_call | solution.py:618
  24.1 0.0 all-to-all-done
  24.1 0.0 copy-done
  24.1 0.3 collective-permute-start.2
  24.4 0.0 copy-done.8
  24.4 1.1 %copy-done.9 = bf16[2,640,256]{2,1,0:T(8,128)(2,1)S(1)} copy-done((bf16[2,640,256]{2,1,0:T(8,128)(2,1)S(1)}, bf16[2,640,256]{2,1,0:T(8,128)(2,1)}, u32[]{:S(2)}) %copy-start.9) | copy-done | bytes 655384
  25.5 0.9 %copy-done.10 = bf16[192,256]{1,0:T(8,128)(2,1)S(1)} copy-done((bf16[192,256]{1,0:T(8,128)(2,1)S(1)}, bf16[192,256]{1,0:T(8,128)(2,1)}, u32[]{:S(2)}) %copy-start.10) | copy-done | bytes 98328
  26.4 0.8 %copy-done.11 = bf16[256,64]{1,0:T(8,128)(2,1)S(1)} copy-done((bf16[256,64]{1,0:T(8,128)(2,1)S(1)}, bf16[256,64]{1,0:T(8,128)(2,1)}, u32[]{:S(2)}) %copy-start.11) | copy-done | bytes 32792
  27.2 14.1 %shard_map.120 = (bf16[2,192,640]{2,1,0:T(8,128)(2,1)S(1)}, bf16[2,192,640]{2,1,0:T(8,128)(2,1)S(1)}, bf16[192,128]{1,0:T(8,128)(2,1)S(1)}) custom-call(s32[16]{0:T(128)S(1)} %copy-done.8, s32[16]{0:T(128)S(1)} %copy-done.12, bf16[16,2,16,128]{3,2,1,0:T(8,128)(2,1)S(1)} %bitcast.19, bf16[192,256]{1,0:T(8,128)(2,1)S(1)} %copy-done.10, ...), custom_call_target="tpu_custom_call" | custom-call | flops 40265318400 | bytes 8388608 | tf_op jit(solution)/shard_map/pallas_call | solution.py:660
  41.3 0.3 collective-permute-start.1
  41.7 1.6 %collective-permute-done.1.came_ref = bf16[2,192,640]{2,1,0:T(8,128)(2,1)S(1)} collective-permute-done((bf16[2,192,640]{2,1,0:T(8,128)(2,1)S(1)}, bf16[2,192,640]{2,1,0:T(8,128)(2,1)S(1)}, u32[]{:S(2)}, u32[]{:S(2)}) %collective-permute-start.1) | collective-permute-done | bytes 491552 | tf_op jit(solution)/shard_map/ppermute | solution.py:682
  43.3 0.0 collective-permute-done.2.w_came_ref
  43.3 0.0 copy-done.2
  43.3 0.0 copy-start.4
  43.3 0.0 copy-start.5
  43.3 6.1 %shard_map.121 = bf16[256,128]{1,0:T(8,128)(2,1)S(1)} custom-call(s32[16]{0:T(128)S(1)} %copy-done.8, bf16[2,192,640]{2,1,0:T(8,128)(2,1)S(1)} %get-tuple-element.26.kept_ref, bf16[2,192,640]{2,1,0:T(8,128)(2,1)S(1)} %collective-permute-done.1.came_ref, bf16[640,2432]{1,0:T(8,128)(2,1)S(1)} %copy-done, ...), custom_call_target="tpu_custom_call" | custom-call | tf_op jit(solution)/shard_map/pallas_call | solution.py:684
  49.5 14.1 %all_to_all.10 = bf16[16,16,128]{2,1,0:T(8,128)(2,1)S(1)} all-to-all(bf16[16,16,128]{2,1,0:T(8,128)(2,1)S(1)} %bitcast.17), channel_id=1, replica_groups=mesh['groups'=16,'mp'=2] {'groups'}, dimensions={0} | all-to-all | bytes 131072 | tf_op jit(solution)/shard_map/all_to_all | solution.py:694
  63.6 1.0 %shard_map.122 = f32[96,128]{1,0:T(8,128)} custom-call(s32[12,128]{1,0:T(8,128)S(1)} %bitcast.22, f32[96,128]{1,0:T(8,128)S(1)} %copy-done.4, bf16[256,128]{1,0:T(8,128)(2,1)S(1)} %bitcast.18), custom_call_target="tpu_custom_call" | custom-call | tf_op jit(solution)/shard_map/pallas_call | solution.py:697
  (18 shorter events, 0.0 us)
Async XLA Ops:
  0.0 9.7 %collective-permute-start = (f32[5,2,2432]{2,1,0:T(2,128)}, f32[5,2,2432]{2,1,0:T(2,128)S(1)}, u32[]{:S(2)}, u32[]{:S(2)}) collective-permute-start(f32[5,2,2432]{2,1,0:T(2,128)} %bitcast.13), channel_id=1, source_target_pairs={{0,2},{2,0},{4,6},{6,4},{8,10},{10,8},{12,14},{14,12},{16,18},{18,... | collective-permute-start | bytes 291848 | tf_op jit(solution)/shard_map/ppermute | solution.py:594
  4.7 19.3 %all-to-all-start = ((bf16[32,16,128]{2,1,0:T(8,128)(2,1)}), bf16[32,16,128]{2,1,0:T(8,128)(2,1)S(1)}, u32[]{:S(2)}, u32[]{:S(2)}) async-start(bf16[32,16,128]{2,1,0:T(8,128)(2,1)} %bitcast.25), calls=%async_computation | async-start | bytes 262144 | tf_op jit(solution)/shard_map/all_to_all | solution.py:603
  9.7 0.6 copy-start.13
  10.3 13.8 %copy-start = (bf16[640,2432]{1,0:T(8,128)(2,1)S(1)}, bf16[640,2432]{1,0:T(8,128)(2,1)}, u32[]{:S(2)}) copy-start(bf16[640,2432]{1,0:T(8,128)(2,1)} %w_own_ref.1) | copy-start | bytes 9338884
  10.3 14.1 %copy-start.7 = (f32[3,64]{1,0:T(4,128)S(1)}, f32[3,64]{1,0:T(4,128)}, u32[]{:S(2)}) copy-start(f32[3,64]{1,0:T(4,128)} %gains_ref.3) | copy-start | bytes 2308
  10.3 14.1 %copy-start.8 = (s32[16]{0:T(128)S(1)}, s32[16]{0:T(128)}, u32[]{:S(2)}) copy-start(s32[16]{0:T(128)} %live_ref.3) | copy-start | bytes 196
  10.3 14.1 %copy-start.12 = (s32[16]{0:T(128)S(1)}, s32[16]{0:T(128)}, u32[]{:S(2)}) copy-start(s32[16]{0:T(128)} %partner_ref.1) | copy-start | bytes 196
  24.1 19.2 %collective-permute-start.2 = (bf16[640,2432]{1,0:T(8,128)(2,1)S(1)}, bf16[640,2432]{1,0:T(8,128)(2,1)S(1)}, u32[]{:S(2)}, u32[]{:S(2)}) collective-permute-start(bf16[640,2432]{1,0:T(8,128)(2,1)S(1)} %copy-done), channel_id=1, source_target_pairs={{0,1},{1,0},{2,3},{3,2},{4,5},{5,4},{6,7},{7,6},{8,9},{9,8},{10,11... | collective-permute-start | bytes 9338888 | tf_op jit(solution)/shard_map/ppermute | solution.py:658
  24.4 1.1 %copy-start.9 = (bf16[2,640,256]{2,1,0:T(8,128)(2,1)S(1)}, bf16[2,640,256]{2,1,0:T(8,128)(2,1)}, u32[]{:S(2)}) copy-start(bf16[2,640,256]{2,1,0:T(8,128)(2,1)} %get-tuple-element.24.text_keys_hbm) | copy-start | bytes 1966084
  25.5 0.9 %copy-start.10 = (bf16[192,256]{1,0:T(8,128)(2,1)S(1)}, bf16[192,256]{1,0:T(8,128)(2,1)}, u32[]{:S(2)}) copy-start(bf16[192,256]{1,0:T(8,128)(2,1)} %get-tuple-element.20.place_ref) | copy-start | bytes 294916
  26.4 0.8 %copy-start.11 = (bf16[256,64]{1,0:T(8,128)(2,1)S(1)}, bf16[256,64]{1,0:T(8,128)(2,1)}, u32[]{:S(2)}) copy-start(bf16[256,64]{1,0:T(8,128)(2,1)} %get-tuple-element.21.gram_ref) | copy-start | bytes 98308
  27.2 16.0 %copy-start.1 = (bf16[64,2432]{1,0:T(8,128)(2,1)S(1)}, bf16[64,2432]{1,0:T(8,128)(2,1)}, u32[]{:S(2)}) copy-start(bf16[64,2432]{1,0:T(8,128)(2,1)} %embed_ref.3) | copy-start | bytes 933892
  27.2 16.0 %copy-start.2 = (f32[1,2,5,2432]{3,1,2,0:T(2,128)S(1)}, f32[1,2,5,2432]{3,1,2,0:T(2,128)}, u32[]{:S(2)}) copy-start(f32[1,2,5,2432]{3,1,2,0:T(2,128)} %param.17) | copy-start | bytes 291844
  27.2 16.0 %copy-start.3 = (bf16[2432,64]{0,1:T(8,128)(2,1)S(1)}, bf16[2432,64]{0,1:T(8,128)(2,1)}, u32[]{:S(2)}) copy-start(bf16[2432,64]{0,1:T(8,128)(2,1)} %param.22) | copy-start | bytes 933892
  27.2 16.0 %copy-start.6 = (bf16[96,256]{1,0:T(8,128)(2,1)S(1)}, bf16[96,256]{1,0:T(8,128)(2,1)}, u32[]{:S(2)}) copy-start(bf16[96,256]{1,0:T(8,128)(2,1)} %get-tuple-element.30.home_ref) | copy-start | bytes 147460
  41.3 1.9 %collective-permute-start.1 = (bf16[2,192,640]{2,1,0:T(8,128)(2,1)S(1)}, bf16[2,192,640]{2,1,0:T(8,128)(2,1)S(1)}, u32[]{:S(2)}, u32[]{:S(2)}) collective-permute-start(bf16[2,192,640]{2,1,0:T(8,128)(2,1)S(1)} %get-tuple-element.27), channel_id=1, source_target_pairs={{0,1},{1,0},{2,3},{3,2},{4,5},{5,4},{6,7},{7,6},{8,9},{9,8},{10,11... | collective-permute-start | bytes 1474568 | tf_op jit(solution)/shard_map/ppermute | solution.py:682
  43.3 20.3 %copy-start.4 = (f32[96,128]{1,0:T(8,128)S(1)}, f32[96,128]{1,0:T(8,128)}, u32[]{:S(2)}) copy-start(f32[96,128]{1,0:T(8,128)} %latents_ref.3) | copy-start | bytes 147460
  43.3 20.3 %copy-start.5 = (s32[1536]{0:T(1024)S(1)}, s32[1536]{0:T(1024)}, u32[]{:S(2)}) copy-start(s32[1536]{0:T(1024)} %param.13) | copy-start | bytes 18436

commit v4 on v3

--- a/solution.py
+++ b/solution.py
@@ -20,7 +20,6 @@
 LOG2E = 1.4426950408889634
 DEAD = -1e30
 SEND_MIB, PREPARE_MIB, ATTEND_MIB, FINISH_MIB, UPDATE_MIB = 60, 56, 52, 24, 16
-AHEAD = 99
 
 F32 = jnp.float32
 BF16 = jnp.bfloat16
@@ -162,25 +161,24 @@
     block,
     back,
     step,
+    slots_hbm,
+    embed_hbm,
+    own_mod_hbm,
+    mate_mod_hbm,
+    gains_hbm,
+    states_hbm,
+    w_text_hbm,
+    w_qkv_hbm,
+    home_out,
+    rows_hbm,
+    turned_hbm,
     slots_ref,
     embed_ref,
     own_mod_ref,
     mate_mod_ref,
     gains_ref,
-    states_hbm,
-    w_text_hbm,
-    w_qkv_hbm,
-    gram_out,
-    place_out,
-    home_out,
-    folds_hbm,
-    turned_hbm,
-    text_keys_hbm,
-    text_values_hbm,
-    folds_out,
+    rows_out,
     turned_out,
-    text_keys_out,
-    text_values_out,
     states,
     mingled,
     w_qkv,
@@ -190,6 +188,7 @@
     left,
     sems,
     out_sems,
+    small_sems,
 ):
     depth = embed_ref.shape[1]
     width = w_qkv.shape[2]
@@ -198,37 +197,53 @@
     group, _ = position()
     own_rows = 2 * CH
     half = own_rows + PACK
+    fold_rows = 2 * CH + PACK
     chunks = spans(depth, step)
     lane_tiles = width // LANES
 
+    small = (
+        (embed_hbm, embed_ref),
+        (own_mod_hbm, own_mod_ref),
+        (mate_mod_hbm, mate_mod_ref),
+        (slots_hbm, slots_ref),
+        (gains_hbm, gains_ref),
+    )
+    small = [
+        pltpu.make_async_copy(source, target, small_sems.at[index])
+        for index, (source, target) in enumerate(small)
+    ]
+    for copy in small:
+        copy.start()
     sources = []
-    for part in range(3):
+
+    def qkv_source(part):
         for low, high in spans(depth, 2 * step):
             rows = pl.ds(low, high - low)
             sources.append((w_qkv_hbm.at[part, rows], w_qkv.at[part, rows]))
-    qkv_n = len(sources) // 3
+        return len(sources)
+
+    query_end = qkv_source(0)
     sources.append((states_hbm, states))
     w_mingled = w_text_hbm.reshape(2 * depth, width)
     for low, high in chunks:
         rows = pl.ds(2 * low, 2 * (high - low))
         sources.append((w_mingled.at[rows], mingled.at[rows]))
+    text_end = len(sources)
+    qkv_source(1)
+    value_end = qkv_source(2)
     copies = [
         pltpu.make_async_copy(source, target, sems.at[index])
         for index, (source, target) in enumerate(sources)
     ]
-    started = [0]
-
-    def start(count):
-        while started[0] < min(count, len(copies)):
-            copies[started[0]].start()
-            started[0] += 1
+    for copy in copies:
+        copy.start()
 
     def wait(first, last):
         for index in range(first, last):
-            start(index + AHEAD)
             copies[index].wait()
 
-    start(AHEAD)
+    for copy in small:
+        copy.wait()
 
     embed = embed_ref[...].astype(F32)
     centred = embed - jnp.mean(embed, axis=1, keepdims=True)
@@ -251,7 +266,8 @@
         for branch in range(2):
             zeros = jnp.zeros((PACK - 2, product.shape[1]), F32)
             stacked = jnp.concatenate(pieces(product, base, branch) + [zeros], axis=0)
-            folds_out[branch, side, :, lanes] = stacked.astype(BF16)
+            at = side * fold_rows
+            rows_out[branch, at : at + fold_rows, lanes] = stacked.astype(BF16)
 
     def keep_turned(product, base, kind, lanes):
         for branch in range(2):
@@ -267,13 +283,14 @@
         parts = (mm_nt(high, high) + (mm_nt(high, low) + mm_nt(low, high))) * (1.0 / depth)
         top, rest = two_terms(parts)
         bottom = (parts - top.astype(F32) - rest.astype(F32)).astype(BF16)
-        gram_out[0:CH, :] = top
-        gram_out[CH : 2 * CH, :] = rest
-        gram_out[2 * CH : 3 * CH, :] = bottom
-        gram_out[3 * CH : 4 * CH, :] = jnp.zeros((CH, CH), BF16)
+        gram = jnp.concatenate([top, rest, bottom, jnp.zeros((CH, CH), BF16)], axis=1)
+        turned_out[0, 4, 2 * tiles : 2 * tiles + CH, :] = gram
         slots, group_of = slots_by_group(slots_ref, tiles)
-        place_out[0:tiles, :] = tables(slots, group_of, group, capacity, block, 0)
-        place_out[tiles : 2 * tiles, :] = tables(slots, group_of, group ^ 1, capacity, block, capacity)
+        lanes_n = turned_out.shape[3]
+        for side in range(2):
+            place = tables(slots, group_of, group ^ side, capacity, block, side * capacity)
+            for turn, (low, high) in enumerate(spans(place.shape[1], lanes_n)):
+                turned_out[0, 4 + turn, side * tiles : (side + 1) * tiles, 0 : high - low] = place[:, low:high]
         home_out[...] = tables(slots, group_of, group, capacity, back, 0)
 
     out_copies = []
@@ -282,8 +299,10 @@
         out_copies.append(pltpu.make_async_copy(source, target, out_sems.at[len(out_copies)]))
         out_copies[-1].start()
 
-    def divide(first, last):
-        for low, high in chunks[first:last]:
+    def divide():
+        for turn, (low, high) in enumerate(chunks):
+            at = query_end + 1 + turn
+            wait(at, at + 1)
             count = high - low
             for index in range(lane_tiles):
                 lanes = slice(index * LANES, (index + 1) * LANES)
@@ -293,46 +312,44 @@
                     lanes = slice(part * width + index * LANES, part * width + (index + 1) * LANES)
                     split[low:high, lanes] = wide[index, pl.ds(part, count, stride=2), :].astype(BF16)
 
-    wait(0, qkv_n)
+    gram_and_tables()
+    wait(0, query_end + 1)
     query_product = mm(left[0:half, :], w_qkv[0])
-    gram_and_tables()
-    wait(qkv_n, 2 * qkv_n)
+    divide()
+    keep_turned(query_product, 0, 0, slice(0, width))
+
+    product = mm(states[...].reshape(2 * text, depth), split[...])
+    for index in range(2 * lane_tiles):
+        sums[index] = product[:, index * LANES : (index + 1) * LANES]
+    wait(text_end, value_end)
     key_product = mm(left[...], w_qkv[1, :, main])
-    keep_turned(query_product, 0, 0, slice(0, width))
-    wait(2 * qkv_n, 3 * qkv_n)
+    gains = column_of(gains_ref, 2)
+    padding = jnp.zeros((turned_out.shape[3] - text, LANES), F32)
+    for branch in range(2):
+        for index in range(lane_tiles):
+            lanes = slice(index * LANES, (index + 1) * LANES)
+            rows = pl.ds(branch, text, stride=2)
+            keys = jnp.concatenate([sums[index, rows, :], padding], axis=0).T
+            turned_out[branch, 3, lanes, :] = head_norm_down(keys, gains).astype(BF16)
+            values = jnp.concatenate([sums[lane_tiles + index, rows, :], padding], axis=0)
+            rows_out[branch, 2 * fold_rows :, lanes] = values.astype(BF16)
+    keep_turned(key_product, 0, 1, main)
+    keep_turned(key_product, half, 2, main)
     value_product = mm(left[...], w_qkv[2, :, main])
+    put(turned_out.at[0, pl.ds(4, turned_out.shape[1] - 4)], turned_hbm.at[0, pl.ds(4, turned_out.shape[1] - 4)])
     if shared < width:
         edge_product = mm(left[...], jnp.concatenate([w_qkv[1, :, edge], w_qkv[2, :, edge]], axis=1))
-    keep_turned(key_product, 0, 1, main)
-    keep_turned(key_product, half, 2, main)
-    wait(3 * qkv_n, len(copies))
+    keep(value_product, 0, 0, main)
+    keep(value_product, half, 1, main)
     if shared < width:
         keys, values = edge_product[:, : width - shared], edge_product[:, width - shared :]
         keep_turned(keys, 0, 1, edge)
         keep_turned(keys, half, 2, edge)
         keep(values, 0, 0, edge)
         keep(values, half, 1, edge)
-    keep(value_product, 0, 0, main)
-    keep(value_product, half, 1, main)
-    divide(0, len(chunks))
-    put(folds_out, folds_hbm)
-    put(turned_out, turned_hbm)
-
-    product = mm(states[...].reshape(2 * text, depth), split[...])
-    for index in range(2 * lane_tiles):
-        sums[index] = product[:, index * LANES : (index + 1) * LANES]
-    gains = column_of(gains_ref, 2)
-    padding = jnp.zeros((text_values_out.shape[1] - text, LANES), F32)
     for branch in range(2):
-        for index in range(lane_tiles):
-            lanes = slice(index * LANES, (index + 1) * LANES)
-            rows = pl.ds(branch, text, stride=2)
-            keys = jnp.concatenate([sums[index, rows, :], padding], axis=0).T
-            text_keys_out[branch, lanes, :] = head_norm_down(keys, gains).astype(BF16)
-            values = jnp.concatenate([sums[lane_tiles + index, rows, :], padding], axis=0)
-            text_values_out[branch, :, lanes] = values.astype(BF16)
-        put(text_keys_out.at[branch], text_keys_hbm.at[branch])
-        put(text_values_out.at[branch], text_values_hbm.at[branch])
+        put(turned_out.at[branch, pl.ds(0, 4)], turned_hbm.at[branch, pl.ds(0, 4)])
+        put(rows_out.at[branch], rows_hbm.at[branch])
     for copy in out_copies:
         copy.wait()
 
@@ -341,20 +358,14 @@
     live_ref,
     partner_ref,
     arrived_ref,
-    place_ref,
-    gram_ref,
     gains_ref,
-    folds_hbm,
+    rows_hbm,
     turned_hbm,
-    text_keys_hbm,
-    text_values_hbm,
     keep_ref,
     send_ref,
     tokens_ref,
-    folds_ref,
+    rows_ref,
     turned_ref,
-    text_keys_ref,
-    text_values_ref,
     queries,
     keys,
     values,
@@ -362,31 +373,43 @@
     *,
     text,
 ):
-    copies = []
-    for source, target in (
-        (turned_hbm, turned_ref),
-        (folds_hbm, folds_ref),
-        (text_keys_hbm, text_keys_ref),
-        (text_values_hbm, text_values_ref),
-    ):
-        copies.append(pltpu.make_async_copy(source, target, sems.at[len(copies)]))
-        copies[-1].start()
+    def fetch(source, target, index):
+        copy = pltpu.make_async_copy(source, target, sems.at[index])
+        copy.start()
+        return copy
+
+    tables_n = turned_hbm.shape[1] - 4
+    tables_at = (0, pl.ds(4, tables_n))
+    tables_copy = fetch(turned_hbm.at[tables_at], turned_ref.at[tables_at], 0)
+    copies = [
+        (
+            fetch(turned_hbm.at[branch, pl.ds(0, 4)], turned_ref.at[branch, pl.ds(0, 4)], 1 + 2 * branch),
+            fetch(rows_hbm.at[branch], rows_ref.at[branch], 2 + 2 * branch),
+        )
+        for branch in range(2)
+    ]
     group, member = position()
     groups_n, _, block, narrow = arrived_ref.shape
-    tiles = place_ref.shape[0] // 2
-    rows = tiles * TILE
-    half_rows = rows // 2
+    rest = turned_ref.shape[3]
+    half_rows = tokens_ref.shape[0]
+    rows = 2 * half_rows
+    tiles = rows // TILE
     width = keep_ref.shape[2]
-    rest = text_values_ref.shape[1]
+    fold_rows = 2 * CH + PACK
     mate = partner_ref[group]
     own_len = live_ref[group]
     mate_len = jnp.where(mate != group, live_ref[mate], 0)
 
     own_parts, mate_parts = [], []
+    tables_copy.wait()
+    gram = turned_ref[0, 4, 2 * tiles : 2 * tiles + CH, :]
     for turn in range(2):
         source = member ^ turn
         block_rows = arrived_ref[:, pl.ds(source, 1)].reshape(groups_n * block, narrow)
-        found = mm(place_ref[...], block_rows)
+        found = sum(
+            mm(turned_ref[0, 4 + turn, 0 : 2 * tiles, 0 : high - low], block_rows[low:high])
+            for turn, (low, high) in enumerate(spans(groups_n * block, rest))
+        )
         for parts, base in ((own_parts, 0), (mate_parts, tiles)):
             pair = found[base : base + tiles]
             parts.append(jnp.concatenate([pair[:, :CH], pair[:, :CH]], axis=1))
@@ -397,9 +420,9 @@
     lane = iota((1, LANES), 1)
 
     def normed(tokens):
-        narrow_tokens = tokens.astype(BF16)
-        image = mm(narrow_tokens, gram_ref[0 : 2 * CH]) + mm(narrow_tokens, gram_ref[2 * CH :])
-        variance = jnp.sum(image * tokens[:, :CH], axis=1, keepdims=True)
+        image = mm(tokens[:, :CH].astype(BF16), gram)
+        image = (image[:, :LANES] + image[:, LANES:]) * tokens
+        variance = jnp.sum(image, axis=1, keepdims=True)
         scaled = tokens * lax.rsqrt(jnp.maximum(variance, 0.0) + EPS)
         high = scaled.astype(BF16).astype(F32)
         ones = jnp.where(lane < CH + 2, 1.0, 0.0)
@@ -429,23 +452,23 @@
     key_gains = column_of(gains_ref, 1)
     filling = jnp.zeros((CH - PACK, width), BF16)
     lane_tiles = width // LANES
-    for copy in copies:
-        copy.wait()
 
     def fold_of(branch, side):
-        fold = folds_ref[branch, side]
+        fold = rows_ref[branch, side * fold_rows : (side + 1) * fold_rows, :]
         return jnp.concatenate([fold[: 2 * CH], fold[:CH], fold[2 * CH :], filling], axis=0)
 
     def project(branch):
+        for copy in copies[branch]:
+            copy.wait()
         query = head_norm_down(mm(turned_ref[branch, 0], own_turned), query_gains)
         queries[branch] = query.T
         for side, turned in ((0, own_turned), (1, mate_turned)):
             key = head_norm_down(mm(turned_ref[branch, 1 + side], turned), key_gains)
             keys[branch, :, side * rows : (side + 1) * rows] = key.astype(BF16)
-        keys[branch, :, 2 * rows :] = text_keys_ref[branch]
+        keys[branch, :, 2 * rows :] = turned_ref[branch, 3]
         values[branch, 0:rows, :] = mm(own_normed, fold_of(branch, 0)).astype(BF16)
         values[branch, rows : 2 * rows, :] = mm(mate_normed, fold_of(branch, 1)).astype(BF16)
-        values[branch, 2 * rows :, :] = text_values_ref[branch]
+        values[branch, 2 * rows :, :] = rows_ref[branch, 2 * fold_rows :, :]
 
     def score(branch, at, side):
         inside_head = even if side == 0 else jnp.logical_not(even)
@@ -509,8 +532,9 @@
     width, depth = w_own_ref.shape
     both = 2 * half_rows
     chunks = spans(depth, step)
-    kept = kept_ref[...].reshape(both, width)
-    came = came_ref[...].reshape(both, width)
+    attended = jnp.concatenate(
+        [kept_ref[...].reshape(both, width), came_ref[...].reshape(both, width)], axis=1
+    )
 
     def rows_of(index, low, high):
         first = jnp.broadcast_to(mod_ref[index, 0:1, low:high], (half_rows, high - low))
@@ -523,10 +547,9 @@
     pivot = None
     total = jnp.zeros((both, LANES), F32)
     squares = jnp.zeros((both, LANES), F32)
-    for turn, (low, high) in enumerate(chunks):
-        mixed = mm(kept, w_own_ref[:, low:high]).astype(BF16).astype(F32) + mm(
-            came, w_came_ref[:, low:high]
-        ).astype(BF16).astype(F32)
+    for low, high in chunks:
+        weights = jnp.concatenate([w_own_ref[:, low:high], w_came_ref[:, low:high]], axis=0)
+        mixed = mm(attended, weights)
         hidden = mm(tokens_ref[:, :CH], embed_ref[:, low:high])
         hidden = jnp.concatenate([hidden, hidden], axis=0)
         value = hidden + rows_of(2, low, high) * mixed
@@ -609,24 +632,25 @@
     qkv_n = len(spans(depth, 2 * step))
     left_rows = 2 * (2 * CH + PACK)
     rest = round_up(2 * rows + text, 2 * LANES) - 2 * rows
-    kept_shapes = [
-        jax.ShapeDtypeStruct((2, 2, 2 * CH + PACK, width), BF16),
-        jax.ShapeDtypeStruct((2, 3, width, 4 * CH), BF16),
-        jax.ShapeDtypeStruct((2, width, rest), BF16),
-        jax.ShapeDtypeStruct((2, rest, width), BF16),
-    ]
-    gram, place, home, folds, turned, text_keys, text_values = pl.pallas_call(
+    rows_shape = (2, 2 * (2 * CH + PACK) + rest, width)
+    turned_shape = (2, 4 + len(spans(groups_n * block, rest)), width, rest)
+    home, rows_kit, turned_kit = pl.pallas_call(
         functools.partial(prepare_kernel, capacity, block, back, step),
         out_shape=[
-            jax.ShapeDtypeStruct((4 * CH, CH), BF16),
-            jax.ShapeDtypeStruct((2 * tiles, groups_n * block), BF16),
             jax.ShapeDtypeStruct((tiles, groups_n * back), BF16),
-            *kept_shapes,
+            jax.ShapeDtypeStruct(rows_shape, BF16),
+            jax.ShapeDtypeStruct(turned_shape, BF16),
         ],
-        in_specs=[spec()] * 5 + [spec(pltpu.HBM)] * 3,
-        out_specs=[spec()] * 3 + [spec(pltpu.HBM)] * 4,
+        in_specs=[spec(pltpu.HBM)] * 8,
+        out_specs=[spec()] + [spec(pltpu.HBM)] * 2,
         scratch_shapes=[
-            *(pltpu.VMEM(kept.shape, BF16) for kept in kept_shapes),
+            pltpu.VMEM(slots.shape, jnp.int32),
+            pltpu.VMEM(w_embed.shape, BF16),
+            pltpu.VMEM(adaptive.shape, F32),
+            pltpu.VMEM(adaptive.shape, F32),
+            pltpu.VMEM(norm_gains.shape, F32),
+            pltpu.VMEM(rows_shape, BF16),
+            pltpu.VMEM(turned_shape, BF16),
             pltpu.VMEM((text, 2, depth), BF16),
             pltpu.VMEM((2 * depth, width), BF16),
             pltpu.VMEM((3, depth, width), BF16),
@@ -635,7 +659,8 @@
             pltpu.VMEM((2 * width // LANES, 2 * text, LANES), F32),
             pltpu.VMEM((left_rows, depth), BF16),
             pltpu.SemaphoreType.DMA((1 + chunk_n + 3 * qkv_n,)),
-            pltpu.SemaphoreType.DMA((6,)),
+            pltpu.SemaphoreType.DMA((7,)),
+            pltpu.SemaphoreType.DMA((5,)),
         ],
         compiler_params=grant(PREPARE_MIB),
         cost_estimate=pl.CostEstimate(
@@ -654,23 +679,21 @@
         jnp.swapaxes(w_qkv, 0, 1),
     )
 
-    arrived, gram, w_out_sent = lax.optimization_barrier((arrived, gram, w_out))
+    arrived, rows_kit, w_out_sent = lax.optimization_barrier((arrived, rows_kit, w_out))
     came_w_out = lax.ppermute(w_out_sent, "mp", cores)
     half = jax.ShapeDtypeStruct((2, rows // 2, width), BF16)
     kept, sent, tokens = pl.pallas_call(
         functools.partial(attend_kernel, text=text),
         out_shape=[half, half, jax.ShapeDtypeStruct((rows // 2, 2 * CH), BF16)],
-        in_specs=[spec(pltpu.SMEM)] * 2 + [spec()] * 4 + [spec(pltpu.HBM)] * 4,
+        in_specs=[spec(pltpu.SMEM)] * 2 + [spec()] * 2 + [spec(pltpu.HBM)] * 2,
         out_specs=[spec()] * 3,
         scratch_shapes=[
-            pltpu.VMEM(folds.shape, BF16),
-            pltpu.VMEM(turned.shape, BF16),
-            pltpu.VMEM(text_keys.shape, BF16),
-            pltpu.VMEM(text_values.shape, BF16),
+            pltpu.VMEM(rows_shape, BF16),
+            pltpu.VMEM(turned_shape, BF16),
             pltpu.VMEM((2, rows, width), F32),
             pltpu.VMEM((2, width, 2 * rows + rest), BF16),
             pltpu.VMEM((2, 2 * rows + rest, width), BF16),
-            pltpu.SemaphoreType.DMA((4,)),
+            pltpu.SemaphoreType.DMA((5,)),
         ],
         compiler_params=grant(ATTEND_MIB),
         cost_estimate=pl.CostEstimate(
@@ -678,7 +701,7 @@
             bytes_accessed=8 * MIB,
             transcendentals=0,
         ),
-    )(live, partner, arrived, place, gram, norm_gains, folds, turned, text_keys, text_values)
+    )(live, partner, arrived, norm_gains, rows_kit, turned_kit)
     came = lax.ppermute(sent, "mp", cores)
 
     homeward = pl.pallas_call(

time: 65 us -> 60.9 us (0.937)
  local copies, waits for them, and re-layouts: 3.49 us -> 0.69 us
  Pallas kernels: 36.8 us -> 35.6 us
    unnamed x28 -> x22, local copies, waits for them, and re-layouts: 3.49 us -> 0.69 us
    pallas_call x1, Pallas kernels: 6.14 us -> 5.42 us  [shards(): pl.pallas_call(functools.partial(finish_kernel, step), out_shape=jax.Shap...]
  transfers between devices with their start and end apart: 4 -> 4, of which waited for: 1 -> 1; matrix products, arithmetic and copies ran while one was open for 0% -> 0% of each run, Pallas kernels for 46% -> 48%
where the time goes in v4:
time: 60.9 us; the launch traced here: 60.6 us
  Pallas kernels  35.6 us (58%)
  blocking collectives  14.1 us (23%)
  starting transfers between devices  8.5 us (14%)
  waiting for transfers between devices  1.63 us (3%)
  local copies, waits for them, and re-layouts  0.69 us (1%)
    all_to_all x1, blocking collectives, shards(): lax.all_to_all(homeward.reshape(groups_n, back, narrow), 'groups', split_...  14.1 us
    pallas_call x1, Pallas kernels, shards(): pl.pallas_call(functools.partial(attend_kernel, text=text), out_shape=[ha...  14 us
    pallas_call x1, Pallas kernels, shards(): pl.pallas_call(functools.partial(prepare_kernel, capacity, block, back, s...  13.4 us
    pallas_call x1, Pallas kernels, shards(): pl.pallas_call(functools.partial(finish_kernel, step), out_shape=jax.Shap...  5.42 us
    all_to_all x1, starting transfers between devices, shards(): lax.all_to_all(outbound.reshape(groups_n * 2, block, narrow), both, split...  4.92 us
    ppermute x1, starting transfers between devices, shards(): mate_mod = lax.ppermute(adaptive, 'groups', pairs)  2.94 us
    pallas_call x1, Pallas kernels, shards(): pl.pallas_call(functools.partial(send_kernel, capacity, block), out_shape...  1.82 us
    ppermute x1, waiting for transfers between devices, shards(): came = lax.ppermute(sent, 'mp', cores)  1.62 us
  transfers between devices with their start and end apart: 4, of which 1 were waited for; matrix products, arithmetic and copies ran while one was open for 0% of the time, Pallas kernels for 48%

profile of v4, /device:TPU:0, one launch (start us, length us, event | category | flops | bytes accessed | tf_op | source)
XLA Modules:
  0.0 60.6 jit_solution(12096642037443979124)
XLA Ops:
  0.0 2.9 %collective-permute-start = (f32[5,2,2432]{2,1,0:T(2,128)}, f32[5,2,2432]{2,1,0:T(2,128)S(1)}, u32[]{:S(2)}, u32[]{:S(2)}) collective-permute-start(f32[5,2,2432]{2,1,0:T(2,128)} %bitcast.13), channel_id=1, source_target_pairs={{0,2},{2,0},{4,6},{6,4},{8,10},{10,8},{12,14},{14,12},{16,18},{18,... | collective-permute-start | bytes 291848 | tf_op jit(solution)/shard_map/ppermute | solution.py:617
  2.9 1.8 %shard_map.118 = bf16[16,2,16,128]{3,2,1,0:T(8,128)(2,1)} custom-call(s32[12,128]{1,0:T(8,128)} %bitcast.20, f32[96,128]{1,0:T(8,128)} %latents_ref.3), custom_call_target="tpu_custom_call" | custom-call | tf_op jit(solution)/shard_map/pallas_call | solution.py:619
  4.8 4.9 %all-to-all-start = ((bf16[32,16,128]{2,1,0:T(8,128)(2,1)}), bf16[32,16,128]{2,1,0:T(8,128)(2,1)S(1)}, u32[]{:S(2)}, u32[]{:S(2)}) async-start(bf16[32,16,128]{2,1,0:T(8,128)(2,1)} %bitcast.25), calls=%async_computation | async-start | bytes 262144 | tf_op jit(solution)/shard_map/all_to_all | solution.py:626
  9.7 0.0 collective-permute-done.mate_mod_hbm
  9.7 0.0 copy-start.10
  9.7 0.6 %copy-done.10 = f32[5,2,2432]{2,1,0:T(2,128)} copy-done((f32[5,2,2432]{2,1,0:T(2,128)}, f32[5,2,2432]{2,1,0:T(2,128)S(1)}, u32[]{:S(2)}) %copy-start.10) | copy-done | bytes 97304
  10.4 13.4 %shard_map.119 = (bf16[96,256]{1,0:T(8,128)(2,1)}, bf16[2,544,640]{2,1,0:T(8,128)(2,1)}, bf16[2,5,640,256]{3,2,1,0:T(8,128)(2,1)}) custom-call(s32[12,128]{1,0:T(8,128)} %bitcast.21, bf16[64,2432]{1,0:T(8,128)(2,1)} %embed_ref.1, f32[5,2,2432]{2,1,0:T(2,128)} %bitcast.14, f32[5,2,2432]{2,1,0:T(2,128)} %copy-done.10, f32[3,64]{1,0:T(4,128)} %gains_ref.1, ...), custom_call_target="tpu_custom_call" | custom-call | flops 4607180800 | bytes 15564800 | tf_op jit(solution)/shard_map/pallas_call | solution.py:637
  23.7 0.0 all-to-all-done
  23.7 0.3 collective-permute-start.2
  24.1 0.0 copy-done.7
  24.1 0.0 copy-done.9
  24.1 0.0 copy-start.2
  24.1 0.0 copy-start.3
  24.1 0.0 copy-start.6
  24.1 14.0 %shard_map.120 = (bf16[2,192,640]{2,1,0:T(8,128)(2,1)S(1)}, bf16[2,192,640]{2,1,0:T(8,128)(2,1)S(1)}, bf16[192,128]{1,0:T(8,128)(2,1)S(1)}) custom-call(s32[16]{0:T(128)S(1)} %copy-done.8, s32[16]{0:T(128)S(1)} %copy-done.9, bf16[16,2,16,128]{3,2,1,0:T(8,128)(2,1)S(1)} %bitcast.19, f32[3,64]{1,0:T(4,128)S(1)} %copy-done.7, ...), custom_call_target="tpu_custom_call" | custom-call | flops 40265318400 | bytes 8388608 | tf_op jit(solution)/shard_map/pallas_call | solution.py:685
  38.1 0.3 collective-permute-start.1
  38.4 1.6 %collective-permute-done.1.came_ref = bf16[2,192,640]{2,1,0:T(8,128)(2,1)S(1)} collective-permute-done((bf16[2,192,640]{2,1,0:T(8,128)(2,1)S(1)}, bf16[2,192,640]{2,1,0:T(8,128)(2,1)S(1)}, u32[]{:S(2)}, u32[]{:S(2)}) %collective-permute-start.1) | collective-permute-done | bytes 491552 | tf_op jit(solution)/shard_map/ppermute | solution.py:705
  40.0 0.0 collective-permute-done.2.w_came_ref
  40.0 0.0 copy-done.1
  40.1 0.0 copy-start.4
  40.1 0.0 copy-start.5
  40.1 5.4 %shard_map.121 = bf16[256,128]{1,0:T(8,128)(2,1)S(1)} custom-call(s32[16]{0:T(128)S(1)} %copy-done.8, bf16[2,192,640]{2,1,0:T(8,128)(2,1)S(1)} %get-tuple-element.18.kept_ref, bf16[2,192,640]{2,1,0:T(8,128)(2,1)S(1)} %collective-permute-done.1.came_ref, bf16[640,2432]{1,0:T(8,128)(2,1)S(1)} %copy-done, ...), custom_call_target="tpu_custom_call" | custom-call | tf_op jit(solution)/shard_map/pallas_call | solution.py:707
  45.5 14.1 %all_to_all.10 = bf16[16,16,128]{2,1,0:T(8,128)(2,1)S(1)} all-to-all(bf16[16,16,128]{2,1,0:T(8,128)(2,1)S(1)} %bitcast.17), channel_id=1, replica_groups=mesh['groups'=16,'mp'=2] {'groups'}, dimensions={0} | all-to-all | bytes 131072 | tf_op jit(solution)/shard_map/all_to_all | solution.py:717
  59.6 1.0 %shard_map.122 = f32[96,128]{1,0:T(8,128)} custom-call(s32[12,128]{1,0:T(8,128)S(1)} %bitcast.22, f32[96,128]{1,0:T(8,128)S(1)} %copy-done.4, bf16[256,128]{1,0:T(8,128)(2,1)S(1)} %bitcast.18), custom_call_target="tpu_custom_call" | custom-call | tf_op jit(solution)/shard_map/pallas_call | solution.py:720
  (12 shorter events, 0.0 us)
Async XLA Ops:
  0.0 9.7 %collective-permute-start = (f32[5,2,2432]{2,1,0:T(2,128)}, f32[5,2,2432]{2,1,0:T(2,128)S(1)}, u32[]{:S(2)}, u32[]{:S(2)}) collective-permute-start(f32[5,2,2432]{2,1,0:T(2,128)} %bitcast.13), channel_id=1, source_target_pairs={{0,2},{2,0},{4,6},{6,4},{8,10},{10,8},{12,14},{14,12},{16,18},{18,... | collective-permute-start | bytes 291848 | tf_op jit(solution)/shard_map/ppermute | solution.py:617
  4.8 19.0 %all-to-all-start = ((bf16[32,16,128]{2,1,0:T(8,128)(2,1)}), bf16[32,16,128]{2,1,0:T(8,128)(2,1)S(1)}, u32[]{:S(2)}, u32[]{:S(2)}) async-start(bf16[32,16,128]{2,1,0:T(8,128)(2,1)} %bitcast.25), calls=%async_computation | async-start | bytes 262144 | tf_op jit(solution)/shard_map/all_to_all | solution.py:626
  9.7 0.6 %copy-start.10 = (f32[5,2,2432]{2,1,0:T(2,128)}, f32[5,2,2432]{2,1,0:T(2,128)S(1)}, u32[]{:S(2)}) copy-start(f32[5,2,2432]{2,1,0:T(2,128)S(1)} %collective-permute-done.mate_mod_hbm) | copy-start | bytes 291844
  10.4 13.4 %copy-start = (bf16[640,2432]{1,0:T(8,128)(2,1)S(1)}, bf16[640,2432]{1,0:T(8,128)(2,1)}, u32[]{:S(2)}) copy-start(bf16[640,2432]{1,0:T(8,128)(2,1)} %w_own_ref.1) | copy-start | bytes 9338884
  10.4 13.7 %copy-start.7 = (f32[3,64]{1,0:T(4,128)S(1)}, f32[3,64]{1,0:T(4,128)}, u32[]{:S(2)}) copy-start(f32[3,64]{1,0:T(4,128)} %gains_ref.1) | copy-start | bytes 2308
  10.4 13.7 %copy-start.8 = (s32[16]{0:T(128)S(1)}, s32[16]{0:T(128)}, u32[]{:S(2)}) copy-start(s32[16]{0:T(128)} %live_ref.3) | copy-start | bytes 196
  10.4 13.7 %copy-start.9 = (s32[16]{0:T(128)S(1)}, s32[16]{0:T(128)}, u32[]{:S(2)}) copy-start(s32[16]{0:T(128)} %partner_ref.1) | copy-start | bytes 196
  23.7 16.3 %collective-permute-start.2 = (bf16[640,2432]{1,0:T(8,128)(2,1)S(1)}, bf16[640,2432]{1,0:T(8,128)(2,1)S(1)}, u32[]{:S(2)}, u32[]{:S(2)}) collective-permute-start(bf16[640,2432]{1,0:T(8,128)(2,1)S(1)} %copy-done), channel_id=1, source_target_pairs={{0,1},{1,0},{2,3},{3,2},{4,5},{5,4},{6,7},{7,6},{8,9},{9,8},{10,11... | collective-permute-start | bytes 9338888 | tf_op jit(solution)/shard_map/ppermute | solution.py:683
  24.1 16.0 %copy-start.1 = (bf16[64,2432]{1,0:T(8,128)(2,1)S(1)}, bf16[64,2432]{1,0:T(8,128)(2,1)}, u32[]{:S(2)}) copy-start(bf16[64,2432]{1,0:T(8,128)(2,1)} %embed_ref.1) | copy-start | bytes 933892
  24.1 16.0 %copy-start.2 = (f32[1,2,5,2432]{3,1,2,0:T(2,128)S(1)}, f32[1,2,5,2432]{3,1,2,0:T(2,128)}, u32[]{:S(2)}) copy-start(f32[1,2,5,2432]{3,1,2,0:T(2,128)} %param.17) | copy-start | bytes 291844
  24.1 15.9 %copy-start.3 = (bf16[2432,64]{0,1:T(8,128)(2,1)S(1)}, bf16[2432,64]{0,1:T(8,128)(2,1)}, u32[]{:S(2)}) copy-start(bf16[2432,64]{0,1:T(8,128)(2,1)} %param.22) | copy-start | bytes 933892
  24.1 15.9 %copy-start.6 = (bf16[96,256]{1,0:T(8,128)(2,1)S(1)}, bf16[96,256]{1,0:T(8,128)(2,1)}, u32[]{:S(2)}) copy-start(bf16[96,256]{1,0:T(8,128)(2,1)} %get-tuple-element.22.home_ref) | copy-start | bytes 147460
  38.1 1.9 %collective-permute-start.1 = (bf16[2,192,640]{2,1,0:T(8,128)(2,1)S(1)}, bf16[2,192,640]{2,1,0:T(8,128)(2,1)S(1)}, u32[]{:S(2)}, u32[]{:S(2)}) collective-permute-start(bf16[2,192,640]{2,1,0:T(8,128)(2,1)S(1)} %get-tuple-element.19), channel_id=1, source_target_pairs={{0,1},{1,0},{2,3},{3,2},{4,5},{5,4},{6,7},{7,6},{8,9},{9,8},{10,11... | collective-permute-start | bytes 1474568 | tf_op jit(solution)/shard_map/ppermute | solution.py:705
  40.1 19.5 %copy-start.4 = (f32[96,128]{1,0:T(8,128)S(1)}, f32[96,128]{1,0:T(8,128)}, u32[]{:S(2)}) copy-start(f32[96,128]{1,0:T(8,128)} %latents_ref.3) | copy-start | bytes 147460
  40.1 19.5 %copy-start.5 = (s32[1536]{0:T(1024)S(1)}, s32[1536]{0:T(1024)}, u32[]{:S(2)}) copy-start(s32[1536]{0:T(1024)} %param.13) | copy-start | bytes 18436

commit v5 on v4

--- a/solution.py
+++ b/solution.py
@@ -445,7 +445,7 @@
     text_dead = jnp.where(iota((1, rest), 1) < text, 0.0, DEAD)
     dead = jnp.concatenate([own_dead, mate_dead, text_dead], axis=1)
     dead = jnp.where(iota((PACK, 1), 0) == 0, dead, 0.0).astype(BF16)
-    dead = jnp.concatenate([dead, jnp.zeros((HEAD - PACK, dead.shape[1]), BF16)], axis=0)
+    one_row = jnp.where(iota((PACK, rows), 0) == 0, 1.0, 0.0)
 
     even = lane < HEAD
     query_gains = column_of(gains_ref, 0) * (LOG2E * HEAD**-0.5)
@@ -461,7 +461,9 @@
         for copy in copies[branch]:
             copy.wait()
         query = head_norm_down(mm(turned_ref[branch, 0], own_turned), query_gains)
-        queries[branch] = query.T
+        for head in range(width // HEAD):
+            stacked = jnp.concatenate([query[head * HEAD : (head + 1) * HEAD], one_row], axis=0)
+            queries[branch, head] = stacked.T.astype(BF16)
         for side, turned in ((0, own_turned), (1, mate_turned)):
             key = head_norm_down(mm(turned_ref[branch, 1 + side], turned), key_gains)
             keys[branch, :, side * rows : (side + 1) * rows] = key.astype(BF16)
@@ -471,13 +473,9 @@
         values[branch, 2 * rows :, :] = rows_ref[branch, 2 * fold_rows :, :]
 
     def score(branch, at, side):
-        inside_head = even if side == 0 else jnp.logical_not(even)
-        marker = lane == (HEAD if side == 0 else 0)
-        query = queries[branch, :, at : at + LANES]
-        query = jnp.where(inside_head, query, jnp.where(marker, 1.0, 0.0)).astype(BF16)
         first = at + side * HEAD
-        one_keys = keys[branch, first : first + HEAD, :]
-        return mm(query, jnp.concatenate([one_keys, dead] if side == 0 else [dead, one_keys], axis=0))
+        one_keys = jnp.concatenate([keys[branch, first : first + HEAD, :], dead], axis=0)
+        return mm(queries[branch, first // HEAD], one_keys)
 
     outs = []
 
@@ -506,7 +504,7 @@
                 if waiting is not None:
                     settle(*waiting)
                 waiting = (branch, at, side, scores)
-            if branch == 0 and pair == lane_tiles // 2:
+            if branch == 0 and pair == 0:
                 project(1)
     settle(*waiting)
 
@@ -690,7 +688,7 @@
         scratch_shapes=[
             pltpu.VMEM(rows_shape, BF16),
             pltpu.VMEM(turned_shape, BF16),
-            pltpu.VMEM((2, rows, width), F32),
+            pltpu.VMEM((2, width // HEAD, rows, HEAD + PACK), BF16),
             pltpu.VMEM((2, width, 2 * rows + rest), BF16),
             pltpu.VMEM((2, 2 * rows + rest, width), BF16),
             pltpu.SemaphoreType.DMA((5,)),

time: 60.9 us -> 60.8 us (level)
  no operation moved by 1% of the time
where the time goes in v5:
time: 60.8 us; the launch traced here: 60.5 us
  Pallas kernels  35.5 us (58%)
  blocking collectives  14.1 us (23%)
  starting transfers between devices  8.5 us (14%)
  waiting for transfers between devices  1.63 us (3%)
  local copies, waits for them, and re-layouts  0.69 us (1%)
    all_to_all x1, blocking collectives, shards(): lax.all_to_all(homeward.reshape(groups_n, back, narrow), 'groups', split_...  14.1 us
    pallas_call x1, Pallas kernels, shards(): pl.pallas_call(functools.partial(attend_kernel, text=text), out_shape=[ha...  13.8 us
    pallas_call x1, Pallas kernels, shards(): pl.pallas_call(functools.partial(prepare_kernel, capacity, block, back, s...  13.4 us
    pallas_call x1, Pallas kernels, shards(): pl.pallas_call(functools.partial(finish_kernel, step), out_shape=jax.Shap...  5.42 us
    all_to_all x1, starting transfers between devices, shards(): lax.all_to_all(outbound.reshape(groups_n * 2, block, narrow), both, split...  4.92 us
    ppermute x1, starting transfers between devices, shards(): mate_mod = lax.ppermute(adaptive, 'groups', pairs)  2.94 us
    pallas_call x1, Pallas kernels, shards(): pl.pallas_call(functools.partial(send_kernel, capacity, block), out_shape...  1.82 us
    ppermute x1, waiting for transfers between devices, shards(): came = lax.ppermute(sent, 'mp', cores)  1.62 us
  transfers between devices with their start and end apart: 4, of which 1 were waited for; matrix products, arithmetic and copies ran while one was open for 0% of the time, Pallas kernels for 48%

profile of v5, /device:TPU:0, one launch (start us, length us, event | category | flops | bytes accessed | tf_op | source)
XLA Modules:
  0.0 60.5 jit_solution(8935817831586072646)
XLA Ops:
  0.0 2.9 %collective-permute-start = (f32[5,2,2432]{2,1,0:T(2,128)}, f32[5,2,2432]{2,1,0:T(2,128)S(1)}, u32[]{:S(2)}, u32[]{:S(2)}) collective-permute-start(f32[5,2,2432]{2,1,0:T(2,128)} %bitcast.13), channel_id=1, source_target_pairs={{0,2},{2,0},{4,6},{6,4},{8,10},{10,8},{12,14},{14,12},{16,18},{18,... | collective-permute-start | bytes 291848 | tf_op jit(solution)/shard_map/ppermute | solution.py:615
  2.9 1.8 %shard_map.118 = bf16[16,2,16,128]{3,2,1,0:T(8,128)(2,1)} custom-call(s32[12,128]{1,0:T(8,128)} %bitcast.20, f32[96,128]{1,0:T(8,128)} %latents_ref.3), custom_call_target="tpu_custom_call" | custom-call | tf_op jit(solution)/shard_map/pallas_call | solution.py:617
  4.8 4.9 %all-to-all-start = ((bf16[32,16,128]{2,1,0:T(8,128)(2,1)}), bf16[32,16,128]{2,1,0:T(8,128)(2,1)S(1)}, u32[]{:S(2)}, u32[]{:S(2)}) async-start(bf16[32,16,128]{2,1,0:T(8,128)(2,1)} %bitcast.25), calls=%async_computation | async-start | bytes 262144 | tf_op jit(solution)/shard_map/all_to_all | solution.py:624
  9.7 0.0 collective-permute-done.mate_mod_hbm
  9.7 0.0 copy-start.10
  9.7 0.6 %copy-done.10 = f32[5,2,2432]{2,1,0:T(2,128)} copy-done((f32[5,2,2432]{2,1,0:T(2,128)}, f32[5,2,2432]{2,1,0:T(2,128)S(1)}, u32[]{:S(2)}) %copy-start.10) | copy-done | bytes 97304
  10.4 13.4 %shard_map.119 = (bf16[96,256]{1,0:T(8,128)(2,1)}, bf16[2,544,640]{2,1,0:T(8,128)(2,1)}, bf16[2,5,640,256]{3,2,1,0:T(8,128)(2,1)}) custom-call(s32[12,128]{1,0:T(8,128)} %bitcast.21, bf16[64,2432]{1,0:T(8,128)(2,1)} %embed_ref.1, f32[5,2,2432]{2,1,0:T(2,128)} %bitcast.14, f32[5,2,2432]{2,1,0:T(2,128)} %copy-done.10, f32[3,64]{1,0:T(4,128)} %gains_ref.1, ...), custom_call_target="tpu_custom_call" | custom-call | flops 4607180800 | bytes 15564800 | tf_op jit(solution)/shard_map/pallas_call | solution.py:635
  23.7 0.0 all-to-all-done
  23.7 0.0 copy-done
  23.7 0.3 collective-permute-start.2
  24.1 0.0 copy-done.7
  24.1 0.0 copy-done.9
  24.1 0.0 copy-start.2
  24.1 0.0 copy-start.3
  24.1 0.0 copy-start.6
  24.1 13.8 %shard_map.120 = (bf16[2,192,640]{2,1,0:T(8,128)(2,1)S(1)}, bf16[2,192,640]{2,1,0:T(8,128)(2,1)S(1)}, bf16[192,128]{1,0:T(8,128)(2,1)S(1)}) custom-call(s32[16]{0:T(128)S(1)} %copy-done.8, s32[16]{0:T(128)S(1)} %copy-done.9, bf16[16,2,16,128]{3,2,1,0:T(8,128)(2,1)S(1)} %bitcast.19, f32[3,64]{1,0:T(4,128)S(1)} %copy-done.7, ...), custom_call_target="tpu_custom_call" | custom-call | flops 40265318400 | bytes 8388608 | tf_op jit(solution)/shard_map/pallas_call | solution.py:683
  38.0 0.3 collective-permute-start.1
  38.3 1.6 %collective-permute-done.1.came_ref = bf16[2,192,640]{2,1,0:T(8,128)(2,1)S(1)} collective-permute-done((bf16[2,192,640]{2,1,0:T(8,128)(2,1)S(1)}, bf16[2,192,640]{2,1,0:T(8,128)(2,1)S(1)}, u32[]{:S(2)}, u32[]{:S(2)}) %collective-permute-start.1) | collective-permute-done | bytes 491552 | tf_op jit(solution)/shard_map/ppermute | solution.py:703
  39.9 0.0 collective-permute-done.2.w_came_ref
  39.9 0.0 copy-start.4
  40.0 0.0 copy-start.5
  40.0 5.4 %shard_map.121 = bf16[256,128]{1,0:T(8,128)(2,1)S(1)} custom-call(s32[16]{0:T(128)S(1)} %copy-done.8, bf16[2,192,640]{2,1,0:T(8,128)(2,1)S(1)} %get-tuple-element.18.kept_ref, bf16[2,192,640]{2,1,0:T(8,128)(2,1)S(1)} %collective-permute-done.1.came_ref, bf16[640,2432]{1,0:T(8,128)(2,1)S(1)} %copy-done, ...), custom_call_target="tpu_custom_call" | custom-call | tf_op jit(solution)/shard_map/pallas_call | solution.py:705
  45.4 14.1 %all_to_all.10 = bf16[16,16,128]{2,1,0:T(8,128)(2,1)S(1)} all-to-all(bf16[16,16,128]{2,1,0:T(8,128)(2,1)S(1)} %bitcast.17), channel_id=1, replica_groups=mesh['groups'=16,'mp'=2] {'groups'}, dimensions={0} | all-to-all | bytes 131072 | tf_op jit(solution)/shard_map/all_to_all | solution.py:715
  59.5 1.0 %shard_map.122 = f32[96,128]{1,0:T(8,128)} custom-call(s32[12,128]{1,0:T(8,128)S(1)} %bitcast.22, f32[96,128]{1,0:T(8,128)S(1)} %copy-done.4, bf16[256,128]{1,0:T(8,128)(2,1)S(1)} %bitcast.18), custom_call_target="tpu_custom_call" | custom-call | tf_op jit(solution)/shard_map/pallas_call | solution.py:718
  (12 shorter events, 0.0 us)
Async XLA Ops:
  0.0 9.7 %collective-permute-start = (f32[5,2,2432]{2,1,0:T(2,128)}, f32[5,2,2432]{2,1,0:T(2,128)S(1)}, u32[]{:S(2)}, u32[]{:S(2)}) collective-permute-start(f32[5,2,2432]{2,1,0:T(2,128)} %bitcast.13), channel_id=1, source_target_pairs={{0,2},{2,0},{4,6},{6,4},{8,10},{10,8},{12,14},{14,12},{16,18},{18,... | collective-permute-start | bytes 291848 | tf_op jit(solution)/shard_map/ppermute | solution.py:615
  4.8 19.0 %all-to-all-start = ((bf16[32,16,128]{2,1,0:T(8,128)(2,1)}), bf16[32,16,128]{2,1,0:T(8,128)(2,1)S(1)}, u32[]{:S(2)}, u32[]{:S(2)}) async-start(bf16[32,16,128]{2,1,0:T(8,128)(2,1)} %bitcast.25), calls=%async_computation | async-start | bytes 262144 | tf_op jit(solution)/shard_map/all_to_all | solution.py:624
  9.7 0.6 %copy-start.10 = (f32[5,2,2432]{2,1,0:T(2,128)}, f32[5,2,2432]{2,1,0:T(2,128)S(1)}, u32[]{:S(2)}) copy-start(f32[5,2,2432]{2,1,0:T(2,128)S(1)} %collective-permute-done.mate_mod_hbm) | copy-start | bytes 291844
  10.4 13.4 %copy-start = (bf16[640,2432]{1,0:T(8,128)(2,1)S(1)}, bf16[640,2432]{1,0:T(8,128)(2,1)}, u32[]{:S(2)}) copy-start(bf16[640,2432]{1,0:T(8,128)(2,1)} %w_own_ref.1) | copy-start | bytes 9338884
  10.4 13.7 %copy-start.7 = (f32[3,64]{1,0:T(4,128)S(1)}, f32[3,64]{1,0:T(4,128)}, u32[]{:S(2)}) copy-start(f32[3,64]{1,0:T(4,128)} %gains_ref.1) | copy-start | bytes 2308
  10.4 13.7 %copy-start.8 = (s32[16]{0:T(128)S(1)}, s32[16]{0:T(128)}, u32[]{:S(2)}) copy-start(s32[16]{0:T(128)} %live_ref.3) | copy-start | bytes 196
  10.4 13.7 %copy-start.9 = (s32[16]{0:T(128)S(1)}, s32[16]{0:T(128)}, u32[]{:S(2)}) copy-start(s32[16]{0:T(128)} %partner_ref.1) | copy-start | bytes 196
  23.7 16.2 %collective-permute-start.2 = (bf16[640,2432]{1,0:T(8,128)(2,1)S(1)}, bf16[640,2432]{1,0:T(8,128)(2,1)S(1)}, u32[]{:S(2)}, u32[]{:S(2)}) collective-permute-start(bf16[640,2432]{1,0:T(8,128)(2,1)S(1)} %copy-done), channel_id=1, source_target_pairs={{0,1},{1,0},{2,3},{3,2},{4,5},{5,4},{6,7},{7,6},{8,9},{9,8},{10,11... | collective-permute-start | bytes 9338888 | tf_op jit(solution)/shard_map/ppermute | solution.py:681
  24.1 15.8 %copy-start.1 = (bf16[64,2432]{1,0:T(8,128)(2,1)S(1)}, bf16[64,2432]{1,0:T(8,128)(2,1)}, u32[]{:S(2)}) copy-start(bf16[64,2432]{1,0:T(8,128)(2,1)} %embed_ref.1) | copy-start | bytes 933892
  24.1 15.8 %copy-start.2 = (f32[1,2,5,2432]{3,1,2,0:T(2,128)S(1)}, f32[1,2,5,2432]{3,1,2,0:T(2,128)}, u32[]{:S(2)}) copy-start(f32[1,2,5,2432]{3,1,2,0:T(2,128)} %param.17) | copy-start | bytes 291844
  24.1 15.8 %copy-start.3 = (bf16[2432,64]{0,1:T(8,128)(2,1)S(1)}, bf16[2432,64]{0,1:T(8,128)(2,1)}, u32[]{:S(2)}) copy-start(bf16[2432,64]{0,1:T(8,128)(2,1)} %param.22) | copy-start | bytes 933892
  24.1 15.8 %copy-start.6 = (bf16[96,256]{1,0:T(8,128)(2,1)S(1)}, bf16[96,256]{1,0:T(8,128)(2,1)}, u32[]{:S(2)}) copy-start(bf16[96,256]{1,0:T(8,128)(2,1)} %get-tuple-element.22.home_ref) | copy-start | bytes 147460
  38.0 1.9 %collective-permute-start.1 = (bf16[2,192,640]{2,1,0:T(8,128)(2,1)S(1)}, bf16[2,192,640]{2,1,0:T(8,128)(2,1)S(1)}, u32[]{:S(2)}, u32[]{:S(2)}) collective-permute-start(bf16[2,192,640]{2,1,0:T(8,128)(2,1)S(1)} %get-tuple-element.19), channel_id=1, source_target_pairs={{0,1},{1,0},{2,3},{3,2},{4,5},{5,4},{6,7},{7,6},{8,9},{9,8},{10,11... | collective-permute-start | bytes 1474568 | tf_op jit(solution)/shard_map/ppermute | solution.py:703
  39.9 19.5 %copy-start.4 = (f32[96,128]{1,0:T(8,128)S(1)}, f32[96,128]{1,0:T(8,128)}, u32[]{:S(2)}) copy-start(f32[96,128]{1,0:T(8,128)} %latents_ref.3) | copy-start | bytes 147460
  40.0 19.5 %copy-start.5 = (s32[1536]{0:T(1024)S(1)}, s32[1536]{0:T(1024)}, u32[]{:S(2)}) copy-start(s32[1536]{0:T(1024)} %param.13) | copy-start | bytes 18436

commit v6 on v5

--- a/solution.py
+++ b/solution.py
@@ -509,12 +509,18 @@
     settle(*waiting)
 
 
+def begin_kernel(step, kept_ref, w_own_ref, out_ref):
+    width, depth = w_own_ref.shape
+    kept = kept_ref[...].reshape(out_ref.shape[0], width)
+    for low, high in spans(depth, step):
+        out_ref[:, low:high] = mm(kept, w_own_ref[:, low:high])
+
+
 def finish_kernel(
     step,
     live_ref,
-    kept_ref,
+    begun_ref,
     came_ref,
-    w_own_ref,
     w_came_ref,
     tokens_ref,
     embed_ref,
@@ -527,12 +533,10 @@
     group, member = position()
     half_rows = tokens_ref.shape[0]
     tiles = home_ref.shape[0]
-    width, depth = w_own_ref.shape
+    width, depth = w_came_ref.shape
     both = 2 * half_rows
     chunks = spans(depth, step)
-    attended = jnp.concatenate(
-        [kept_ref[...].reshape(both, width), came_ref[...].reshape(both, width)], axis=1
-    )
+    came = came_ref[...].reshape(both, width)
 
     def rows_of(index, low, high):
         first = jnp.broadcast_to(mod_ref[index, 0:1, low:high], (half_rows, high - low))
@@ -546,8 +550,7 @@
     total = jnp.zeros((both, LANES), F32)
     squares = jnp.zeros((both, LANES), F32)
     for low, high in chunks:
-        weights = jnp.concatenate([w_own_ref[:, low:high], w_came_ref[:, low:high]], axis=0)
-        mixed = mm(attended, weights)
+        mixed = begun_ref[:, low:high] + mm(came, w_came_ref[:, low:high])
         hidden = mm(tokens_ref[:, :CH], embed_ref[:, low:high])
         hidden = jnp.concatenate([hidden, hidden], axis=0)
         value = hidden + rows_of(2, low, high) * mixed
@@ -702,16 +705,26 @@
     )(live, partner, arrived, norm_gains, rows_kit, turned_kit)
     came = lax.ppermute(sent, "mp", cores)
 
+    begun = pl.pallas_call(
+        functools.partial(begin_kernel, step),
+        out_shape=jax.ShapeDtypeStruct((rows, depth), F32),
+        in_specs=[spec()] * 2,
+        out_specs=spec(),
+        compiler_params=grant(FINISH_MIB),
+        cost_estimate=pl.CostEstimate(
+            flops=2 * rows * depth * width, bytes_accessed=8 * MIB, transcendentals=0
+        ),
+    )(kept, w_out)
     homeward = pl.pallas_call(
         functools.partial(finish_kernel, step),
         out_shape=jax.ShapeDtypeStruct((groups_n * back, narrow), BF16),
-        in_specs=[spec(pltpu.SMEM)] + [spec()] * 9,
+        in_specs=[spec(pltpu.SMEM)] + [spec()] * 8,
         out_specs=spec(),
         scratch_shapes=[
             pltpu.VMEM((rows, depth), F32),
         ],
         compiler_params=grant(FINISH_MIB),
-    )(live, kept, came, w_out, came_w_out, tokens, w_embed, adaptive, w_final.T, home)
+    )(live, begun, came, came_w_out, tokens, w_embed, adaptive, w_final.T, home)
     returned = lax.all_to_all(
         homeward.reshape(groups_n, back, narrow), "groups", split_axis=0, concat_axis=0, tiled=True
     ).reshape(groups_n * back, narrow)

time: 60.8 us -> 60.2 us (level)
  waiting for transfers between devices: 1.63 us -> 0.01 us
  Pallas kernels: 35.5 us -> 36.4 us
    pallas_call x0 -> x1, Pallas kernels: none -> 1.67 us  [shards(): pl.pallas_call(functools.partial(begin_kernel, step), out_shape=jax.Shape...]
    ppermute x1, waiting for transfers between devices: 1.62 us -> 0.01 us  [shards(): came = lax.ppermute(sent, 'mp', cores)]
    pallas_call x1, Pallas kernels: 5.42 us -> 4.71 us  [shards(): pl.pallas_call(functools.partial(finish_kernel, step), out_shape=jax.Shap...]
  transfers between devices with their start and end apart: 4 -> 4, of which waited for: 1 -> 0; matrix products, arithmetic and copies ran while one was open for 0% -> 0% of each run, Pallas kernels for 48% -> 51%
where the time goes in v6:
time: 60.2 us; the launch traced here: 59.9 us
  Pallas kernels  36.4 us (60%)
  blocking collectives  14.2 us (24%)
  starting transfers between devices  8.5 us (14%)
  local copies, waits for them, and re-layouts  0.68 us (1%)
    all_to_all x1, blocking collectives, shards(): lax.all_to_all(homeward.reshape(groups_n, back, narrow), 'groups', split_...  14.2 us
    pallas_call x1, Pallas kernels, shards(): pl.pallas_call(functools.partial(attend_kernel, text=text), out_shape=[ha...  13.8 us
    pallas_call x1, Pallas kernels, shards(): pl.pallas_call(functools.partial(prepare_kernel, capacity, block, back, s...  13.4 us
    all_to_all x1, starting transfers between devices, shards(): lax.all_to_all(outbound.reshape(groups_n * 2, block, narrow), both, split...  4.92 us
    pallas_call x1, Pallas kernels, shards(): pl.pallas_call(functools.partial(finish_kernel, step), out_shape=jax.Shap...  4.71 us
    ppermute x1, starting transfers between devices, shards(): mate_mod = lax.ppermute(adaptive, 'groups', pairs)  2.94 us
    pallas_call x1, Pallas kernels, shards(): pl.pallas_call(functools.partial(send_kernel, capacity, block), out_shape...  1.82 us
    pallas_call x1, Pallas kernels, shards(): pl.pallas_call(functools.partial(begin_kernel, step), out_shape=jax.Shape...  1.67 us
  transfers between devices with their start and end apart: 4, of which 0 were waited for; matrix products, arithmetic and copies ran while one was open for 0% of the time, Pallas kernels for 51%

profile of v6, /device:TPU:0, one launch (start us, length us, event | category | flops | bytes accessed | tf_op | source)
XLA Modules:
  0.0 59.9 jit_solution(14694264748542067474)
XLA Ops:
  0.0 2.9 %collective-permute-start = (f32[5,2,2432]{2,1,0:T(2,128)}, f32[5,2,2432]{2,1,0:T(2,128)S(1)}, u32[]{:S(2)}, u32[]{:S(2)}) collective-permute-start(f32[5,2,2432]{2,1,0:T(2,128)} %bitcast.13), channel_id=1, source_target_pairs={{0,2},{2,0},{4,6},{6,4},{8,10},{10,8},{12,14},{14,12},{16,18},{18,... | collective-permute-start | bytes 291848 | tf_op jit(solution)/shard_map/ppermute | solution.py:618
  2.9 1.8 %shard_map.118 = bf16[16,2,16,128]{3,2,1,0:T(8,128)(2,1)} custom-call(s32[12,128]{1,0:T(8,128)} %bitcast.20, f32[96,128]{1,0:T(8,128)} %latents_ref.3), custom_call_target="tpu_custom_call" | custom-call | tf_op jit(solution)/shard_map/pallas_call | solution.py:620
  4.8 4.9 %all-to-all-start = ((bf16[32,16,128]{2,1,0:T(8,128)(2,1)}), bf16[32,16,128]{2,1,0:T(8,128)(2,1)S(1)}, u32[]{:S(2)}, u32[]{:S(2)}) async-start(bf16[32,16,128]{2,1,0:T(8,128)(2,1)} %bitcast.25), calls=%async_computation | async-start | bytes 262144 | tf_op jit(solution)/shard_map/all_to_all | solution.py:627
  9.7 0.0 collective-permute-done.mate_mod_hbm
  9.7 0.0 copy-start.10
  9.7 0.6 %copy-done.10 = f32[5,2,2432]{2,1,0:T(2,128)} copy-done((f32[5,2,2432]{2,1,0:T(2,128)}, f32[5,2,2432]{2,1,0:T(2,128)S(1)}, u32[]{:S(2)}) %copy-start.10) | copy-done | bytes 97304
  10.4 13.4 %shard_map.119 = (bf16[96,256]{1,0:T(8,128)(2,1)}, bf16[2,544,640]{2,1,0:T(8,128)(2,1)}, bf16[2,5,640,256]{3,2,1,0:T(8,128)(2,1)}) custom-call(s32[12,128]{1,0:T(8,128)} %bitcast.21, bf16[64,2432]{1,0:T(8,128)(2,1)} %embed_ref.1, f32[5,2,2432]{2,1,0:T(2,128)} %bitcast.14, f32[5,2,2432]{2,1,0:T(2,128)} %copy-done.10, f32[3,64]{1,0:T(4,128)} %gains_ref.1, ...), custom_call_target="tpu_custom_call" | custom-call | flops 4607180800 | bytes 15564800 | tf_op jit(solution)/shard_map/pallas_call | solution.py:638
  23.7 0.0 all-to-all-done
  23.7 0.0 copy-done
  23.7 0.3 collective-permute-start.2
  24.1 0.0 copy-done.7
  24.1 0.0 copy-done.8
  24.1 0.0 copy-done.9
  24.1 13.8 %shard_map.120 = (bf16[2,192,640]{2,1,0:T(8,128)(2,1)S(1)}, bf16[2,192,640]{2,1,0:T(8,128)(2,1)S(1)}, bf16[192,128]{1,0:T(8,128)(2,1)S(1)}) custom-call(s32[16]{0:T(128)S(1)} %copy-done.8, s32[16]{0:T(128)S(1)} %copy-done.9, bf16[16,2,16,128]{3,2,1,0:T(8,128)(2,1)S(1)} %bitcast.19, f32[3,64]{1,0:T(4,128)S(1)} %copy-done.7, ...), custom_call_target="tpu_custom_call" | custom-call | flops 40265318400 | bytes 8388608 | tf_op jit(solution)/shard_map/pallas_call | solution.py:686
  37.9 0.3 collective-permute-start.1
  38.3 1.7 %shard_map.121.begun_ref = f32[384,2432]{1,0:T(8,128)S(1)} custom-call(bf16[2,192,640]{2,1,0:T(8,128)(2,1)S(1)} %get-tuple-element.18.kept_ref, bf16[640,2432]{1,0:T(8,128)(2,1)S(1)} %copy-done), custom_call_target="tpu_custom_call" | custom-call | flops 1195376640 | bytes 8388608 | tf_op jit(solution)/shard_map/pallas_call | solution.py:708
  39.9 0.0 collective-permute-done.1.came_ref
  39.9 0.0 collective-permute-done.2.w_came_ref
  40.0 0.0 copy-done.1
  40.0 0.0 copy-start.4
  40.0 0.0 copy-start.5
  40.0 4.7 %shard_map.122 = bf16[256,128]{1,0:T(8,128)(2,1)S(1)} custom-call(s32[16]{0:T(128)S(1)} %copy-done.8, f32[384,2432]{1,0:T(8,128)S(1)} %shard_map.121.begun_ref, bf16[2,192,640]{2,1,0:T(8,128)(2,1)S(1)} %collective-permute-done.1.came_ref, bf16[640,2432]{1,0:T(8,128)(2,1)S(1)} %collective-permute-done.2.w_came_ref, ...), custom_call_target="tpu_custom_call" | custom-call | tf_op jit(solution)/shard_map/pallas_call | solution.py:718
  44.7 14.2 %all_to_all.10 = bf16[16,16,128]{2,1,0:T(8,128)(2,1)S(1)} all-to-all(bf16[16,16,128]{2,1,0:T(8,128)(2,1)S(1)} %bitcast.17), channel_id=1, replica_groups=mesh['groups'=16,'mp'=2] {'groups'}, dimensions={0} | all-to-all | bytes 131072 | tf_op jit(solution)/shard_map/all_to_all | solution.py:728
  58.9 1.0 %shard_map.123 = f32[96,128]{1,0:T(8,128)} custom-call(s32[12,128]{1,0:T(8,128)S(1)} %bitcast.22, f32[96,128]{1,0:T(8,128)S(1)} %copy-done.4, bf16[256,128]{1,0:T(8,128)(2,1)S(1)} %bitcast.18), custom_call_target="tpu_custom_call" | custom-call | tf_op jit(solution)/shard_map/pallas_call | solution.py:731
  (13 shorter events, 0.0 us)
Async XLA Ops:
  0.0 9.7 %collective-permute-start = (f32[5,2,2432]{2,1,0:T(2,128)}, f32[5,2,2432]{2,1,0:T(2,128)S(1)}, u32[]{:S(2)}, u32[]{:S(2)}) collective-permute-start(f32[5,2,2432]{2,1,0:T(2,128)} %bitcast.13), channel_id=1, source_target_pairs={{0,2},{2,0},{4,6},{6,4},{8,10},{10,8},{12,14},{14,12},{16,18},{18,... | collective-permute-start | bytes 291848 | tf_op jit(solution)/shard_map/ppermute | solution.py:618
  4.8 19.0 %all-to-all-start = ((bf16[32,16,128]{2,1,0:T(8,128)(2,1)}), bf16[32,16,128]{2,1,0:T(8,128)(2,1)S(1)}, u32[]{:S(2)}, u32[]{:S(2)}) async-start(bf16[32,16,128]{2,1,0:T(8,128)(2,1)} %bitcast.25), calls=%async_computation | async-start | bytes 262144 | tf_op jit(solution)/shard_map/all_to_all | solution.py:627
  9.7 0.6 %copy-start.10 = (f32[5,2,2432]{2,1,0:T(2,128)}, f32[5,2,2432]{2,1,0:T(2,128)S(1)}, u32[]{:S(2)}) copy-start(f32[5,2,2432]{2,1,0:T(2,128)S(1)} %collective-permute-done.mate_mod_hbm) | copy-start | bytes 291844
  10.4 13.4 %copy-start = (bf16[640,2432]{1,0:T(8,128)(2,1)S(1)}, bf16[640,2432]{1,0:T(8,128)(2,1)}, u32[]{:S(2)}) copy-start(bf16[640,2432]{1,0:T(8,128)(2,1)} %w_own_ref.1) | copy-start | bytes 9338884
  10.4 13.7 %copy-start.7 = (f32[3,64]{1,0:T(4,128)S(1)}, f32[3,64]{1,0:T(4,128)}, u32[]{:S(2)}) copy-start(f32[3,64]{1,0:T(4,128)} %gains_ref.1) | copy-start | bytes 2308
  10.4 13.7 %copy-start.8 = (s32[16]{0:T(128)S(1)}, s32[16]{0:T(128)}, u32[]{:S(2)}) copy-start(s32[16]{0:T(128)} %live_ref.3) | copy-start | bytes 196
  10.4 13.7 %copy-start.9 = (s32[16]{0:T(128)S(1)}, s32[16]{0:T(128)}, u32[]{:S(2)}) copy-start(s32[16]{0:T(128)} %partner_ref.1) | copy-start | bytes 196
  23.7 16.2 %collective-permute-start.2 = (bf16[640,2432]{1,0:T(8,128)(2,1)S(1)}, bf16[640,2432]{1,0:T(8,128)(2,1)S(1)}, u32[]{:S(2)}, u32[]{:S(2)}) collective-permute-start(bf16[640,2432]{1,0:T(8,128)(2,1)S(1)} %copy-done), channel_id=1, source_target_pairs={{0,1},{1,0},{2,3},{3,2},{4,5},{5,4},{6,7},{7,6},{8,9},{9,8},{10,11... | collective-permute-start | bytes 9338888 | tf_op jit(solution)/shard_map/ppermute | solution.py:684
  37.9 2.0 %collective-permute-start.1 = (bf16[2,192,640]{2,1,0:T(8,128)(2,1)S(1)}, bf16[2,192,640]{2,1,0:T(8,128)(2,1)S(1)}, u32[]{:S(2)}, u32[]{:S(2)}) collective-permute-start(bf16[2,192,640]{2,1,0:T(8,128)(2,1)S(1)} %get-tuple-element.19), channel_id=1, source_target_pairs={{0,1},{1,0},{2,3},{3,2},{4,5},{5,4},{6,7},{7,6},{8,9},{9,8},{10,11... | collective-permute-start | bytes 1474568 | tf_op jit(solution)/shard_map/ppermute | solution.py:706
  38.2 1.7 %copy-start.1 = (bf16[64,2432]{1,0:T(8,128)(2,1)S(1)}, bf16[64,2432]{1,0:T(8,128)(2,1)}, u32[]{:S(2)}) copy-start(bf16[64,2432]{1,0:T(8,128)(2,1)} %embed_ref.1) | copy-start | bytes 933892
  38.2 1.7 %copy-start.2 = (f32[1,2,5,2432]{3,1,2,0:T(2,128)S(1)}, f32[1,2,5,2432]{3,1,2,0:T(2,128)}, u32[]{:S(2)}) copy-start(f32[1,2,5,2432]{3,1,2,0:T(2,128)} %param.17) | copy-start | bytes 291844
  38.2 1.7 %copy-start.3 = (bf16[2432,64]{0,1:T(8,128)(2,1)S(1)}, bf16[2432,64]{0,1:T(8,128)(2,1)}, u32[]{:S(2)}) copy-start(bf16[2432,64]{0,1:T(8,128)(2,1)} %param.22) | copy-start | bytes 933892
  38.3 1.7 %copy-start.6 = (bf16[96,256]{1,0:T(8,128)(2,1)S(1)}, bf16[96,256]{1,0:T(8,128)(2,1)}, u32[]{:S(2)}) copy-start(bf16[96,256]{1,0:T(8,128)(2,1)} %get-tuple-element.22.home_ref) | copy-start | bytes 147460
  40.0 18.9 %copy-start.4 = (f32[96,128]{1,0:T(8,128)S(1)}, f32[96,128]{1,0:T(8,128)}, u32[]{:S(2)}) copy-start(f32[96,128]{1,0:T(8,128)} %latents_ref.3) | copy-start | bytes 147460
  40.0 18.9 %copy-start.5 = (s32[1536]{0:T(1024)S(1)}, s32[1536]{0:T(1024)}, u32[]{:S(2)}) copy-start(s32[1536]{0:T(1024)} %param.13) | copy-start | bytes 18436
